TPU v7x, 32 devices: a whole 2x2x4 slice. The times are simulated.
32 devices in a mesh: groups: 2 (over x), ff: 8 (over z, y), var: 2 (over core).
Axes of the slice: x: 2, y: 2, z: 4, core: 2. Of those that a mesh axis runs over, the one named last changes fastest.
Arguments:
- tokens: bfloat16 [128, 8192], P(('groups', 'ff'), 'var'), parts along dimension 0, may hold values from -6 to 6
- gate_weight: bfloat16 [8192, 16384], P('var', 'ff'), may hold values from -0.0625 to 0.0625
- up_weight: bfloat16 [8192, 16384], P('var', 'ff'), may hold values from -0.0625 to 0.0625
- down_weight: bfloat16 [16384, 8192], P('ff', 'var'), may hold values from -0.046875 to 0.046875
- shrink_gu: bfloat16 [64, 32, 8192], P(('groups', 'ff'), None, 'var'), parts along dimension 0, may hold values from -0.0625 to 0.0625
- expand_gu: bfloat16 [64, 2, 16, 16384], P(('groups', 'ff'), None, 'var'), parts along dimension 0, may hold values from -1.5 to 1.5
- shrink_down: bfloat16 [64, 16, 16384], P(('groups', 'ff')), parts along dimension 0, may hold values from -0.046875 to 0.046875
- expand_down: bfloat16 [64, 16, 8192], P(('groups', 'ff'), None, 'var'), parts along dimension 0, may hold values from -1.5 to 1.5
- variant_ids: int32 [128, 1], P('groups'), parts along dimension 0, may hold values from 0 to 31; in each aligned block of 64 rows (0 to 63, 64 to 127, ...) at most 8 rows name the same one
- variant_slot: int32 [64], P('groups'), parts along dimension 0, may hold values from 0 to 31, each once
Outputs:
- mixed: bfloat16 [128, 8192], P(('groups', 'ff'), 'var'), parts along dimension 0
There are 2 independent parts, one for each index of `groups`. A program takes and returns all parts, laid end to end along the dimension named above; an argument that names none is the same for every part. Nothing has to cross between parts.
Inputs may be any that keep to these rules, and one draw needn't show every extreme that they name: `variant_ids`: no variant is used by more than 8 rows of a group and one variant by exactly 8; every variant is used by some row. `variant_slot`: each slot holds exactly one variant.
All inputs are finite; a program needn't handle non-finite values.
Results may differ from a plain program's by a relative error of at most 0.0063.
Values may be sent and summed in bfloat16 or wider, within the bound.
No kernel may reach another device: no remote copies, remote signals or barrier semaphores. Data moves between devices by JAX's collectives and lax.ppermute only.
A program may use at most 192 MiB of HBM per device.

v0:
```python
import jax
import jax.numpy as jnp
from jax import lax
from jax.sharding import PartitionSpec as P

MOST = 8


def per_device(
    tokens,
    gate_weight,
    up_weight,
    down_weight,
    shrink_gu,
    expand_gu,
    shrink_down,
    expand_down,
    variant_ids,
    variant_slot,
):
    owner_index = lax.axis_index("ff")
    var_index = lax.axis_index("var")
    local_slots = shrink_gu.shape[0]
    variants = variant_slot.shape[0]
    rank_size = shrink_down.shape[1]
    half_rank = expand_gu.shape[2]
    gathered = lax.all_gather(tokens, "ff", axis=0, tiled=True)
    total_rows = gathered.shape[0]
    width_half = gathered.shape[1]
    matches = variant_ids[:, 0][:, None] == jnp.arange(variants, dtype=jnp.int32)[None, :]
    slot_row = jnp.sum(jnp.where(matches, variant_slot[None, :], 0), axis=1)
    slot_hits = slot_row[:, None] == jnp.arange(variants, dtype=jnp.int32)[None, :]
    counts = jnp.sum(slot_hits.astype(jnp.int32), axis=0)
    offsets = jnp.cumsum(counts) - counts
    sorted_rows = jnp.argsort(slot_row, stable=True)
    padded_rows = jnp.concatenate([sorted_rows, jnp.zeros((MOST,), jnp.int32)])
    first_slot = owner_index * local_slots
    own_starts = lax.dynamic_slice_in_dim(offsets, first_slot, local_slots, 0)
    own_counts = lax.dynamic_slice_in_dim(counts, first_slot, local_slots, 0)
    positions = jnp.arange(MOST, dtype=jnp.int32)[None, :]
    pick_index = padded_rows[own_starts[:, None] + positions]
    live_slots = positions < own_counts[:, None]
    flat_index = pick_index.reshape(-1)
    picked = gathered[flat_index].reshape(local_slots, MOST, width_half)
    partial_in = jnp.einsum("jmd,jkd->jmk", picked, shrink_gu, preferred_element_type=jnp.float32)
    partial_in = jnp.where(live_slots[:, :, None], partial_in, 0.0)
    spread_in = (
        jnp.zeros((total_rows, 2 * rank_size), jnp.float32)
        .at[flat_index]
        .add(partial_in.reshape(-1, 2 * rank_size))
    )
    low_in = lax.psum(spread_in, ("ff", "var")).astype(jnp.bfloat16)
    ff_local = gate_weight.shape[1]
    expand_local = expand_gu.reshape(local_slots, 2 * half_rank, expand_gu.shape[3])
    got_expand, got_shrink = (
        lax.all_to_all(expand_local, "ff", split_axis=2, concat_axis=0, tiled=True),
        lax.all_to_all(shrink_down, "ff", split_axis=2, concat_axis=0, tiled=True),
    )
    row_expand = got_expand[slot_row].reshape(total_rows, 2, half_rank, ff_local)
    low_half = lax.dynamic_slice_in_dim(
        low_in.reshape(total_rows, 2, rank_size), var_index * half_rank, half_rank, 2
    )
    delta_gu = jnp.einsum("tgk,tgkf->tgf", low_half, row_expand, preferred_element_type=jnp.float32)
    base_gate = jnp.dot(gathered, gate_weight, preferred_element_type=jnp.float32)
    base_up = jnp.dot(gathered, up_weight, preferred_element_type=jnp.float32)
    partial_gu = jnp.stack([base_gate, base_up], axis=1) + delta_gu
    summed = lax.psum(partial_gu, "var")
    hidden = (jax.nn.silu(summed[:, 0]) * summed[:, 1]).astype(jnp.bfloat16)
    row_shrink = got_shrink[slot_row]
    partial_out = jnp.einsum("tf,tkf->tk", hidden, row_shrink, preferred_element_type=jnp.float32)
    low_out = lax.psum(partial_out, "ff").astype(jnp.bfloat16)
    picked_out = low_out[flat_index].reshape(local_slots, MOST, rank_size)
    delta_rows = jnp.einsum(
        "jmk,jkd->jmd", picked_out, expand_down, preferred_element_type=jnp.float32
    )
    delta_rows = jnp.where(live_slots[:, :, None], delta_rows, 0.0)
    delta_term = (
        jnp.zeros((total_rows, width_half), jnp.float32)
        .at[flat_index]
        .add(delta_rows.reshape(-1, width_half))
    )
    base_part = lax.psum_scatter(
        jnp.dot(hidden, down_weight, preferred_element_type=jnp.float32),
        "ff",
        scatter_dimension=0,
        tiled=True,
    )
    delta_part = lax.psum_scatter(delta_term, "ff", scatter_dimension=0, tiled=True)
    mixed = (base_part + delta_part).astype(jnp.bfloat16)
    return mixed


def solution(mesh):
    placed = (
        P(("groups", "ff"), "var"),
        P("var", "ff"),
        P("var", "ff"),
        P("ff", "var"),
        P(("groups", "ff"), None, "var"),
        P(("groups", "ff"), None, "var", None),
        P(("groups", "ff"), None, None),
        P(("groups", "ff"), None, "var"),
        P("groups", None),
        P("groups"),
    )
    return jax.shard_map(
        per_device,
        mesh=mesh,
        in_specs=placed,
        out_specs=P(("groups", "ff"), "var"),
        check_vma=False,
    )
```

profile of v0, /device:TPU:0, one launch (start us, length us, event | category | flops | bytes accessed | tf_op | source)
XLA Modules:
  0.0 450.9 jit_solution(13101627601052014159)
XLA Ops:
  6.5 19.6 %copy.44 = bf16[4,16,16384]{1,0,2:T(4,128)(2,1)} copy(bf16[4,16,16384]{2,1,0:T(8,128)(2,1)} %bitcast.89) | data formatting | bytes 4194304 | tf_op jit(solution)/shard_map/reshape | solution.py:54
  26.1 19.6 %reshape.233 = bf16[8,2,65536]{2,1,0:T(2,128)(2,1)} reshape(bf16[16384,4,16]{2,1,0:T(4,128)(2,1)} %bitcast.85) | data formatting | bytes 4194304
  45.7 7.4 %all-to-all-start = ((bf16[8,2,65536]{2,1,0:T(2,128)(2,1)}), bf16[8,2,65536]{2,1,0:T(2,128)(2,1)}, u32[]{:S(2)}, u32[]{:S(2)}) async-start(bf16[8,2,65536]{2,1,0:T(2,128)(2,1)} %reshape.233), calls=%async_computation | async-start | bytes 4194304 | tf_op jit(solution)/shard_map/all_to_all | solution.py:56
  53.2 2.0 sort.17
  56.7 65.8 %all_gather.3 = bf16[64,4096]{1,0:T(8,128)(2,1)S(1)} all-gather(bf16[8,4096]{1,0:T(8,128)(2,1)S(1)} %copy-done.6), channel_id=1, replica_groups=mesh['groups'=2,'ff'=8,'var'=2] {'ff'}, dimensions={0}, use_global_device_ids=true | all-gather | bytes 589824 | tf_op jit(solution)/shard_map/all_gather | solution.py:27
  124.5 57.6 %psum.21 = bf16[64,32]{0,1:T(8,128)(2,1)S(1)} all-reduce(f32[64,32]{0,1:T(8,128)S(1)} %copy.43), channel_id=1, replica_groups=mesh['groups'=2,'ff'=8,'var'=2] {'ff','var'}, use_global_device_ids=true, to_apply=%region_5.6 | all-reduce | flops 2048 | bytes 12288 | tf_op jit(solution)/shard_map/psum | solution.py:52
  182.2 19.5 %copy.47 = bf16[4,16,16384]{1,0,2:T(4,128)(2,1)} copy(bf16[4,16,16384]{2,1,0:T(8,128)(2,1)} %param.16) | data formatting | bytes 4194304 | tf_op args[6]
  201.7 19.6 %reshape.231 = bf16[8,2,65536]{2,1,0:T(2,128)(2,1)} reshape(bf16[16384,4,16]{2,1,0:T(4,128)(2,1)} %bitcast.86) | data formatting | bytes 4194304
  221.3 4.4 all-to-all-start.1
  225.9 9.6 %convolution_bitcast_fusion = f32[64,1,2048]{2,0,1:T(8,128)} fusion(bf16[64,4096]{1,0:T(8,128)(2,1)S(1)} %all_gather.3, bf16[4096,2048]{1,0:T(8,128)(2,1)} %param.12), kind=kOutput, calls=%fused_computation.12 | convolution fusion | flops 1073741824 | bytes 17825792 | tf_op jit(solution)/shard_map/dot_general | solution.py:65
  235.5 9.6 %convolution_bitcast_fusion.1 = f32[64,1,2048]{2,0,1:T(8,128)} fusion(bf16[64,4096]{1,0:T(8,128)(2,1)S(1)} %all_gather.3, bf16[4096,2048]{1,0:T(8,128)(2,1)} %param.11), kind=kOutput, calls=%fused_computation.13 | convolution fusion | flops 1073741824 | bytes 17825792 | tf_op jit(solution)/shard_map/dot_general | solution.py:64
  245.1 13.9 %reshape.234 = bf16[16384,4,16]{2,1,0:T(4,128)(2,1)} reshape(bf16[8,2,65536]{2,1,0:T(2,128)(2,1)} %all-to-all-done) | data formatting | bytes 4194304
  259.0 21.3 %copy.55 = bf16[4,16,8,2048]{3,1,0,2:T(8,128)(2,1)S(1)} copy(bf16[4,16,8,2048]{1,0,3,2:T(4,128)(2,1)} %bitcast.83) | data formatting | bytes 4194304 | tf_op jit(solution)/shard_map/all_to_all | solution.py:56
  280.4 2.7 gather_fusion.2
  283.1 3.5 fusion.1
  286.7 1.7 maximum_add_fusion
  288.5 13.9 %reshape.232 = bf16[16384,4,16]{2,1,0:T(4,128)(2,1)} reshape(bf16[8,2,65536]{2,1,0:T(2,128)(2,1)} %all-to-all-done.1) | data formatting | bytes 4194304
  302.4 21.5 %copy.57 = bf16[4,16,8,2048]{3,1,0,2:T(8,128)(2,1)S(1)} copy(bf16[4,16,8,2048]{1,0,3,2:T(4,128)(2,1)} %bitcast.84) | data formatting | bytes 4194304 | tf_op jit(solution)/shard_map/all_to_all | solution.py:57
  323.9 2.7 gather_fusion.3
  328.0 3.8 fusion.6
  331.9 37.2 %psum.23 = bf16[64,16]{1,0:T(8,128)(2,1)S(1)} all-reduce(f32[64,16]{1,0:T(8,128)S(1)} %bitcast.90), channel_id=1, replica_groups=mesh['groups'=2,'ff'=8,'var'=2] {'ff'}, use_global_device_ids=true, to_apply=%region_8.9 | all-reduce | flops 1024 | bytes 6144 | tf_op jit(solution)/shard_map/psum | solution.py:71
  371.5 9.9 %convolution_add_fusion = f32[64,4096]{1,0:T(8,128)} fusion(f32[64,4096]{1,0:T(8,128)S(1)} %scatter_custom_fusion.1, bf16[2048,4096]{1,0:T(8,128)(2,1)} %param.13, f32[64,2,2048]{2,0,1:T(8,128)S(1)} %copy-done.2), kind=kOutput, calls=%fused_computation.7 | convolution fusion | flops 1074790400 | bytes 19922944 | tf_op jit(solution)/shard_map/dot_general | solution.py:83
  381.3 61.2 %reduce-scatter.2.cloned.1.call-done = f32[8,4096]{1,0:T(8,128)} async-done(((f32[64,4096]{1,0:T(8,128)}), f32[8,4096]{1,0:T(8,128)}) %reduce-scatter.2.cloned.1.call-update) | async-done | bytes 131088 | tf_op jit(solution)/shard_map/reduce_scatter | solution.py:82
  442.5 1.5 convert_element_type.19
  (54 shorter events, 7.6 us)
Async XLA Ops:
  6.5 116.7 %copy-start = (bf16[4,32,4096]{2,1,0:T(8,128)(2,1)S(1)}, bf16[4,32,4096]{2,1,0:T(8,128)(2,1)}, u32[]{:S(2)}) copy-start(bf16[4,32,4096]{2,1,0:T(8,128)(2,1)} %param.14) | copy-start | bytes 3145732
  45.7 7.4 %copy-start.7 = (s32[32]{0:T(128)S(1)}, s32[32]{0:T(128)}, u32[]{:S(2)}) copy-start(s32[32]{0:T(128)} %param.19) | copy-start | bytes 388
  45.7 7.4 %copy-start.8 = (s32[64,1]{0,1:T(1,128)S(1)}, s32[64,1]{0,1:T(1,128)}, u32[]{:S(2)}) copy-start(s32[64,1]{0,1:T(1,128)} %param.18) | copy-start | bytes 772
  45.7 11.0 %copy-start.6 = (bf16[8,4096]{1,0:T(8,128)(2,1)S(1)}, bf16[8,4096]{1,0:T(8,128)(2,1)}, u32[]{:S(2)}) copy-start(bf16[8,4096]{1,0:T(8,128)(2,1)} %param.10) | copy-start | bytes 196612
  45.7 175.6 %all-to-all-start = ((bf16[8,2,65536]{2,1,0:T(2,128)(2,1)}), bf16[8,2,65536]{2,1,0:T(2,128)(2,1)}, u32[]{:S(2)}, u32[]{:S(2)}) async-start(bf16[8,2,65536]{2,1,0:T(2,128)(2,1)} %reshape.233), calls=%async_computation | async-start | bytes 4194304 | tf_op jit(solution)/shard_map/all_to_all | solution.py:56
  221.3 67.2 %all-to-all-start.1 = ((bf16[8,2,65536]{2,1,0:T(2,128)(2,1)}), bf16[8,2,65536]{2,1,0:T(2,128)(2,1)}, u32[]{:S(2)}, u32[]{:S(2)}) async-start(bf16[8,2,65536]{2,1,0:T(2,128)(2,1)} %reshape.231), calls=%async_computation.1 | async-start | bytes 4194304 | tf_op jit(solution)/shard_map/all_to_all | solution.py:57
  225.7 101.0 %all-reduce.3.cloned.1.call-start = ((), (), s32[]{:S(2)}) async-start(), calls=%async_computation.3 | async-start | bytes 2097152 | tf_op jit(solution)/shard_map/psum | solution.py:67
  283.1 3.5 copy-start.3
  283.1 3.5 copy-start.4
  288.4 154.2 %reduce-scatter.2.cloned.1.call-start = ((), (), s32[]{:S(2)}) async-start(), calls=%async_computation.4 | async-start | bytes 1179648 | tf_op jit(solution)/shard_map/reduce_scatter | solution.py:82
  326.6 43.1 %copy-start.5 = (bf16[4,16,4096]{2,1,0:T(8,128)(2,1)S(1)}, bf16[4,16,4096]{2,1,0:T(8,128)(2,1)}, u32[]{:S(2)}) copy-start(bf16[4,16,4096]{2,1,0:T(8,128)(2,1)} %param.17) | copy-start | bytes 1572868
  328.0 43.4 %copy-start.2 = (f32[64,2,2048]{2,0,1:T(8,128)S(1)}, f32[64,2,2048]{2,0,1:T(8,128)}, u32[]{:S(2)}) copy-start(f32[64,2,2048]{2,0,1:T(8,128)} %all-reduce.3.cloned.1.call-done) | copy-start | bytes 3145732
  371.4 72.7 %copy-start.1 = (bf16[4,32,4096]{2,1,0:T(8,128)(2,1)S(1)}, bf16[4,32,4096]{2,1,0:T(8,128)(2,1)}, u32[]{:S(2)}) copy-start(bf16[4,32,4096]{2,1,0:T(8,128)(2,1)} %param.14) | copy-start | bytes 3145732
Sparse Core Ops, SparseCore 0:
  288.5 20.6 all-reduce.2
  381.5 61.0 reduce-scatter.1
where the time goes:
time: 454 us; the launch traced here: 451 us
  blocking collectives  161 us (35%)
  local copies, waits for them, and re-layouts  157 us (35%)
  waiting for transfers between devices  61.2 us (13%)
  matrix products  37 us (8%)
  between operations  13.6 us (3%)
  starting transfers between devices  12.1 us (3%)
  other arithmetic  9.49 us (2%)
    unnamed x23, local copies, waits for them, and re-layouts  86.5 us
    all_gather x1, blocking collectives, per_device(): gathered = lax.all_gather(tokens, 'ff', axis=0, tiled=True)  65.8 us
    reduce_scatter x1, waiting for transfers between devices, per_device(): lax.psum_scatter(jnp.dot(hidden, down_weight, preferred_element_type=jnp....  61.2 us
    psum x1, blocking collectives, per_device(): low_in = lax.psum(spread_in, ('ff', 'var')).astype(jnp.bfloat16)  57.6 us
    psum x1, blocking collectives, per_device(): low_out = lax.psum(partial_out, 'ff').astype(jnp.bfloat16)  37.2 us
    all_to_all x1, local copies, waits for them, and re-layouts, per_device(): lax.all_to_all(shrink_down, 'ff', split_axis=2, concat_axis=0, tiled=True)  21.5 us
    all_to_all x1, local copies, waits for them, and re-layouts, per_device(): lax.all_to_all(expand_local, 'ff', split_axis=2, concat_axis=0, tiled=True)  21.3 us
    reshape x1, local copies, waits for them, and re-layouts, per_device(): expand_gu.reshape(local_slots, 2 * half_rank, expand_gu.shape[3])  19.6 us
  transfers between devices with their start and end apart: 4, of which 1 were waited for; matrix products, arithmetic and copies ran while one was open for 32% of the time, Pallas kernels for 0%

commit v1 on v0

v1 whole, which is shorter than its diff:
```python
import functools

import jax
import jax.numpy as jnp
from jax import lax
from jax.experimental import pallas as pl
from jax.experimental.pallas import tpu as pltpu
from jax.sharding import PartitionSpec as P

MOST = 8
BF = jnp.bfloat16
F32 = jnp.float32
MIB = 1024 * 1024


def dot(a, b):
    return jnp.dot(a, b, preferred_element_type=F32)


def dot_last(a, b):
    return lax.dot_general(a, b, (((1,), (1,)), ((), ())), preferred_element_type=F32)


def params(mib):
    return pltpu.CompilerParams(vmem_limit_bytes=mib * MIB)


def cost(flops, moved):
    return pl.CostEstimate(flops=flops, bytes_accessed=moved, transcendentals=0)


def copy_kernel(core_ref, in_ref, out_ref):
    out_ref[...] = in_ref[...]


def other_half(core, factors, shards, half):
    depth = factors.shape[0]
    return pl.pallas_call(
        copy_kernel,
        out_shape=jax.ShapeDtypeStruct((depth, shards * half), factors.dtype),
        grid_spec=pltpu.PrefetchScalarGridSpec(
            num_scalar_prefetch=1,
            grid=(shards,),
            in_specs=[pl.BlockSpec((depth, half), lambda j, core: (0, 2 * j + 1 - core[0]))],
            out_specs=pl.BlockSpec((depth, half), lambda j, core: (0, j)),
        ),
        compiler_params=params(8),
        cost_estimate=cost(0, 4 * depth * shards * half),
    )(core, factors)


def low_in_kernel(x_ref, shrink_ref, mask_ref, out_ref):
    pairs = dot_last(x_ref[...], shrink_ref[...])
    out_ref[...] = jnp.where(mask_ref[...] > 0, pairs, 0.0)


def low_in_pairs(x, shrink, mask):
    rows, width = x.shape
    return pl.pallas_call(
        low_in_kernel,
        out_shape=jax.ShapeDtypeStruct(mask.shape, F32),
        compiler_params=params(16),
        cost_estimate=cost(2 * rows * width * shrink.shape[0], 2 * shrink.size + 2 * x.size),
    )(x, shrink, mask)


def expand_kernel(
    core_ref, own_ref, got_ref, pick_ref, cols_ref, near_ref, far_ref, out_ref, lhs_near, lhs_far
):
    cap = pick_ref.shape[0]

    @pl.when(pl.program_id(0) == 0)
    def _():
        low = (own_ref[...] + got_ref[...]).astype(BF)
        picked = dot(pick_ref[...], low).astype(BF)
        for kind in range(2):
            at = pl.ds(kind * cap, cap)
            lhs_near[at] = dot(picked, cols_ref[kind, 0]).astype(BF)
            lhs_far[at] = dot(picked, cols_ref[kind, 1]).astype(BF)

    delta = dot(lhs_near[...], near_ref[...]) + dot(lhs_far[...], far_ref[...])
    out_ref[0] = delta.astype(BF)


def expand_rows(core, own, got, pick, cols, near, far, shards, half):
    cap = pick.shape[0]
    depth = near.shape[0]
    whole = lambda shape: pl.BlockSpec(shape, lambda j, core: (0,) * len(shape))
    return pl.pallas_call(
        expand_kernel,
        out_shape=jax.ShapeDtypeStruct((shards, 2 * cap, half), BF),
        grid_spec=pltpu.PrefetchScalarGridSpec(
            num_scalar_prefetch=1,
            grid=(shards,),
            in_specs=[
                whole(own.shape),
                whole(got.shape),
                whole(pick.shape),
                whole(cols.shape),
                pl.BlockSpec((depth, half), lambda j, core: (0, 2 * j + core[0])),
                pl.BlockSpec((depth, half), lambda j, core: (0, j)),
            ],
            out_specs=pl.BlockSpec((1, 2 * cap, half), lambda j, core: (j, 0, 0)),
            scratch_shapes=[pltpu.VMEM((2 * cap, depth), BF), pltpu.VMEM((2 * cap, depth), BF)],
        ),
        compiler_params=params(16),
        cost_estimate=cost(8 * cap * depth * shards * half, 4 * (depth + cap) * shards * half),
    )(core, own, got, pick, cols, near, far)


def base_kernel(side_ref, x_ref, gate_ref, up_ref, out_ref):
    out_ref[0] = dot(x_ref[...], gate_ref[...]).astype(out_ref.dtype)
    out_ref[1] = dot(x_ref[...], up_ref[...]).astype(out_ref.dtype)


def base_half(side, x, gate_weight, up_weight, half, kind):
    rows, width = x.shape
    block = min(256, half)
    steps = half // block
    weight = pl.BlockSpec((width, block), lambda n, side: (0, side[0] * steps + n))
    return pl.pallas_call(
        base_kernel,
        out_shape=jax.ShapeDtypeStruct((2, rows, half), kind),
        grid_spec=pltpu.PrefetchScalarGridSpec(
            num_scalar_prefetch=1,
            grid=(steps,),
            in_specs=[pl.BlockSpec((rows, width), lambda n, side: (0, 0)), weight, weight],
            out_specs=pl.BlockSpec((2, rows, block), lambda n, side: (0, 0, n)),
        ),
        compiler_params=params(24),
        cost_estimate=cost(4 * rows * width * half, 4 * width * half + 2 * rows * width),
    )(side, x, gate_weight, up_weight)


def hidden_kernel(own_ref, got_ref, delta_ref, place_ref, send_ref, hid_ref, out_ref):
    rows = hid_ref.shape[0]
    delta = dot(place_ref[...], delta_ref[...])
    gate = own_ref[0] + got_ref[0].astype(F32) + delta[:rows]
    up = own_ref[1] + got_ref[1].astype(F32) + delta[rows:]
    hidden = (gate / (1.0 + jnp.exp(-gate)) * up).astype(BF)
    hid_ref[...] = hidden
    out_ref[...] = dot(send_ref[...], hidden).astype(BF)


def hidden_half(own, got, delta, place, send):
    rows, half = own.shape[1:]
    block = min(256, half)
    cells = send.shape[0]
    return pl.pallas_call(
        hidden_kernel,
        out_shape=(
            jax.ShapeDtypeStruct((rows, half), BF),
            jax.ShapeDtypeStruct((cells, half), BF),
        ),
        grid=(half // block,),
        in_specs=[
            pl.BlockSpec((2, rows, block), lambda n: (0, 0, n)),
            pl.BlockSpec((2, rows, block), lambda n: (0, 0, n)),
            pl.BlockSpec((delta.shape[0], block), lambda n: (0, n)),
            pl.BlockSpec(place.shape, lambda n: (0, 0)),
            pl.BlockSpec(send.shape, lambda n: (0, 0)),
        ],
        out_specs=(
            pl.BlockSpec((rows, block), lambda n: (0, n)),
            pl.BlockSpec((cells, block), lambda n: (0, n)),
        ),
        compiler_params=params(40),
        cost_estimate=cost(
            2 * half * (place.size + send.size), 2 * half * (6 * rows + delta.shape[0] + cells)
        ),
    )(own, got, delta, place, send)


def down_kernel(core_ref, near_ref, far_ref, near_weight, far_weight, out_ref):
    out_ref[...] = dot(near_ref[...], near_weight[...]) + dot(far_ref[...], far_weight[...])


def down_base(core, near, far, weight):
    rows, half = near.shape
    width = weight.shape[1]
    block = min(512, width)
    return pl.pallas_call(
        down_kernel,
        out_shape=jax.ShapeDtypeStruct((rows, width), F32),
        grid_spec=pltpu.PrefetchScalarGridSpec(
            num_scalar_prefetch=1,
            grid=(width // block,),
            in_specs=[
                pl.BlockSpec((rows, half), lambda n, core: (0, 0)),
                pl.BlockSpec((rows, half), lambda n, core: (0, 0)),
                pl.BlockSpec((half, block), lambda n, core: (core[0], n)),
                pl.BlockSpec((half, block), lambda n, core: (1 - core[0], n)),
            ],
            out_specs=pl.BlockSpec((rows, block), lambda n, core: (0, n)),
        ),
        compiler_params=params(24),
        cost_estimate=cost(4 * rows * half * width, 4 * half * width + 4 * rows * width),
    )(core, near, far, weight, weight)


def low_out_kernel(core_ref, hid_ref, shrink_ref, mask_ref, out_ref):
    step = pl.program_id(0)

    @pl.when(step == 0)
    def _():
        out_ref[...] = jnp.zeros_like(out_ref)

    out_ref[...] += dot_last(hid_ref[0], shrink_ref[...])

    @pl.when(step == pl.num_programs(0) - 1)
    def _():
        out_ref[...] = jnp.where(mask_ref[...] > 0, out_ref[...], 0.0)


def low_out_pairs(core, hidden, shrink, mask):
    shards, cap, half = hidden.shape
    depth = shrink.shape[0]
    return pl.pallas_call(
        low_out_kernel,
        out_shape=jax.ShapeDtypeStruct((cap, depth), F32),
        grid_spec=pltpu.PrefetchScalarGridSpec(
            num_scalar_prefetch=1,
            grid=(shards,),
            in_specs=[
                pl.BlockSpec((1, cap, half), lambda j, core: (j, 0, 0)),
                pl.BlockSpec((depth, half), lambda j, core: (0, 2 * j + core[0])),
                pl.BlockSpec(mask.shape, lambda j, core: (0, 0)),
            ],
            out_specs=pl.BlockSpec((cap, depth), lambda j, core: (0, 0)),
        ),
        compiler_params=params(8),
        cost_estimate=cost(2 * cap * depth * shards * half, 2 * shards * half * (depth + cap)),
    )(core, hidden, shrink, mask)


def add_kernel(base_ref, own_ref, got_ref, pick_ref, expand_ref, out_ref):
    low = (own_ref[...] + got_ref[...]).astype(BF)
    spread = lax.dot_general(
        pick_ref[...], low, (((0,), (0,)), ((), ())), preferred_element_type=F32
    ).astype(BF)
    out_ref[...] = (base_ref[...] + dot(spread, expand_ref[...])).astype(BF)


def add_delta(base, own, got, pick, expand):
    rows, width = base.shape
    block = min(1024, width)
    depth = expand.shape[0]
    fixed = lambda shape: pl.BlockSpec(shape, lambda n: (0, 0))
    return pl.pallas_call(
        add_kernel,
        out_shape=jax.ShapeDtypeStruct((rows, width), BF),
        grid=(width // block,),
        in_specs=[
            pl.BlockSpec((rows, block), lambda n: (0, n)),
            fixed(own.shape),
            fixed(got.shape),
            fixed(pick.shape),
            pl.BlockSpec((depth, block), lambda n: (0, n)),
        ],
        out_specs=pl.BlockSpec((rows, block), lambda n: (0, n)),
        compiler_params=params(24),
        cost_estimate=cost(2 * rows * depth * width, width * (6 * rows + 2 * depth)),
    )(base, own, got, pick, expand)


def per_device(
    tokens,
    gate_weight,
    up_weight,
    down_weight,
    shrink_gu,
    expand_gu,
    shrink_down,
    expand_down,
    variant_ids,
    variant_slot,
):
    shards = lax.axis_size("ff")
    me = lax.axis_index("ff")
    core = lax.axis_index("var")
    own_rows, width = tokens.shape
    rows = own_rows * shards
    slots = shrink_gu.shape[0]
    variants = variant_slot.shape[0]
    rank = shrink_down.shape[1]
    half_rank = expand_gu.shape[2]
    half = gate_weight.shape[1] // 2
    cap = min(slots * MOST, rows)
    first = me * slots
    here = core.astype(jnp.int32).reshape(1)
    there = 1 - here
    swap = lambda a: lax.ppermute(a, "var", [(0, 1), (1, 0)])
    spread = lambda a: lax.all_to_all(a, "ff", split_axis=0, concat_axis=0, tiled=True)

    x = spread(jnp.broadcast_to(tokens, (shards, own_rows, width))).reshape(rows, width)

    near = expand_gu.reshape(slots * 2 * half_rank, -1)
    far = swap(other_half(here, near, shards, half))

    ids = variant_ids[:, 0]
    matches = ids[:, None] == jnp.arange(variants, dtype=jnp.int32)[None, :]
    slot_row = jnp.sum(jnp.where(matches, variant_slot[None, :], 0), axis=1)
    owner = slot_row // slots
    order = jnp.arange(rows, dtype=jnp.int32)
    earlier = (owner[:, None] == owner[None, :]) & (order[None, :] < order[:, None])
    place = jnp.sum(earlier.astype(jnp.int32), axis=1)
    cells = jnp.arange(shards * cap, dtype=jnp.int32)
    cell = owner * cap + place
    send_rows = (cells[:, None] == cell[None, :]).astype(BF)
    kinds = jnp.arange(2, dtype=jnp.int32)
    kind_cell = (owner * 2 + kinds[:, None]) * cap + place
    kind_cells = jnp.arange(2 * shards * cap, dtype=jnp.int32)
    place_rows = (kind_cell.reshape(-1)[:, None] == kind_cells[None, :]).astype(BF)
    spots = jnp.arange(cap, dtype=jnp.int32)
    picked = (spots[:, None] == place[None, :]) & (owner[None, :] == me)
    pick = picked.astype(BF)
    local = slot_row - first
    in_cols = jnp.arange(slots * 2 * rank, dtype=jnp.int32)
    mask_in = (local[:, None] == (in_cols // (2 * rank))[None, :]).astype(F32)
    spot_slot = jnp.sum(jnp.where(picked, local[None, :] + 1, 0), axis=1) - 1
    out_cols = jnp.arange(slots * rank, dtype=jnp.int32)
    mask_out = (spot_slot[:, None] == (out_cols // rank)[None, :]).astype(F32)
    rank_at = in_cols % rank
    kind_at = in_cols // rank % 2
    row_at = in_cols // (2 * rank) * (2 * half_rank) + kind_at * half_rank + rank_at % half_rank
    near_cols = jnp.arange(slots * 2 * half_rank, dtype=jnp.int32)
    hit = row_at[:, None] == near_cols[None, :]
    side = jnp.stack([core, 1 - core])
    cols = (
        hit[None, None]
        & (kind_at[None, :] == kinds[:, None])[:, None, :, None]
        & ((rank_at // half_rank)[None, :] == side[:, None])[None, :, :, None]
    ).astype(BF)

    low_own = low_in_pairs(x, shrink_gu.reshape(slots * 2 * rank, width), mask_in)
    low_got = swap(low_own)
    base_got = swap(base_half(there, x, gate_weight, up_weight, half, BF))
    delta = spread(
        expand_rows(here, low_own, low_got, pick, cols, near, far, shards, half)
    ).reshape(2 * shards * cap, half)
    base_own = base_half(here, x, gate_weight, up_weight, half, F32)
    hidden, hidden_send = hidden_half(base_own, base_got, delta, place_rows, send_rows)
    hidden_far = swap(hidden)
    hidden_rows = spread(hidden_send.reshape(shards, cap, half))
    base = down_base(here, hidden, hidden_far, down_weight)
    out_own = low_out_pairs(here, hidden_rows, shrink_down.reshape(slots * rank, -1), mask_out)
    out_got = swap(out_own)
    partial = add_delta(base, out_own, out_got, pick, expand_down.reshape(slots * rank, width))
    parts = spread(partial.reshape(shards, own_rows, width))
    return jnp.sum(parts.astype(F32), axis=0).astype(BF)


def solution(mesh):
    placed = (
        P(("groups", "ff"), "var"),
        P("var", "ff"),
        P("var", "ff"),
        P("ff", "var"),
        P(("groups", "ff"), None, "var"),
        P(("groups", "ff"), None, "var", None),
        P(("groups", "ff"), None, None),
        P(("groups", "ff"), None, "var"),
        P("groups", None),
        P("groups"),
    )
    return jax.shard_map(
        per_device,
        mesh=mesh,
        in_specs=placed,
        out_specs=P(("groups", "ff"), "var"),
        check_vma=False,
    )
```

time: 454 us -> 124 us (0.27)
  blocking collectives: 161 us -> 18.6 us
  local copies, waits for them, and re-layouts: 157 us -> 25.1 us
  matrix products: 37 us -> 0 us
  waiting for transfers between devices: 61.2 us -> 30.1 us
  Pallas kernels: 0 us -> 29.6 us
  between operations: 13.6 us -> 0.21 us
  other arithmetic: 9.49 us -> 2.53 us
  starting transfers between devices: 12.1 us -> 16.8 us
    psum x2 -> x0, blocking collectives: 94.9 us -> none  [the longest x1 57.6 us: per_device(): low_in = lax.psum(spread_in, ('ff', 'var')).astype(jnp.bfloat16)]
    all_gather x1 -> x0, blocking collectives: 65.8 us -> none  [per_device(): gathered = lax.all_gather(tokens, 'ff', axis=0, tiled=True)]
    unnamed x23 -> x16, local copies, waits for them, and re-layouts: 86.5 us -> 23.3 us
    reduce_scatter x1 -> x0, waiting for transfers between devices: 61.2 us -> none  [per_device(): lax.psum_scatter(jnp.dot(hidden, down_weight, preferred_element_type=jnp....]
    all_to_all x2 -> x0, local copies, waits for them, and re-layouts: 42.8 us -> none  [the longest x1 21.5 us: per_device(): lax.all_to_all(shrink_down, 'ff', split_axis=2, concat_axis=0, tiled=True)]
    dot_general x7 -> x0, matrix products: 37 us -> none  [the longest x1 9.87 us: per_device(): jnp.dot(hidden, down_weight, preferred_element_type=jnp.float32)]
    pallas_call x0 -> x9, Pallas kernels: none -> 29.6 us  [the longest x2 13.6 us: base_half(): pl.pallas_call(base_kernel, out_shape=jax.ShapeDtypeStruct((2, rows, half...]
    all_to_all x2 -> x3, waiting for transfers between devices: 0.01 us -> 28.9 us  [per_device(): lax.all_to_all(a, 'ff', split_axis=0, concat_axis=0, tiled=True)]
  transfers between devices with their start and end apart: 4 -> 8, of which waited for: 1 -> 4; matrix products, arithmetic and copies ran while one was open for 32% -> 3% of each run, Pallas kernels for 0% -> 17%
where the time goes in v1:
time: 124 us; the launch traced here: 123 us
  waiting for transfers between devices  30.1 us (24%)
  Pallas kernels  29.6 us (24%)
  local copies, waits for them, and re-layouts  25.1 us (20%)
  blocking collectives  18.6 us (15%)
  starting transfers between devices  16.8 us (14%)
  other arithmetic  2.53 us (2%)
    all_to_all x3, waiting for transfers between devices, per_device(): lax.all_to_all(a, 'ff', split_axis=0, concat_axis=0, tiled=True)  28.9 us
    unnamed x16, local copies, waits for them, and re-layouts  23.3 us
    all_to_all x1, blocking collectives, per_device(): lax.all_to_all(a, 'ff', split_axis=0, concat_axis=0, tiled=True)  18.6 us
    all_to_all x3, starting transfers between devices, per_device(): lax.all_to_all(a, 'ff', split_axis=0, concat_axis=0, tiled=True)  15.8 us
    pallas_call x2, Pallas kernels, base_half(): pl.pallas_call(base_kernel, out_shape=jax.ShapeDtypeStruct((2, rows, half...  13.6 us
    pallas_call x1, Pallas kernels, down_base(): pl.pallas_call(down_kernel, out_shape=jax.ShapeDtypeStruct((rows, width),...  5.35 us
    pallas_call x1, Pallas kernels, expand_rows(): pl.pallas_call(expand_kernel, out_shape=jax.ShapeDtypeStruct((shards, 2 *...  4.05 us
    pallas_call x1, Pallas kernels, hidden_half(): pl.pallas_call(hidden_kernel, out_shape=(jax.ShapeDtypeStruct((rows, half...  2.75 us
  transfers between devices with their start and end apart: 8, of which 4 were waited for; matrix products, arithmetic and copies ran while one was open for 3% of the time, Pallas kernels for 17%

profile of v1, /device:TPU:0, one launch (start us, length us, event | category | flops | bytes accessed | tf_op | source)
XLA Modules:
  0.0 123.0 jit_solution(12180327718339484327)
XLA Ops:
  0.0 1.6 %copy-done.3 = bf16[4,2,8,16384]{3,2,1,0:T(8,128)(2,1)S(1)} copy-done((bf16[4,2,8,16384]{3,2,1,0:T(8,128)(2,1)S(1)}, bf16[4,2,8,16384]{3,2,1,0:T(8,128)(2,1)}, u32[]{:S(2)}) %copy-start.3) | copy-done | bytes 2097176
  2.5 1.7 %broadcast_in_dim.22 = bf16[8,8,4096]{2,1,0:T(8,128)(2,1)} broadcast(bf16[8,4096]{1,0:T(8,128)(2,1)} %param.10), dimensions={1,2} | broadcast | bytes 589824 | tf_op jit(solution)/shard_map/broadcast_in_dim | solution.py:295
  4.2 6.8 %all-to-all-start = ((bf16[8,8,4096]{2,1,0:T(8,128)(2,1)}), bf16[8,8,4096]{2,1,0:T(8,128)(2,1)S(1)}, u32[]{:S(2)}, u32[]{:S(2)}) async-start(bf16[8,8,4096]{2,1,0:T(8,128)(2,1)} %broadcast_in_dim.22), calls=%async_computation | async-start | bytes 1048576 | tf_op jit(solution)/shard_map/all_to_all | solution.py:293
  11.1 0.8 select_reduce_fusion.1
  12.6 13.6 %all-to-all-done = bf16[8,8,4096]{2,1,0:T(8,128)(2,1)S(1)} async-done(((bf16[8,8,4096]{2,1,0:T(8,128)(2,1)}), bf16[8,8,4096]{2,1,0:T(8,128)(2,1)S(1)}, u32[]{:S(2)}, u32[]{:S(2)}) %all-to-all-start) | async-done | bytes 524320 | tf_op jit(solution)/shard_map/all_to_all | solution.py:293
  26.2 1.2 copy-done.6
  28.0 1.2 collective-permute-done.1.got_ref
  29.2 1.6 %copy-done.4 = bf16[4,2,8,16384]{3,2,1,0:T(8,128)(2,1)S(1)} copy-done((bf16[4,2,8,16384]{3,2,1,0:T(8,128)(2,1)S(1)}, bf16[4,2,8,16384]{3,2,1,0:T(8,128)(2,1)}, u32[]{:S(2)}) %copy-start.4) | copy-done | bytes 2097176
  30.8 4.1 %shard_map.104 = bf16[8,64,1024]{2,1,0:T(8,128)(2,1)} custom-call(s32[1]{0:T(128)} %bitcast.side_ref.core_ref, f32[64,128]{1,0:T(8,128)S(1)} %shard_map.102.own_ref, f32[64,128]{1,0:T(8,128)S(1)} %collective-permute-done.1.got_ref, bf16[32,64]{1,0:T(8,128)(2,1)S(1)} %fusion.4.pick_ref, bf16[2,2,128,64]{3,2,1,0:T(8,128)(2,1)S(1)} %and_convert_fusion.cols_ref, ...), custom_call_target="tpu_custom_call" | custom-call | flops 134217728 | bytes 3145728 | tf_op jit(solution)/shard_map/pallas_call | solution.py:89
  34.8 3.6 %all-to-all-start.1 = ((bf16[8,64,1024]{2,1,0:T(8,128)(2,1)}), bf16[8,64,1024]{2,1,0:T(8,128)(2,1)S(1)}, u32[]{:S(2)}, u32[]{:S(2)}) async-start(bf16[8,64,1024]{2,1,0:T(8,128)(2,1)} %shard_map.104), calls=%async_computation.1 | async-start | bytes 2097152 | tf_op jit(solution)/shard_map/all_to_all | solution.py:293
  38.7 5.8 %copy-done.1 = bf16[4096,2048]{1,0:T(8,128)(2,1)S(1)} copy-done((bf16[4096,2048]{1,0:T(8,128)(2,1)S(1)}, bf16[4096,2048]{1,0:T(8,128)(2,1)}, u32[]{:S(2)}) %copy-start.1) | copy-done | bytes 16777240
  44.4 6.8 %shard_map.101 = bf16[2,64,1024]{2,1,0:T(8,128)(2,1)S(1)} custom-call(s32[1]{0:T(128)S(6)} %sub.52.side_ref, bf16[64,4096]{1,0:T(8,128)(2,1)S(1)} %bitcast.12, bf16[4096,2048]{1,0:T(8,128)(2,1)S(1)} %copy-done.1, bf16[4096,2048]{1,0:T(8,128)(2,1)} %up_ref.3), custom_call_target="tpu_custom_call" | custom-call | flops 1073741824 | bytes 17301504 | tf_op jit(solution)/shard_map/pallas_call | solution.py:121
  51.4 5.8 %copy-done.2 = bf16[4096,2048]{1,0:T(8,128)(2,1)S(1)} copy-done((bf16[4096,2048]{1,0:T(8,128)(2,1)S(1)}, bf16[4096,2048]{1,0:T(8,128)(2,1)}, u32[]{:S(2)}) %copy-start.2) | copy-done | bytes 16777240
  57.2 6.8 %shard_map.100.own_ref = f32[2,64,1024]{2,1,0:T(8,128)S(1)} custom-call(s32[1]{0:T(128)} %bitcast.side_ref.core_ref, bf16[64,4096]{1,0:T(8,128)(2,1)S(1)} %bitcast.13, bf16[4096,2048]{1,0:T(8,128)(2,1)S(1)} %copy-done.2, bf16[4096,2048]{1,0:T(8,128)(2,1)} %up_ref.3), custom_call_target="tpu_custom_call" | custom-call | flops 1073741824 | bytes 17301504 | tf_op jit(solution)/shard_map/pallas_call | solution.py:121
  64.7 2.8 %shard_map.105 = (bf16[64,1024]{1,0:T(8,128)(2,1)S(1)}, bf16[256,1024]{1,0:T(8,128)(2,1)}) custom-call(f32[2,64,1024]{2,1,0:T(8,128)S(1)} %shard_map.100.own_ref, bf16[2,64,1024]{2,1,0:T(8,128)(2,1)S(1)} %collective-permute-done.got_ref, bf16[512,1024]{1,0:T(8,128)(2,1)S(1)} %bitcast.16, bf16[128,512]{1,0:T(8,128)(2,1)S(1)} %fusion.place_ref, ...), custom_call_target="tpu_custom_call" | custom-call | flops 167772160 | bytes 2359296 | tf_op jit(solution)/shard_map/pallas_call | solution.py:149
  67.4 5.3 %all-to-all-start.2 = ((bf16[8,32,1024]{2,1,0:T(8,128)(2,1)}), bf16[8,32,1024]{2,1,0:T(8,128)(2,1)S(1)}, u32[]{:S(2)}, u32[]{:S(2)}) async-start(bf16[8,32,1024]{2,1,0:T(8,128)(2,1)} %bitcast.7), calls=%async_computation.2 | async-start | bytes 1048576 | tf_op jit(solution)/shard_map/all_to_all | solution.py:293
  73.2 14.7 %all-to-all-done.2.hid_ref = bf16[8,32,1024]{2,1,0:T(8,128)(2,1)S(1)} async-done(((bf16[8,32,1024]{2,1,0:T(8,128)(2,1)}), bf16[8,32,1024]{2,1,0:T(8,128)(2,1)S(1)}, u32[]{:S(2)}, u32[]{:S(2)}) %all-to-all-start.2) | async-done | bytes 524320 | tf_op jit(solution)/shard_map/all_to_all | solution.py:293
  87.9 1.6 %copy-done.5 = bf16[4,16,16384]{2,1,0:T(8,128)(2,1)S(1)} copy-done((bf16[4,16,16384]{2,1,0:T(8,128)(2,1)S(1)}, bf16[4,16,16384]{2,1,0:T(8,128)(2,1)}, u32[]{:S(2)}) %copy-start.5) | copy-done | bytes 2097176
  89.4 1.5 %shard_map.107.own_ref = f32[32,64]{1,0:T(8,128)S(1)} custom-call(s32[1]{0:T(128)} %bitcast.side_ref.core_ref, bf16[8,32,1024]{2,1,0:T(8,128)(2,1)S(1)} %all-to-all-done.2.hid_ref, bf16[64,16384]{1,0:T(8,128)(2,1)S(1)} %bitcast.17, f32[32,64]{1,0:T(8,128)S(1)} %compare_convert_fusion.1.mask_ref), custom_call_target="tpu_custom_call" | custom-call | flops 33554432 | bytes 1572864 | tf_op jit(solution)/shard_map/pallas_call | solution.py:218
  91.0 5.8 %copy-done = bf16[2048,4096]{1,0:T(8,128)(2,1)S(1)} copy-done((bf16[2048,4096]{1,0:T(8,128)(2,1)S(1)}, bf16[2048,4096]{1,0:T(8,128)(2,1)}, u32[]{:S(2)}) %copy-start) | copy-done | bytes 16777240
  96.8 5.3 %shard_map.106.base_ref = f32[64,4096]{1,0:T(8,128)S(1)} custom-call(s32[1]{0:T(128)} %bitcast.side_ref.core_ref, bf16[64,1024]{1,0:T(8,128)(2,1)S(1)} %get-tuple-element.7.near_ref, bf16[64,1024]{1,0:T(8,128)(2,1)S(1)} %collective-permute-done.3.far_ref, bf16[2048,4096]{1,0:T(8,128)(2,1)S(1)} %copy-done, bf16[2048,4096]{1,0:T(8,128)(2,1)S(1)} %copy-done), custom_call_target="tpu_custom_call" | custom-call | flops 1073741824 | bytes 17825792 | tf_op jit(solution)/shard_map/pallas_call | solution.py:182
  102.1 1.5 %shard_map.108 = bf16[64,4096]{1,0:T(8,128)(2,1)S(1)} custom-call(f32[64,4096]{1,0:T(8,128)S(1)} %shard_map.106.base_ref, f32[32,64]{1,0:T(8,128)S(1)} %shard_map.107.own_ref, f32[32,64]{1,0:T(8,128)S(1)} %collective-permute-done.4.got_ref, bf16[32,64]{1,0:T(8,128)(2,1)S(1)} %fusion.4.pick_ref, bf16[64,4096]{1,0:T(8,128)(2,1)S(1)} %bitcast.20), custom_call_target="tpu_custom_call" | custom-call | flops 33554432 | bytes 2097152 | tf_op jit(solution)/shard_map/pallas_call | solution.py:249
  103.7 18.6 %all_to_all.20 = bf16[8,8,4096]{2,1,0:T(8,128)(2,1)S(1)} all-to-all(bf16[8,8,4096]{2,1,0:T(8,128)(2,1)S(1)} %bitcast.18), channel_id=1, replica_groups=mesh['groups'=2,'ff'=8,'var'=2] {'ff'}, dimensions={0} | all-to-all | bytes 1048576 | tf_op jit(solution)/shard_map/all_to_all | solution.py:293
  122.3 0.7 reduce_sum.42
  (45 shorter events, 3.9 us)
Async XLA Ops:
  0.0 1.6 %copy-start.3 = (bf16[4,2,8,16384]{3,2,1,0:T(8,128)(2,1)S(1)}, bf16[4,2,8,16384]{3,2,1,0:T(8,128)(2,1)}, u32[]{:S(2)}) copy-start(bf16[4,2,8,16384]{3,2,1,0:T(8,128)(2,1)} %param.15) | copy-start | bytes 6291460
  2.0 27.2 %collective-permute-start.2 = (bf16[64,8192]{1,0:T(8,128)(2,1)S(1)}, bf16[64,8192]{1,0:T(8,128)(2,1)S(1)}, u32[]{:S(2)}, u32[]{:S(2)}) collective-permute-start(bf16[64,8192]{1,0:T(8,128)(2,1)S(1)} %shard_map.103), channel_id=1, source_target_pairs={{0,1},{1,0},{2,3},{3,2},{4,5},{5,4},{6,7},{7,6},{8,9},{9,8},{10,11... | collective-permute-start | bytes 3145736 | tf_op jit(solution)/shard_map/ppermute | solution.py:292
  4.2 22.0 %all-to-all-start = ((bf16[8,8,4096]{2,1,0:T(8,128)(2,1)}), bf16[8,8,4096]{2,1,0:T(8,128)(2,1)S(1)}, u32[]{:S(2)}, u32[]{:S(2)}) async-start(bf16[8,8,4096]{2,1,0:T(8,128)(2,1)} %broadcast_in_dim.22), calls=%async_computation | async-start | bytes 1048576 | tf_op jit(solution)/shard_map/all_to_all | solution.py:293
  26.2 1.2 copy-start.6
  27.9 1.3 %collective-permute-start.1 = (f32[64,128]{1,0:T(8,128)S(1)}, f32[64,128]{1,0:T(8,128)S(1)}, u32[]{:S(2)}, u32[]{:S(2)}) collective-permute-start(f32[64,128]{1,0:T(8,128)S(1)} %shard_map.102.own_ref), channel_id=1, source_target_pairs={{0,1},{1,0},{2,3},{3,2},{4,5},{5,4},{6,7},{7,6},{8,9},{9,8},{10,11... | collective-permute-start | bytes 98312 | tf_op jit(solution)/shard_map/ppermute | solution.py:292
  29.2 1.6 %copy-start.4 = (bf16[4,2,8,16384]{3,2,1,0:T(8,128)(2,1)S(1)}, bf16[4,2,8,16384]{3,2,1,0:T(8,128)(2,1)}, u32[]{:S(2)}) copy-start(bf16[4,2,8,16384]{3,2,1,0:T(8,128)(2,1)} %param.15) | copy-start | bytes 6291460
  34.8 29.9 %all-to-all-start.1 = ((bf16[8,64,1024]{2,1,0:T(8,128)(2,1)}), bf16[8,64,1024]{2,1,0:T(8,128)(2,1)S(1)}, u32[]{:S(2)}, u32[]{:S(2)}) async-start(bf16[8,64,1024]{2,1,0:T(8,128)(2,1)} %shard_map.104), calls=%async_computation.1 | async-start | bytes 2097152 | tf_op jit(solution)/shard_map/all_to_all | solution.py:293
  38.7 5.8 %copy-start.1 = (bf16[4096,2048]{1,0:T(8,128)(2,1)S(1)}, bf16[4096,2048]{1,0:T(8,128)(2,1)}, u32[]{:S(2)}) copy-start(bf16[4096,2048]{1,0:T(8,128)(2,1)} %gate_ref.3) | copy-start | bytes 50331652
  51.2 12.8 %collective-permute-start = (bf16[2,64,1024]{2,1,0:T(8,128)(2,1)S(1)}, bf16[2,64,1024]{2,1,0:T(8,128)(2,1)S(1)}, u32[]{:S(2)}, u32[]{:S(2)}) collective-permute-start(bf16[2,64,1024]{2,1,0:T(8,128)(2,1)S(1)} %shard_map.101), channel_id=1, source_target_pairs={{0,1},{1,0},{2,3},{3,2},{4,5},{5,4},{6,7},{7,6},{8,9},{9,8},{10,11... | collective-permute-start | bytes 786440 | tf_op jit(solution)/shard_map/ppermute | solution.py:292
  51.4 5.8 %copy-start.2 = (bf16[4096,2048]{1,0:T(8,128)(2,1)S(1)}, bf16[4096,2048]{1,0:T(8,128)(2,1)}, u32[]{:S(2)}) copy-start(bf16[4096,2048]{1,0:T(8,128)(2,1)} %gate_ref.3) | copy-start | bytes 50331652
  67.4 20.4 %all-to-all-start.2 = ((bf16[8,32,1024]{2,1,0:T(8,128)(2,1)}), bf16[8,32,1024]{2,1,0:T(8,128)(2,1)S(1)}, u32[]{:S(2)}, u32[]{:S(2)}) async-start(bf16[8,32,1024]{2,1,0:T(8,128)(2,1)} %bitcast.7), calls=%async_computation.2 | async-start | bytes 1048576 | tf_op jit(solution)/shard_map/all_to_all | solution.py:293
  72.8 18.2 %collective-permute-start.3 = (bf16[64,1024]{1,0:T(8,128)(2,1)S(1)}, bf16[64,1024]{1,0:T(8,128)(2,1)S(1)}, u32[]{:S(2)}, u32[]{:S(2)}) collective-permute-start(bf16[64,1024]{1,0:T(8,128)(2,1)S(1)} %get-tuple-element.7.near_ref), channel_id=1, source_target_pairs={{0,1},{1,0},{2,3},{3,2},{4,5},{5,4},{6,7},{7,6},{8,9},{9,8},{10,11... | collective-permute-start | bytes 393224 | tf_op jit(solution)/shard_map/ppermute | solution.py:292
  87.8 1.6 %copy-start.5 = (bf16[4,16,16384]{2,1,0:T(8,128)(2,1)S(1)}, bf16[4,16,16384]{2,1,0:T(8,128)(2,1)}, u32[]{:S(2)}) copy-start(bf16[4,16,16384]{2,1,0:T(8,128)(2,1)} %param.16) | copy-start | bytes 6291460
  89.4 12.7 %copy-start.7 = (bf16[4,16,4096]{2,1,0:T(8,128)(2,1)S(1)}, bf16[4,16,4096]{2,1,0:T(8,128)(2,1)}, u32[]{:S(2)}) copy-start(bf16[4,16,4096]{2,1,0:T(8,128)(2,1)} %param.17) | copy-start | bytes 1572868
  90.9 11.2 %collective-permute-start.4 = (f32[32,64]{1,0:T(8,128)S(1)}, f32[32,64]{1,0:T(8,128)S(1)}, u32[]{:S(2)}, u32[]{:S(2)}) collective-permute-start(f32[32,64]{1,0:T(8,128)S(1)} %shard_map.107.own_ref), channel_id=1, source_target_pairs={{0,1},{1,0},{2,3},{3,2},{4,5},{5,4},{6,7},{7,6},{8,9},{9,8},{10,11... | collective-permute-start | bytes 24584 | tf_op jit(solution)/shard_map/ppermute | solution.py:292
  91.0 5.8 %copy-start = (bf16[2048,4096]{1,0:T(8,128)(2,1)S(1)}, bf16[2048,4096]{1,0:T(8,128)(2,1)}, u32[]{:S(2)}) copy-start(bf16[2048,4096]{1,0:T(8,128)(2,1)} %far_weight.1) | copy-start | bytes 50331652

commit v2 on v1

v2 whole, which is shorter than its diff:
```python
import jax
import jax.numpy as jnp
from jax import lax
from jax.experimental import pallas as pl
from jax.experimental.pallas import tpu as pltpu
from jax.sharding import PartitionSpec as P

MOST = 8
DIRECT = 8
BF = jnp.bfloat16
F32 = jnp.float32
I32 = jnp.int32
MIB = 1024 * 1024


def dot(a, b):
    return jnp.dot(a, b, preferred_element_type=F32)


def dot_last(a, b):
    return lax.dot_general(a, b, (((1,), (1,)), ((), ())), preferred_element_type=F32)


def params(mib):
    return pltpu.CompilerParams(vmem_limit_bytes=mib * MIB)


def cost(flops, moved):
    return pl.CostEstimate(flops=flops, bytes_accessed=moved, transcendentals=0)


def fixed(array):
    zeros = (0,) * array.ndim
    return pl.BlockSpec(array.shape, lambda *_: zeros)


class Ways:
    def __init__(self):
        self.shards = lax.axis_size("ff")
        self.fast = 2 if self.shards % 2 == 0 else 1
        self.slow = self.shards // self.fast
        self.direct = self.shards <= DIRECT
        me = lax.axis_index("ff").astype(I32)
        steps = jnp.arange(self.shards, dtype=I32)
        if self.direct:
            slow = (me // self.fast - steps // self.fast) % self.slow
            fast = (me % self.fast - steps % self.fast) % self.fast
            self.order = slow * self.fast + fast
        else:
            self.order = steps

    def back(self, a, c):
        S, F = self.slow, self.fast
        return [(s * F + f, (s - a) % S * F + (f - c) % F) for s in range(S) for f in range(F)]

    def gather(self, block):
        if not self.direct:
            return list(lax.all_gather(block, "ff"))
        got = [None] * self.shards
        for a in range(self.slow):
            got[a * self.fast] = lax.ppermute(block, "ff", self.back(-a, 0)) if a else block
        for a in range(self.slow):
            for c in range(1, self.fast):
                got[a * self.fast + c] = lax.ppermute(
                    got[a * self.fast], "ff", self.back(0, -c)
                )
        return got

    def deliver(self, blocks):
        if not self.direct:
            return list(lax.all_to_all(jnp.stack(blocks), "ff", 0, 0, tiled=True))
        got = [None] * self.shards
        got[0] = blocks[0]
        for b in range(1, self.shards):
            a, c = b // self.fast, b % self.fast
            back = (-a) % self.slow * self.fast + (-c) % self.fast
            got[back] = lax.ppermute(blocks[b], "ff", self.back(a, c))
        return got


def copy_kernel(at_ref, in_ref, out_ref):
    out_ref[...] = in_ref[...]


def pick_columns(at, factors, half):
    depth, count = factors.shape[0], at.shape[0]
    return pl.pallas_call(
        copy_kernel,
        out_shape=jax.ShapeDtypeStruct((depth, count * half), factors.dtype),
        grid_spec=pltpu.PrefetchScalarGridSpec(
            num_scalar_prefetch=1,
            grid=(count,),
            in_specs=[pl.BlockSpec((depth, half), lambda j, at: (0, at[j]))],
            out_specs=pl.BlockSpec((depth, half), lambda j, at: (0, j)),
        ),
        compiler_params=params(8),
        cost_estimate=cost(0, 4 * depth * count * half),
    )(at, factors)


def low_in_kernel(count, shrink_ref, mask_ref, *refs):
    parts, x_ref, out_ref = refs[:count], refs[count], refs[count + 1]
    x = jnp.concatenate([part[...].astype(F32) for part in parts], axis=0).astype(BF)
    x_ref[...] = x

    @pl.when(pl.program_id(0) == 0)
    def _():
        out_ref[...] = jnp.zeros_like(out_ref)

    out_ref[...] += jnp.where(mask_ref[...] > 0, dot_last(x, shrink_ref[...]), 0.0)


def low_in_pairs(parts, shrink, mask):
    count = len(parts)
    own_rows, width = parts[0].shape
    rows, block = count * own_rows, min(1024, width)
    return pl.pallas_call(
        lambda *refs: low_in_kernel(count, *refs),
        out_shape=(
            jax.ShapeDtypeStruct((rows, width), BF),
            jax.ShapeDtypeStruct(mask.shape, F32),
        ),
        grid=(width // block,),
        in_specs=[pl.BlockSpec((shrink.shape[0], block), lambda n: (0, n)), fixed(mask)]
        + [pl.BlockSpec((own_rows, block), lambda n: (0, n))] * count,
        out_specs=(pl.BlockSpec((rows, block), lambda n: (0, n)), fixed(mask)),
        compiler_params=params(16),
        cost_estimate=cost(2 * rows * width * shrink.shape[0], 2 * shrink.size + 4 * rows * width),
    )(shrink, mask, *parts)


def expand_kernel(count, at_ref, own_ref, got_ref, pick_ref, cols_ref, far_ref, *refs):
    near_refs, out_refs = refs[:count], refs[count:]
    cap = pick_ref.shape[0]
    half = out_refs[0].shape[1]
    low = (own_ref[...] + got_ref[...]).astype(BF)
    picked = dot(pick_ref[...], low).astype(BF)
    lhs = [
        jnp.concatenate([dot(picked, cols_ref[kind, side]) for kind in range(2)], axis=0)
        for side in range(2)
    ]
    lhs = [side.astype(BF) for side in lhs]
    for b in range(count):
        far = far_ref[:, b * half : (b + 1) * half]
        out_refs[b][...] = (dot(lhs[0], near_refs[b][...]) + dot(lhs[1], far)).astype(BF)


def expand_rows(at, own, got, pick, cols, near, far, half):
    cap, count, depth = pick.shape[0], at.shape[0], near.shape[0]
    column = lambda b: pl.BlockSpec((depth, half), lambda i, at: (0, at[b]))
    out = jax.ShapeDtypeStruct((2 * cap, half), BF)
    return pl.pallas_call(
        lambda *refs: expand_kernel(count, *refs),
        out_shape=(out,) * count,
        grid_spec=pltpu.PrefetchScalarGridSpec(
            num_scalar_prefetch=1,
            grid=(1,),
            in_specs=[fixed(own), fixed(got), fixed(pick), fixed(cols), fixed(far)]
            + [column(b) for b in range(count)],
            out_specs=(fixed(out),) * count,
        ),
        compiler_params=params(16),
        cost_estimate=cost(8 * cap * depth * count * half, 4 * (depth + cap) * count * half),
    )(at, own, got, pick, cols, far, *[near] * count)


def base_kernel(side_ref, x_ref, gate_ref, up_ref, out_ref, gate_sum, up_sum):
    step = pl.program_id(0)

    @pl.when(step == 0)
    def _():
        gate_sum[...] = jnp.zeros_like(gate_sum)
        up_sum[...] = jnp.zeros_like(up_sum)

    gate_sum[...] += dot(x_ref[...], gate_ref[...])
    up_sum[...] += dot(x_ref[...], up_ref[...])

    @pl.when(step == pl.num_programs(0) - 1)
    def _():
        out_ref[0] = gate_sum[...].astype(out_ref.dtype)
        out_ref[1] = up_sum[...].astype(out_ref.dtype)


def base_half(side, x, gate_weight, up_weight, half, kind):
    rows, width = x.shape
    block = min(512, width)
    weight = pl.BlockSpec((block, half), lambda n, side: (n, side[0]))
    return pl.pallas_call(
        base_kernel,
        out_shape=jax.ShapeDtypeStruct((2, rows, half), kind),
        grid_spec=pltpu.PrefetchScalarGridSpec(
            num_scalar_prefetch=1,
            grid=(width // block,),
            in_specs=[pl.BlockSpec((rows, block), lambda n, side: (0, n)), weight, weight],
            out_specs=pl.BlockSpec((2, rows, half), lambda n, side: (0, 0, 0)),
            scratch_shapes=[pltpu.VMEM((rows, half), F32), pltpu.VMEM((rows, half), F32)],
        ),
        compiler_params=params(56),
        cost_estimate=cost(4 * rows * width * half, 4 * width * half + 2 * rows * width),
    )(side, x, gate_weight, up_weight)


def hidden_kernel(count, own_ref, got_ref, place_ref, send_ref, *refs):
    parts, hid_ref, out_refs = refs[:count], refs[count], refs[count + 1 :]
    rows = hid_ref.shape[0]
    cap = out_refs[0].shape[0]
    delta = dot(place_ref[...], jnp.concatenate([part[...] for part in parts], axis=0))
    gate = own_ref[0] + got_ref[0].astype(F32) + delta[:rows]
    up = own_ref[1] + got_ref[1].astype(F32) + delta[rows:]
    hidden = (gate / (1.0 + jnp.exp(-gate)) * up).astype(BF)
    hid_ref[...] = hidden
    sent = dot(send_ref[...], hidden).astype(BF)
    for b in range(count):
        out_refs[b][...] = sent[b * cap : (b + 1) * cap]


def hidden_half(own, got, parts, place, send):
    count = len(parts)
    rows, half = own.shape[1:]
    block = min(256, half)
    cap = send.shape[0] // count
    both = pl.BlockSpec((2, rows, block), lambda n: (0, 0, n))
    flat = lambda depth: pl.BlockSpec((depth, block), lambda n: (0, n))
    return pl.pallas_call(
        lambda *refs: hidden_kernel(count, *refs),
        out_shape=(jax.ShapeDtypeStruct((rows, half), BF),)
        + (jax.ShapeDtypeStruct((cap, half), BF),) * count,
        grid=(half // block,),
        in_specs=[both, both, fixed(place), fixed(send)] + [flat(parts[0].shape[0])] * count,
        out_specs=(flat(rows),) + (flat(cap),) * count,
        compiler_params=params(40),
        cost_estimate=cost(
            2 * half * (place.size + send.size), 2 * half * (6 * rows + 3 * count * cap)
        ),
    )(own, got, place, send, *parts)


def down_kernel(core_ref, near_ref, far_ref, near_weight, far_weight, out_ref):
    out_ref[...] = dot(near_ref[...], near_weight[...]) + dot(far_ref[...], far_weight[...])


def down_base(core, near, far, weight):
    rows, half = near.shape
    width = weight.shape[1]
    block = min(512, width)
    return pl.pallas_call(
        down_kernel,
        out_shape=jax.ShapeDtypeStruct((rows, width), F32),
        grid_spec=pltpu.PrefetchScalarGridSpec(
            num_scalar_prefetch=1,
            grid=(width // block,),
            in_specs=[
                fixed(near),
                fixed(far),
                pl.BlockSpec((half, block), lambda n, core: (core[0], n)),
                pl.BlockSpec((half, block), lambda n, core: (1 - core[0], n)),
            ],
            out_specs=pl.BlockSpec((rows, block), lambda n, core: (0, n)),
        ),
        compiler_params=params(56),
        cost_estimate=cost(4 * rows * half * width, 4 * half * width + 4 * rows * width),
    )(core, near, far, weight, weight)


def low_out_kernel(count, at_ref, mask_ref, *refs):
    parts, shrinks, out_ref = refs[:count], refs[count : 2 * count], refs[2 * count]
    pairs = sum(dot_last(part[...], shrink[...]) for part, shrink in zip(parts, shrinks))
    out_ref[...] = jnp.where(mask_ref[...] > 0, pairs, 0.0)


def low_out_pairs(at, parts, shrink, mask):
    count = len(parts)
    cap, half = parts[0].shape
    depth = shrink.shape[0]
    column = lambda b: pl.BlockSpec((depth, half), lambda i, at: (0, at[b]))
    return pl.pallas_call(
        lambda *refs: low_out_kernel(count, *refs),
        out_shape=jax.ShapeDtypeStruct((cap, depth), F32),
        grid_spec=pltpu.PrefetchScalarGridSpec(
            num_scalar_prefetch=1,
            grid=(1,),
            in_specs=[fixed(mask)]
            + [fixed(part) for part in parts]
            + [column(b) for b in range(count)],
            out_specs=fixed(mask),
        ),
        compiler_params=params(16),
        cost_estimate=cost(2 * cap * depth * count * half, 2 * count * half * (depth + cap)),
    )(at, mask, *parts, *[shrink] * count)


def add_kernel(base_ref, own_ref, got_ref, pick_ref, expand_ref, *out_refs):
    low = (own_ref[...] + got_ref[...]).astype(BF)
    spread = lax.dot_general(
        pick_ref[...], low, (((0,), (0,)), ((), ())), preferred_element_type=F32
    ).astype(BF)
    total = base_ref[...] + dot(spread, expand_ref[...])
    own_rows = out_refs[0].shape[0]
    for b, out_ref in enumerate(out_refs):
        out_ref[...] = total[b * own_rows : (b + 1) * own_rows].astype(BF)


def add_delta(base, own, got, pick, expand, count):
    rows, width = base.shape
    block = min(1024, width)
    depth = expand.shape[0]
    flat = lambda tall: pl.BlockSpec((tall, block), lambda n: (0, n))
    return pl.pallas_call(
        add_kernel,
        out_shape=(jax.ShapeDtypeStruct((rows // count, width), BF),) * count,
        grid=(width // block,),
        in_specs=[flat(rows), fixed(own), fixed(got), fixed(pick), flat(depth)],
        out_specs=(flat(rows // count),) * count,
        compiler_params=params(24),
        cost_estimate=cost(2 * rows * depth * width, width * (6 * rows + 2 * depth)),
    )(base, own, got, pick, expand)


def per_device(
    tokens,
    gate_weight,
    up_weight,
    down_weight,
    shrink_gu,
    expand_gu,
    shrink_down,
    expand_down,
    variant_ids,
    variant_slot,
):
    ways = Ways()
    shards, order = ways.shards, ways.order
    me = lax.axis_index("ff").astype(I32)
    core = lax.axis_index("var").astype(I32)
    own_rows, width = tokens.shape
    rows = own_rows * shards
    slots = shrink_gu.shape[0]
    variants = variant_slot.shape[0]
    rank = shrink_down.shape[1]
    half_rank = expand_gu.shape[2]
    half = gate_weight.shape[1] // 2
    cap = min(slots * MOST, rows)
    here = core.reshape(1)
    there = 1 - here
    at_here = 2 * order + core
    at_there = 2 * order + 1 - core
    swap = lambda a: lax.ppermute(a, "var", [(0, 1), (1, 0)])

    token_parts = ways.gather(tokens)

    near = expand_gu.reshape(slots * 2 * half_rank, -1)
    far = swap(pick_columns(at_there, near, half))

    ids = variant_ids[:, 0]
    matches = ids[:, None] == jnp.arange(variants, dtype=I32)[None, :]
    slot_row = jnp.sum(jnp.where(matches, variant_slot[None, :], 0), axis=1)
    owner = slot_row // slots
    index = jnp.arange(rows, dtype=I32)
    earlier = (owner[:, None] == owner[None, :]) & (index[None, :] < index[:, None])
    place = jnp.sum(earlier.astype(I32), axis=1)
    where_row = order[:, None] == jnp.arange(shards, dtype=I32)[None, :]
    turn = lambda a: jnp.sum(
        jnp.where(where_row[:, :, None], a.reshape(1, shards, own_rows), 0), axis=1
    ).reshape(rows)
    slot_row, place = turn(slot_row), turn(place)
    owner = slot_row // slots
    step = jnp.sum(
        jnp.where(owner[:, None] == order[None, :], jnp.arange(shards, dtype=I32)[None, :], 0),
        axis=1,
    )
    cells = jnp.arange(shards * cap, dtype=I32)
    send_rows = (cells[:, None] == (step * cap + place)[None, :]).astype(BF)
    kinds = jnp.arange(2, dtype=I32)
    kind_cell = (step * 2 + kinds[:, None]) * cap + place
    kind_cells = jnp.arange(2 * shards * cap, dtype=I32)
    place_rows = (kind_cell[:, :, None] == kind_cells).astype(BF).reshape(2 * rows, -1)
    spots = jnp.arange(cap, dtype=I32)
    picked = (spots[:, None] == place[None, :]) & (owner[None, :] == me)
    pick = picked.astype(BF)
    local = slot_row - me * slots
    in_cols = jnp.arange(slots * 2 * rank, dtype=I32)
    mask_in = (local[:, None] == (in_cols // (2 * rank))[None, :]).astype(F32)
    spot_slot = jnp.sum(jnp.where(picked, local[None, :] + 1, 0), axis=1) - 1
    out_cols = jnp.arange(slots * rank, dtype=I32)
    mask_out = (spot_slot[:, None] == (out_cols // rank)[None, :]).astype(F32)
    rank_at = in_cols % rank
    kind_at = in_cols // rank % 2
    row_at = in_cols // (2 * rank) * (2 * half_rank) + kind_at * half_rank + rank_at % half_rank
    near_cols = jnp.arange(slots * 2 * half_rank, dtype=I32)
    hit = row_at[:, None] == near_cols[None, :]
    side = jnp.stack([core, 1 - core])
    cols = (
        hit[None, None]
        & (kind_at[None, :] == kinds[:, None])[:, None, :, None]
        & ((rank_at // half_rank)[None, :] == side[:, None])[None, :, :, None]
    ).astype(BF)

    x, low_own = low_in_pairs(token_parts, shrink_gu.reshape(slots * 2 * rank, width), mask_in)
    low_got = swap(low_own)
    base_got = swap(base_half(there, x, gate_weight, up_weight, half, BF))
    delta = ways.deliver(expand_rows(at_here, low_own, low_got, pick, cols, near, far, half))
    base_own = base_half(here, x, gate_weight, up_weight, half, F32)
    hidden, *sent = hidden_half(base_own, base_got, delta, place_rows, send_rows)
    hidden_far = swap(hidden)
    hidden_rows = ways.deliver(sent)
    base = down_base(here, hidden, hidden_far, down_weight)
    out_own = low_out_pairs(at_here, hidden_rows, shrink_down.reshape(slots * rank, -1), mask_out)
    out_got = swap(out_own)
    expand = expand_down.reshape(slots * rank, width)
    parts = ways.deliver(add_delta(base, out_own, out_got, pick, expand, shards))
    return sum(part.astype(F32) for part in parts).astype(BF)


def solution(mesh):
    placed = (
        P(("groups", "ff"), "var"),
        P("var", "ff"),
        P("var", "ff"),
        P("ff", "var"),
        P(("groups", "ff"), None, "var"),
        P(("groups", "ff"), None, "var", None),
        P(("groups", "ff"), None, None),
        P(("groups", "ff"), None, "var"),
        P("groups", None),
        P("groups"),
    )
    return jax.shard_map(
        per_device,
        mesh=mesh,
        in_specs=placed,
        out_specs=P(("groups", "ff"), "var"),
        check_vma=False,
    )
```

time: 124 us -> 114 us (0.919)
  starting transfers between devices: 16.8 us -> 49.5 us
  blocking collectives: 18.6 us -> 0 us
  local copies, waits for them, and re-layouts: 25.1 us -> 7.94 us
  waiting for transfers between devices: 30.1 us -> 14.4 us
  Pallas kernels: 29.6 us -> 38.8 us
    ppermute x0 -> x28, starting transfers between devices: none -> 48.8 us  [the longest x21 37.8 us: deliver(): got[back] = lax.ppermute(blocks[b], 'ff', self.back(a, c))]
    all_to_all x3 -> x0, waiting for transfers between devices: 28.9 us -> none  [per_device(): lax.all_to_all(a, 'ff', split_axis=0, concat_axis=0, tiled=True)]
    all_to_all x1 -> x0, blocking collectives: 18.6 us -> none  [per_device(): lax.all_to_all(a, 'ff', split_axis=0, concat_axis=0, tiled=True)]
    unnamed x16 -> x22, local copies, waits for them, and re-layouts: 23.3 us -> 7.36 us
    all_to_all x3 -> x0, starting transfers between devices: 15.8 us -> none  [per_device(): lax.all_to_all(a, 'ff', split_axis=0, concat_axis=0, tiled=True)]
    ppermute x0 -> x28, waiting for transfers between devices: none -> 14.4 us  [the longest x21 9.63 us: deliver(): got[back] = lax.ppermute(blocks[b], 'ff', self.back(a, c))]
    pallas_call x2, Pallas kernels: 13.6 us -> 20.6 us  [base_half(): pl.pallas_call(base_kernel, out_shape=jax.ShapeDtypeStruct((2, rows, half...]
    pallas_call x1, Pallas kernels: 5.35 us -> 10.2 us  [down_base(): pl.pallas_call(down_kernel, out_shape=jax.ShapeDtypeStruct((rows, width),...]
  transfers between devices with their start and end apart: 8 -> 33, of which waited for: 4 -> 10; matrix products, arithmetic and copies ran while one was open for 3% -> 2% of each run, Pallas kernels for 17% -> 31%
where the time goes in v2:
time: 114 us
  starting transfers between devices  49.5 us (43%)
  Pallas kernels  38.8 us (34%)
  waiting for transfers between devices  14.4 us (13%)
  local copies, waits for them, and re-layouts  7.94 us (7%)
  other arithmetic  2.83 us (2%)
    ppermute x21, starting transfers between devices, deliver(): got[back] = lax.ppermute(blocks[b], 'ff', self.back(a, c))  37.8 us
    pallas_call x2, Pallas kernels, base_half(): pl.pallas_call(base_kernel, out_shape=jax.ShapeDtypeStruct((2, rows, half...  20.6 us
    pallas_call x1, Pallas kernels, down_base(): pl.pallas_call(down_kernel, out_shape=jax.ShapeDtypeStruct((rows, width),...  10.2 us
    ppermute x21, waiting for transfers between devices, deliver(): got[back] = lax.ppermute(blocks[b], 'ff', self.back(a, c))  9.63 us
    unnamed x22, local copies, waits for them, and re-layouts  7.36 us
    ppermute x3, starting transfers between devices, gather(): lax.ppermute(block, 'ff', self.back(-a, 0))  6.96 us
    ppermute x4, waiting for transfers between devices, gather(): lax.ppermute(got[a * self.fast], 'ff', self.back(0, -c))  4.75 us
    ppermute x4, starting transfers between devices, gather(): lax.ppermute(got[a * self.fast], 'ff', self.back(0, -c))  4.12 us
  transfers between devices with their start and end apart: 33, of which 10 were waited for; matrix products, arithmetic and copies ran while one was open for 2% of the time, Pallas kernels for 31%

profile of v2, /device:TPU:0, one launch (start us, length us, event | category | flops | bytes accessed | tf_op | source)
XLA Modules:
  0.0 113.7 jit_solution(17005945806500055395)
XLA Ops:
  0.0 3.0 %collective-permute-start.1 = (bf16[8,4096]{1,0:T(8,128)(2,1)}, bf16[8,4096]{1,0:T(8,128)(2,1)S(1)}, u32[]{:S(2)}, u32[]{:S(2)}) collective-permute-start(bf16[8,4096]{1,0:T(8,128)(2,1)} %refs_2_.1), channel_id=1, source_target_pairs={{0,4},{2,6},{4,8},{6,10},{8,12},{10,14},{12,0},{14,2},{1,5},{3,7},... | collective-permute-start | bytes 196616 | tf_op jit(solution)/shard_map/ppermute | solution.py:61
  3.0 2.6 %collective-permute-start.3 = (bf16[8,4096]{1,0:T(8,128)(2,1)}, bf16[8,4096]{1,0:T(8,128)(2,1)S(1)}, u32[]{:S(2)}, u32[]{:S(2)}) collective-permute-start(bf16[8,4096]{1,0:T(8,128)(2,1)} %refs_2_.1), channel_id=1, source_target_pairs={{0,8},{2,10},{4,12},{6,14},{8,0},{10,2},{12,4},{14,6},{1,9},{3,11}... | collective-permute-start | bytes 196616 | tf_op jit(solution)/shard_map/ppermute | solution.py:61
  7.0 1.5 %collective-permute-start = (bf16[8,4096]{1,0:T(8,128)(2,1)}, bf16[8,4096]{1,0:T(8,128)(2,1)S(1)}, u32[]{:S(2)}, u32[]{:S(2)}) collective-permute-start(bf16[8,4096]{1,0:T(8,128)(2,1)} %refs_2_.1), channel_id=1, source_target_pairs={{0,2},{2,0},{4,6},{6,4},{8,10},{10,8},{12,14},{14,12},{1,3},{3,1},... | collective-permute-start | bytes 196616 | tf_op jit(solution)/shard_map/ppermute | solution.py:64
  8.5 1.6 %copy-done = bf16[4,2,8,16384]{3,2,1,0:T(8,128)(2,1)S(1)} copy-done((bf16[4,2,8,16384]{3,2,1,0:T(8,128)(2,1)S(1)}, bf16[4,2,8,16384]{3,2,1,0:T(8,128)(2,1)}, u32[]{:S(2)}) %copy-start) | copy-done | bytes 2097176
  14.3 1.5 %collective-permute-start.4 = (bf16[8,4096]{1,0:T(8,128)(2,1)S(1)}, bf16[8,4096]{1,0:T(8,128)(2,1)S(1)}, u32[]{:S(2)}, u32[]{:S(2)}) collective-permute-start(bf16[8,4096]{1,0:T(8,128)(2,1)S(1)} %collective-permute-done.3.refs_6_), channel_id=1, source_target_pairs={{0,2},{2,0},{4,6},{6,4},{8,10},{10,8},{12,14},{14,12},{1,3},{3,1},... | collective-permute-start | bytes 196616 | tf_op jit(solution)/shard_map/ppermute | solution.py:64
  16.3 2.3 %collective-permute-done.2.refs_5_ = bf16[8,4096]{1,0:T(8,128)(2,1)S(1)} collective-permute-done((bf16[8,4096]{1,0:T(8,128)(2,1)S(1)}, bf16[8,4096]{1,0:T(8,128)(2,1)S(1)}, u32[]{:S(2)}, u32[]{:S(2)}) %collective-permute-start.2) | collective-permute-done | bytes 65568 | tf_op jit(solution)/shard_map/ppermute | solution.py:64
  25.0 10.2 %shard_map.102 = bf16[2,64,1024]{2,1,0:T(8,128)(2,1)} custom-call(s32[1]{0:T(128)S(6)} %sub.105.side_ref, bf16[64,4096]{1,0:T(8,128)(2,1)} %copy-done.4, bf16[4096,2048]{1,0:T(8,128)(2,1)} %gate_ref.3, bf16[4096,2048]{1,0:T(8,128)(2,1)} %up_ref.3), custom_call_target="tpu_custom_call" | custom-call | flops 1073741824 | bytes 17301504 | tf_op jit(solution)/shard_map/pallas_call | solution.py:188
  35.7 1.5 %shard_map.104 = (bf16[64,1024]{1,0:T(8,128)(2,1)S(1)}, bf16[64,1024]{1,0:T(8,128)(2,1)S(1)}, bf16[64,1024]{1,0:T(8,128)(2,1)S(1)}, bf16[64,1024]{1,0:T(8,128)(2...) custom-call(s32[8]{0:T(128)S(1)} %multiply_add_fusion.2.refs_0_, ...), custom_call_target="tpu_custom_call" | custom-call | flops 134217728 | bytes 3145728 | tf_op jit(solution)/shard_map/pallas_call | solution.py:152
  39.8 3.5 %collective-permute-start.13 = (bf16[64,1024]{1,0:T(8,128)(2,1)S(1)}, bf16[64,1024]{1,0:T(8,128)(2,1)S(1)}, u32[]{:S(2)}, u32[]{:S(2)}) collective-permute-start(bf16[64,1024]{1,0:T(8,128)(2,1)S(1)} %get-tuple-element.38), channel_id=1, source_target_pairs={{0,8},{2,10},{4,12},{6,14},{8,0},{10,2},{12,4},{14,6},{1,9},{3,11}... | collective-permute-start | bytes 393224 | tf_op jit(solution)/shard_map/ppermute | solution.py:77
  43.3 3.0 %collective-permute-start.15 = (bf16[64,1024]{1,0:T(8,128)(2,1)S(1)}, bf16[64,1024]{1,0:T(8,128)(2,1)S(1)}, u32[]{:S(2)}, u32[]{:S(2)}) collective-permute-start(bf16[64,1024]{1,0:T(8,128)(2,1)S(1)} %get-tuple-element.40), channel_id=1, source_target_pairs={{0,12},{2,14},{4,0},{6,2},{8,4},{10,6},{12,8},{14,10},{1,13},{3,15... | collective-permute-start | bytes 393224 | tf_op jit(solution)/shard_map/ppermute | solution.py:77
  46.3 2.3 %collective-permute-start.16 = (bf16[64,1024]{1,0:T(8,128)(2,1)S(1)}, bf16[64,1024]{1,0:T(8,128)(2,1)S(1)}, u32[]{:S(2)}, u32[]{:S(2)}) collective-permute-start(bf16[64,1024]{1,0:T(8,128)(2,1)S(1)} %get-tuple-element.41), channel_id=1, source_target_pairs={{0,14},{2,12},{4,2},{6,0},{8,6},{10,4},{12,10},{14,8},{1,15},{3,13... | collective-permute-start | bytes 393224 | tf_op jit(solution)/shard_map/ppermute | solution.py:77
  48.6 10.4 %shard_map.101.refs_0_ = f32[2,64,1024]{2,1,0:T(8,128)} custom-call(s32[1]{0:T(128)} %bitcast.side_ref.core_ref, bf16[64,4096]{1,0:T(8,128)(2,1)} %copy-done.4, bf16[4096,2048]{1,0:T(8,128)(2,1)} %gate_ref.3, bf16[4096,2048]{1,0:T(8,128)(2,1)} %up_ref.3), custom_call_target="tpu_custom_call" | custom-call | flops 1073741824 | bytes 17301504 | tf_op jit(solution)/shard_map/pallas_call | solution.py:188
  60.9 2.1 %shard_map.105 = (bf16[64,1024]{1,0:T(8,128)(2,1)S(1)}, bf16[32,1024]{1,0:T(8,128)(2,1)S(1)}, bf16[32,1024]{1,0:T(8,128)(2,1)S(1)}, bf16[32,1024]{1,0:T(8,128)(2...) custom-call(f32[2,64,1024]{2,1,0:T(8,128)S(1)} %copy-done.5, ...), custom_call_target="tpu_custom_call" | custom-call | flops 167772160 | bytes 2359296 | tf_op jit(solution)/shard_map/pallas_call | solution.py:224
  63.6 6.1 %collective-permute-start.19 = (bf16[32,1024]{1,0:T(8,128)(2,1)S(1)}, bf16[32,1024]{1,0:T(8,128)(2,1)S(1)}, u32[]{:S(2)}, u32[]{:S(2)}) collective-permute-start(bf16[32,1024]{1,0:T(8,128)(2,1)S(1)} %get-tuple-element.45), channel_id=1, source_target_pairs={{0,4},{2,6},{4,8},{6,10},{8,12},{10,14},{12,0},{14,2},{1,5},{3,7},... | collective-permute-start | bytes 196616 | tf_op jit(solution)/shard_map/ppermute | solution.py:77
  70.6 2.9 %collective-permute-start.22 = (bf16[32,1024]{1,0:T(8,128)(2,1)S(1)}, bf16[32,1024]{1,0:T(8,128)(2,1)S(1)}, u32[]{:S(2)}, u32[]{:S(2)}) collective-permute-start(bf16[32,1024]{1,0:T(8,128)(2,1)S(1)} %get-tuple-element.48), channel_id=1, source_target_pairs={{0,10},{2,8},{4,14},{6,12},{8,2},{10,0},{12,6},{14,4},{1,11},{3,9}... | collective-permute-start | bytes 196616 | tf_op jit(solution)/shard_map/ppermute | solution.py:77
  73.6 3.8 %collective-permute-start.23 = (bf16[32,1024]{1,0:T(8,128)(2,1)S(1)}, bf16[32,1024]{1,0:T(8,128)(2,1)S(1)}, u32[]{:S(2)}, u32[]{:S(2)}) collective-permute-start(bf16[32,1024]{1,0:T(8,128)(2,1)S(1)} %get-tuple-element.49), channel_id=1, source_target_pairs={{0,12},{2,14},{4,0},{6,2},{8,4},{10,6},{12,8},{14,10},{1,13},{3,15... | collective-permute-start | bytes 196616 | tf_op jit(solution)/shard_map/ppermute | solution.py:77
  78.4 1.7 %collective-permute-done.21.refs_6_ = bf16[32,1024]{1,0:T(8,128)(2,1)S(1)} collective-permute-done((bf16[32,1024]{1,0:T(8,128)(2,1)S(1)}, bf16[32,1024]{1,0:T(8,128)(2,1)S(1)}, u32[]{:S(2)}, u32[]{:S(2)}) %collective-permute-start.21) | collective-permute-done | bytes 65568 | tf_op jit(solution)/shard_map/ppermute | solution.py:77
  84.2 10.2 %shard_map.106.base_ref = f32[64,4096]{1,0:T(8,128)} custom-call(s32[1]{0:T(128)} %bitcast.side_ref.core_ref, bf16[64,1024]{1,0:T(8,128)(2,1)} %copy-done.8, bf16[64,1024]{1,0:T(8,128)(2,1)} %copy-done.10, bf16[2048,4096]{1,0:T(8,128)(2,1)} %far_weight.1, bf16[2048,4096]{1,0:T(8,128)(2,1)} %far_weight.1), custom_call_target="tpu_custom_call" | custom-call | flops 1073741824 | bytes 17825792 | tf_op jit(solution)/shard_map/pallas_call | solution.py:246
  95.6 1.5 %shard_map.108 = (bf16[8,4096]{1,0:T(8,128)(2,1)S(1)}, bf16[8,4096]{1,0:T(8,128)(2,1)S(1)}, bf16[8,4096]{1,0:T(8,128)(2,1)S(1)}, bf16[8,4096]{1,0:T(8,128)(2,1)S...) custom-call(f32[64,4096]{1,0:T(8,128)S(1)} %copy-done.3, ...), custom_call_target="tpu_custom_call" | custom-call | flops 33554432 | bytes 2097152 | tf_op jit(solution)/shard_map/pallas_call | solution.py:308
  97.1 1.6 %collective-permute-start.26 = (bf16[8,4096]{1,0:T(8,128)(2,1)S(1)}, bf16[8,4096]{1,0:T(8,128)(2,1)S(1)}, u32[]{:S(2)}, u32[]{:S(2)}) collective-permute-start(bf16[8,4096]{1,0:T(8,128)(2,1)S(1)} %get-tuple-element.52), channel_id=1, source_target_pairs={{0,2},{2,0},{4,6},{6,4},{8,10},{10,8},{12,14},{14,12},{1,3},{3,1},... | collective-permute-start | bytes 196616 | tf_op jit(solution)/shard_map/ppermute | solution.py:77
  100.2 2.8 %collective-permute-start.29 = (bf16[8,4096]{1,0:T(8,128)(2,1)S(1)}, bf16[8,4096]{1,0:T(8,128)(2,1)S(1)}, u32[]{:S(2)}, u32[]{:S(2)}) collective-permute-start(bf16[8,4096]{1,0:T(8,128)(2,1)S(1)} %get-tuple-element.55), channel_id=1, source_target_pairs={{0,8},{2,10},{4,12},{6,14},{8,0},{10,2},{12,4},{14,6},{1,9},{3,11}... | collective-permute-start | bytes 196616 | tf_op jit(solution)/shard_map/ppermute | solution.py:77
  104.0 3.8 %collective-permute-start.31 = (bf16[8,4096]{1,0:T(8,128)(2,1)S(1)}, bf16[8,4096]{1,0:T(8,128)(2,1)S(1)}, u32[]{:S(2)}, u32[]{:S(2)}) collective-permute-start(bf16[8,4096]{1,0:T(8,128)(2,1)S(1)} %get-tuple-element.57), channel_id=1, source_target_pairs={{0,12},{2,14},{4,0},{6,2},{8,4},{10,6},{12,8},{14,10},{1,13},{3,15... | collective-permute-start | bytes 196616 | tf_op jit(solution)/shard_map/ppermute | solution.py:77
  108.3 1.7 %collective-permute-done.29 = bf16[8,4096]{1,0:T(8,128)(2,1)S(1)} collective-permute-done((bf16[8,4096]{1,0:T(8,128)(2,1)S(1)}, bf16[8,4096]{1,0:T(8,128)(2,1)S(1)}, u32[]{:S(2)}, u32[]{:S(2)}) %collective-permute-start.29) | collective-permute-done | bytes 65568 | tf_op jit(solution)/shard_map/ppermute | solution.py:77
  110.0 2.4 %collective-permute-done.30 = bf16[8,4096]{1,0:T(8,128)(2,1)S(1)} collective-permute-done((bf16[8,4096]{1,0:T(8,128)(2,1)S(1)}, bf16[8,4096]{1,0:T(8,128)(2,1)S(1)}, u32[]{:S(2)}, u32[]{:S(2)}) %collective-permute-start.30) | collective-permute-done | bytes 65568 | tf_op jit(solution)/shard_map/ppermute | solution.py:77
  (114 shorter events, 29.6 us)
Async XLA Ops:
  0.0 13.7 %collective-permute-start.1 = (bf16[8,4096]{1,0:T(8,128)(2,1)}, bf16[8,4096]{1,0:T(8,128)(2,1)S(1)}, u32[]{:S(2)}, u32[]{:S(2)}) collective-permute-start(bf16[8,4096]{1,0:T(8,128)(2,1)} %refs_2_.1), channel_id=1, source_target_pairs={{0,4},{2,6},{4,8},{6,10},{8,12},{10,14},{12,0},{14,2},{1,5},{3,7},... | collective-permute-start | bytes 196616 | tf_op jit(solution)/shard_map/ppermute | solution.py:61
  3.0 11.3 %collective-permute-start.3 = (bf16[8,4096]{1,0:T(8,128)(2,1)}, bf16[8,4096]{1,0:T(8,128)(2,1)S(1)}, u32[]{:S(2)}, u32[]{:S(2)}) collective-permute-start(bf16[8,4096]{1,0:T(8,128)(2,1)} %refs_2_.1), channel_id=1, source_target_pairs={{0,8},{2,10},{4,12},{6,14},{8,0},{10,2},{12,4},{14,6},{1,9},{3,11}... | collective-permute-start | bytes 196616 | tf_op jit(solution)/shard_map/ppermute | solution.py:61
  5.6 10.2 %collective-permute-start.5 = (bf16[8,4096]{1,0:T(8,128)(2,1)}, bf16[8,4096]{1,0:T(8,128)(2,1)S(1)}, u32[]{:S(2)}, u32[]{:S(2)}) collective-permute-start(bf16[8,4096]{1,0:T(8,128)(2,1)} %refs_2_.1), channel_id=1, source_target_pairs={{0,12},{2,14},{4,0},{6,2},{8,4},{10,6},{12,8},{14,10},{1,13},{3,15... | collective-permute-start | bytes 196616 | tf_op jit(solution)/shard_map/ppermute | solution.py:61
  7.0 9.4 %collective-permute-start = (bf16[8,4096]{1,0:T(8,128)(2,1)}, bf16[8,4096]{1,0:T(8,128)(2,1)S(1)}, u32[]{:S(2)}, u32[]{:S(2)}) collective-permute-start(bf16[8,4096]{1,0:T(8,128)(2,1)} %refs_2_.1), channel_id=1, source_target_pairs={{0,2},{2,0},{4,6},{6,4},{8,10},{10,8},{12,14},{14,12},{1,3},{3,1},... | collective-permute-start | bytes 196616 | tf_op jit(solution)/shard_map/ppermute | solution.py:64
  11.1 24.7 %collective-permute-start.9 = (bf16[64,8192]{1,0:T(8,128)(2,1)S(1)}, bf16[64,8192]{1,0:T(8,128)(2,1)S(1)}, u32[]{:S(2)}, u32[]{:S(2)}) collective-permute-start(bf16[64,8192]{1,0:T(8,128)(2,1)S(1)} %shard_map.103), channel_id=1, source_target_pairs={{0,1},{1,0},{2,3},{3,2},{4,5},{5,4},{6,7},{7,6},{8,9},{9,8},{10,11... | collective-permute-start | bytes 3145736 | tf_op jit(solution)/shard_map/ppermute | solution.py:347
  25.0 10.8 %collective-permute-start.8 = (f32[64,128]{1,0:T(8,128)S(1)}, f32[64,128]{1,0:T(8,128)S(1)}, u32[]{:S(2)}, u32[]{:S(2)}) collective-permute-start(f32[64,128]{1,0:T(8,128)S(1)} %get-tuple-element.33.refs_1_), channel_id=1, source_target_pairs={{0,1},{1,0},{2,3},{3,2},{4,5},{5,4},{6,7},{7,6},{8,9},{9,8},{10,11... | collective-permute-start | bytes 98312 | tf_op jit(solution)/shard_map/ppermute | solution.py:347
  35.2 8.1 %collective-permute-start.7 = (bf16[2,64,1024]{2,1,0:T(8,128)(2,1)}, bf16[2,64,1024]{2,1,0:T(8,128)(2,1)S(1)}, u32[]{:S(2)}, u32[]{:S(2)}) collective-permute-start(bf16[2,64,1024]{2,1,0:T(8,128)(2,1)} %shard_map.102), channel_id=1, source_target_pairs={{0,1},{1,0},{2,3},{3,2},{4,5},{5,4},{6,7},{7,6},{8,9},{9,8},{10,11... | collective-permute-start | bytes 786440 | tf_op jit(solution)/shard_map/ppermute | solution.py:347
  37.8 8.5 %collective-permute-start.11 = (bf16[64,1024]{1,0:T(8,128)(2,1)S(1)}, bf16[64,1024]{1,0:T(8,128)(2,1)S(1)}, u32[]{:S(2)}, u32[]{:S(2)}) collective-permute-start(bf16[64,1024]{1,0:T(8,128)(2,1)S(1)} %get-tuple-element.36), channel_id=1, source_target_pairs={{0,4},{2,6},{4,8},{6,10},{8,12},{10,14},{12,0},{14,2},{1,5},{3,7},... | collective-permute-start | bytes 393224 | tf_op jit(solution)/shard_map/ppermute | solution.py:77
  38.6 20.4 %collective-permute-start.12 = (bf16[64,1024]{1,0:T(8,128)(2,1)S(1)}, bf16[64,1024]{1,0:T(8,128)(2,1)S(1)}, u32[]{:S(2)}, u32[]{:S(2)}) collective-permute-start(bf16[64,1024]{1,0:T(8,128)(2,1)S(1)} %get-tuple-element.37), channel_id=1, source_target_pairs={{0,6},{2,4},{4,10},{6,8},{8,14},{10,12},{12,2},{14,0},{1,7},{3,5},... | collective-permute-start | bytes 393224 | tf_op jit(solution)/shard_map/ppermute | solution.py:77
  39.8 19.1 %collective-permute-start.13 = (bf16[64,1024]{1,0:T(8,128)(2,1)S(1)}, bf16[64,1024]{1,0:T(8,128)(2,1)S(1)}, u32[]{:S(2)}, u32[]{:S(2)}) collective-permute-start(bf16[64,1024]{1,0:T(8,128)(2,1)S(1)} %get-tuple-element.38), channel_id=1, source_target_pairs={{0,8},{2,10},{4,12},{6,14},{8,0},{10,2},{12,4},{14,6},{1,9},{3,11}... | collective-permute-start | bytes 393224 | tf_op jit(solution)/shard_map/ppermute | solution.py:77
  43.3 16.5 %collective-permute-start.14 = (bf16[64,1024]{1,0:T(8,128)(2,1)S(1)}, bf16[64,1024]{1,0:T(8,128)(2,1)S(1)}, u32[]{:S(2)}, u32[]{:S(2)}) collective-permute-start(bf16[64,1024]{1,0:T(8,128)(2,1)S(1)} %get-tuple-element.39), channel_id=1, source_target_pairs={{0,10},{2,8},{4,14},{6,12},{8,2},{10,0},{12,6},{14,4},{1,11},{3,9}... | collective-permute-start | bytes 393224 | tf_op jit(solution)/shard_map/ppermute | solution.py:77
  43.3 16.5 %collective-permute-start.15 = (bf16[64,1024]{1,0:T(8,128)(2,1)S(1)}, bf16[64,1024]{1,0:T(8,128)(2,1)S(1)}, u32[]{:S(2)}, u32[]{:S(2)}) collective-permute-start(bf16[64,1024]{1,0:T(8,128)(2,1)S(1)} %get-tuple-element.40), channel_id=1, source_target_pairs={{0,12},{2,14},{4,0},{6,2},{8,4},{10,6},{12,8},{14,10},{1,13},{3,15... | collective-permute-start | bytes 393224 | tf_op jit(solution)/shard_map/ppermute | solution.py:77
  46.3 13.5 %collective-permute-start.16 = (bf16[64,1024]{1,0:T(8,128)(2,1)S(1)}, bf16[64,1024]{1,0:T(8,128)(2,1)S(1)}, u32[]{:S(2)}, u32[]{:S(2)}) collective-permute-start(bf16[64,1024]{1,0:T(8,128)(2,1)S(1)} %get-tuple-element.41), channel_id=1, source_target_pairs={{0,14},{2,12},{4,2},{6,0},{8,6},{10,4},{12,10},{14,8},{1,15},{3,13... | collective-permute-start | bytes 393224 | tf_op jit(solution)/shard_map/ppermute | solution.py:77
  63.0 10.5 %collective-permute-start.18 = (bf16[32,1024]{1,0:T(8,128)(2,1)S(1)}, bf16[32,1024]{1,0:T(8,128)(2,1)S(1)}, u32[]{:S(2)}, u32[]{:S(2)}) collective-permute-start(bf16[32,1024]{1,0:T(8,128)(2,1)S(1)} %get-tuple-element.44), channel_id=1, source_target_pairs={{0,2},{2,0},{4,6},{6,4},{8,10},{10,8},{12,14},{14,12},{1,3},{3,1},... | collective-permute-start | bytes 196616 | tf_op jit(solution)/shard_map/ppermute | solution.py:77
  63.6 13.7 %collective-permute-start.19 = (bf16[32,1024]{1,0:T(8,128)(2,1)S(1)}, bf16[32,1024]{1,0:T(8,128)(2,1)S(1)}, u32[]{:S(2)}, u32[]{:S(2)}) collective-permute-start(bf16[32,1024]{1,0:T(8,128)(2,1)S(1)} %get-tuple-element.45), channel_id=1, source_target_pairs={{0,4},{2,6},{4,8},{6,10},{8,12},{10,14},{12,0},{14,2},{1,5},{3,7},... | collective-permute-start | bytes 196616 | tf_op jit(solution)/shard_map/ppermute | solution.py:77
  69.7 8.7 %collective-permute-start.20 = (bf16[32,1024]{1,0:T(8,128)(2,1)S(1)}, bf16[32,1024]{1,0:T(8,128)(2,1)S(1)}, u32[]{:S(2)}, u32[]{:S(2)}) collective-permute-start(bf16[32,1024]{1,0:T(8,128)(2,1)S(1)} %get-tuple-element.46), channel_id=1, source_target_pairs={{0,6},{2,4},{4,10},{6,8},{8,14},{10,12},{12,2},{14,0},{1,7},{3,5},... | collective-permute-start | bytes 196616 | tf_op jit(solution)/shard_map/ppermute | solution.py:77
  70.6 9.5 %collective-permute-start.21 = (bf16[32,1024]{1,0:T(8,128)(2,1)S(1)}, bf16[32,1024]{1,0:T(8,128)(2,1)S(1)}, u32[]{:S(2)}, u32[]{:S(2)}) collective-permute-start(bf16[32,1024]{1,0:T(8,128)(2,1)S(1)} %get-tuple-element.47), channel_id=1, source_target_pairs={{0,8},{2,10},{4,12},{6,14},{8,0},{10,2},{12,4},{14,6},{1,9},{3,11}... | collective-permute-start | bytes 196616 | tf_op jit(solution)/shard_map/ppermute | solution.py:77
  70.6 10.8 %collective-permute-start.22 = (bf16[32,1024]{1,0:T(8,128)(2,1)S(1)}, bf16[32,1024]{1,0:T(8,128)(2,1)S(1)}, u32[]{:S(2)}, u32[]{:S(2)}) collective-permute-start(bf16[32,1024]{1,0:T(8,128)(2,1)S(1)} %get-tuple-element.48), channel_id=1, source_target_pairs={{0,10},{2,8},{4,14},{6,12},{8,2},{10,0},{12,6},{14,4},{1,11},{3,9}... | collective-permute-start | bytes 196616 | tf_op jit(solution)/shard_map/ppermute | solution.py:77
  83.4 10.9 %collective-permute-start.25 = (f32[32,64]{1,0:T(8,128)S(1)}, f32[32,64]{1,0:T(8,128)S(1)}, u32[]{:S(2)}, u32[]{:S(2)}) collective-permute-start(f32[32,64]{1,0:T(8,128)S(1)} %shard_map.107.own_ref), channel_id=1, source_target_pairs={{0,1},{1,0},{2,3},{3,2},{4,5},{5,4},{6,7},{7,6},{8,9},{9,8},{10,11... | collective-permute-start | bytes 24584 | tf_op jit(solution)/shard_map/ppermute | solution.py:347
  98.7 9.1 %collective-permute-start.27 = (bf16[8,4096]{1,0:T(8,128)(2,1)S(1)}, bf16[8,4096]{1,0:T(8,128)(2,1)S(1)}, u32[]{:S(2)}, u32[]{:S(2)}) collective-permute-start(bf16[8,4096]{1,0:T(8,128)(2,1)S(1)} %get-tuple-element.53), channel_id=1, source_target_pairs={{0,4},{2,6},{4,8},{6,10},{8,12},{10,14},{12,0},{14,2},{1,5},{3,7},... | collective-permute-start | bytes 196616 | tf_op jit(solution)/shard_map/ppermute | solution.py:77
  100.1 8.2 %collective-permute-start.28 = (bf16[8,4096]{1,0:T(8,128)(2,1)S(1)}, bf16[8,4096]{1,0:T(8,128)(2,1)S(1)}, u32[]{:S(2)}, u32[]{:S(2)}) collective-permute-start(bf16[8,4096]{1,0:T(8,128)(2,1)S(1)} %get-tuple-element.54), channel_id=1, source_target_pairs={{0,6},{2,4},{4,10},{6,8},{8,14},{10,12},{12,2},{14,0},{1,7},{3,5},... | collective-permute-start | bytes 196616 | tf_op jit(solution)/shard_map/ppermute | solution.py:77
  100.2 9.8 %collective-permute-start.29 = (bf16[8,4096]{1,0:T(8,128)(2,1)S(1)}, bf16[8,4096]{1,0:T(8,128)(2,1)S(1)}, u32[]{:S(2)}, u32[]{:S(2)}) collective-permute-start(bf16[8,4096]{1,0:T(8,128)(2,1)S(1)} %get-tuple-element.55), channel_id=1, source_target_pairs={{0,8},{2,10},{4,12},{6,14},{8,0},{10,2},{12,4},{14,6},{1,9},{3,11}... | collective-permute-start | bytes 196616 | tf_op jit(solution)/shard_map/ppermute | solution.py:77
  103.0 9.4 %collective-permute-start.30 = (bf16[8,4096]{1,0:T(8,128)(2,1)S(1)}, bf16[8,4096]{1,0:T(8,128)(2,1)S(1)}, u32[]{:S(2)}, u32[]{:S(2)}) collective-permute-start(bf16[8,4096]{1,0:T(8,128)(2,1)S(1)} %get-tuple-element.56), channel_id=1, source_target_pairs={{0,10},{2,8},{4,14},{6,12},{8,2},{10,0},{12,6},{14,4},{1,11},{3,9}... | collective-permute-start | bytes 196616 | tf_op jit(solution)/shard_map/ppermute | solution.py:77
  104.0 8.4 %collective-permute-start.31 = (bf16[8,4096]{1,0:T(8,128)(2,1)S(1)}, bf16[8,4096]{1,0:T(8,128)(2,1)S(1)}, u32[]{:S(2)}, u32[]{:S(2)}) collective-permute-start(bf16[8,4096]{1,0:T(8,128)(2,1)S(1)} %get-tuple-element.57), channel_id=1, source_target_pairs={{0,12},{2,14},{4,0},{6,2},{8,4},{10,6},{12,8},{14,10},{1,13},{3,15... | collective-permute-start | bytes 196616 | tf_op jit(solution)/shard_map/ppermute | solution.py:77
  (20 other events, 136.0 us)

commit v3 on v2

--- a/solution.py
+++ b/solution.py
@@ -7,6 +7,7 @@
 
 MOST = 8
 DIRECT = 8
+USUAL = 16
 BF = jnp.bfloat16
 F32 = jnp.float32
 I32 = jnp.int32
@@ -164,38 +165,45 @@
     )(at, own, got, pick, cols, far, *[near] * count)
 
 
-def base_kernel(side_ref, x_ref, gate_ref, up_ref, out_ref, gate_sum, up_sum):
-    step = pl.program_id(0)
-
-    @pl.when(step == 0)
-    def _():
-        gate_sum[...] = jnp.zeros_like(gate_sum)
-        up_sum[...] = jnp.zeros_like(up_sum)
-
-    gate_sum[...] += dot(x_ref[...], gate_ref[...])
-    up_sum[...] += dot(x_ref[...], up_ref[...])
-
-    @pl.when(step == pl.num_programs(0) - 1)
-    def _():
-        out_ref[0] = gate_sum[...].astype(out_ref.dtype)
-        out_ref[1] = up_sum[...].astype(out_ref.dtype)
+def base_kernel(side_ref, x_ref, gate_ref, up_ref, out_ref, held, sums, sems):
+    half = held.shape[2]
+    chunks = sems.shape[1]
+    depth = held.shape[1] // chunks
+    columns = pl.ds(pl.multiple_of(side_ref[0] * half, half), half)
+    copies = []
+    for c in range(chunks):
+        here = pl.ds(c * depth, depth)
+        for kind, weight in enumerate((gate_ref, up_ref)):
+            copy = pltpu.make_async_copy(
+                weight.at[here, columns], held.at[kind, here], sems.at[kind, c]
+            )
+            copy.start()
+            copies.append((kind, here, copy))
+    for kind, here, copy in copies:
+        copy.wait()
+        part = dot(x_ref[:, here], held[kind, here])
+        sums[kind] = part if here.start == 0 else sums[kind] + part
+    out_ref[...] = sums[...].astype(out_ref.dtype)
 
 
 def base_half(side, x, gate_weight, up_weight, half, kind):
     rows, width = x.shape
-    block = min(512, width)
-    weight = pl.BlockSpec((block, half), lambda n, side: (n, side[0]))
+    chunks = max(width // 512, 1)
     return pl.pallas_call(
         base_kernel,
         out_shape=jax.ShapeDtypeStruct((2, rows, half), kind),
         grid_spec=pltpu.PrefetchScalarGridSpec(
             num_scalar_prefetch=1,
-            grid=(width // block,),
-            in_specs=[pl.BlockSpec((rows, block), lambda n, side: (0, n)), weight, weight],
+            grid=(1,),
+            in_specs=[fixed(x), pl.BlockSpec(memory_space=pl.ANY), pl.BlockSpec(memory_space=pl.ANY)],
             out_specs=pl.BlockSpec((2, rows, half), lambda n, side: (0, 0, 0)),
-            scratch_shapes=[pltpu.VMEM((rows, half), F32), pltpu.VMEM((rows, half), F32)],
-        ),
-        compiler_params=params(56),
+            scratch_shapes=[
+                pltpu.VMEM((2, width, half), BF),
+                pltpu.VMEM((2, rows, half), F32),
+                pltpu.SemaphoreType.DMA((2, chunks)),
+            ],
+        ),
+        compiler_params=params(48),
         cost_estimate=cost(4 * rows * width * half, 4 * width * half + 2 * rows * width),
     )(side, x, gate_weight, up_weight)
 
@@ -235,31 +243,49 @@
     )(own, got, place, send, *parts)
 
 
-def down_kernel(core_ref, near_ref, far_ref, near_weight, far_weight, out_ref):
-    out_ref[...] = dot(near_ref[...], near_weight[...]) + dot(far_ref[...], far_weight[...])
+def down_kernel(core_ref, near_ref, far_ref, weight_ref, out_ref, held, sems):
+    chunks = sems.shape[1]
+    half, width = held.shape[1:]
+    block = width // chunks
+    copies = []
+    for c in range(chunks):
+        here = pl.ds(c * block, block)
+        for side, at in enumerate((core_ref[0], 1 - core_ref[0])):
+            lines = pl.ds(pl.multiple_of(at * half, half), half)
+            copy = pltpu.make_async_copy(
+                weight_ref.at[lines, here], held.at[side, :, here], sems.at[side, c]
+            )
+            copy.start()
+            copies.append(copy)
+    for c in range(chunks):
+        here = pl.ds(c * block, block)
+        copies[2 * c].wait()
+        copies[2 * c + 1].wait()
+        out_ref[:, here] = dot(near_ref[...], held[0, :, here]) + dot(
+            far_ref[...], held[1, :, here]
+        )
 
 
 def down_base(core, near, far, weight):
     rows, half = near.shape
     width = weight.shape[1]
-    block = min(512, width)
+    chunks = max(width // 512, 1)
     return pl.pallas_call(
         down_kernel,
         out_shape=jax.ShapeDtypeStruct((rows, width), F32),
         grid_spec=pltpu.PrefetchScalarGridSpec(
             num_scalar_prefetch=1,
-            grid=(width // block,),
-            in_specs=[
-                fixed(near),
-                fixed(far),
-                pl.BlockSpec((half, block), lambda n, core: (core[0], n)),
-                pl.BlockSpec((half, block), lambda n, core: (1 - core[0], n)),
+            grid=(1,),
+            in_specs=[fixed(near), fixed(far), pl.BlockSpec(memory_space=pl.ANY)],
+            out_specs=pl.BlockSpec((rows, width), lambda n, core: (0, 0)),
+            scratch_shapes=[
+                pltpu.VMEM((2, half, width), BF),
+                pltpu.SemaphoreType.DMA((2, chunks)),
             ],
-            out_specs=pl.BlockSpec((rows, block), lambda n, core: (0, n)),
-        ),
-        compiler_params=params(56),
+        ),
+        compiler_params=params(48),
         cost_estimate=cost(4 * rows * half * width, 4 * half * width + 4 * rows * width),
-    )(core, near, far, weight, weight)
+    )(core, near, far, weight)
 
 
 def low_out_kernel(count, at_ref, mask_ref, *refs):
@@ -314,6 +340,10 @@
         compiler_params=params(24),
         cost_estimate=cost(2 * rows * depth * width, width * (6 * rows + 2 * depth)),
     )(base, own, got, pick, expand)
+
+
+def tied(first, *others):
+    return lax.optimization_barrier((first, *others))
 
 
 def per_device(
@@ -332,6 +362,7 @@
     shards, order = ways.shards, ways.order
     me = lax.axis_index("ff").astype(I32)
     core = lax.axis_index("var").astype(I32)
+    groups = lax.axis_size("groups")
     own_rows, width = tokens.shape
     rows = own_rows * shards
     slots = shrink_gu.shape[0]
@@ -339,7 +370,7 @@
     rank = shrink_down.shape[1]
     half_rank = expand_gu.shape[2]
     half = gate_weight.shape[1] // 2
-    cap = min(slots * MOST, rows)
+    most = min(slots * MOST, rows)
     here = core.reshape(1)
     there = 1 - here
     at_here = 2 * order + core
@@ -347,6 +378,7 @@
     swap = lambda a: lax.ppermute(a, "var", [(0, 1), (1, 0)])
 
     token_parts = ways.gather(tokens)
+    at_there, *token_parts[:: ways.fast] = tied(at_there, *token_parts[:: ways.fast])
 
     near = expand_gu.reshape(slots * 2 * half_rank, -1)
     far = swap(pick_columns(at_there, near, half))
@@ -358,31 +390,24 @@
     index = jnp.arange(rows, dtype=I32)
     earlier = (owner[:, None] == owner[None, :]) & (index[None, :] < index[:, None])
     place = jnp.sum(earlier.astype(I32), axis=1)
+    highest = jnp.max(place).reshape(1)
+    for turn in range(1, groups):
+        pairs = [(g, (g + turn) % groups) for g in range(groups)]
+        highest = jnp.maximum(highest, lax.ppermute(highest, "groups", pairs))
     where_row = order[:, None] == jnp.arange(shards, dtype=I32)[None, :]
-    turn = lambda a: jnp.sum(
+    turned = lambda a: jnp.sum(
         jnp.where(where_row[:, :, None], a.reshape(1, shards, own_rows), 0), axis=1
     ).reshape(rows)
-    slot_row, place = turn(slot_row), turn(place)
+    slot_row, place = turned(slot_row), turned(place)
     owner = slot_row // slots
     step = jnp.sum(
         jnp.where(owner[:, None] == order[None, :], jnp.arange(shards, dtype=I32)[None, :], 0),
         axis=1,
     )
-    cells = jnp.arange(shards * cap, dtype=I32)
-    send_rows = (cells[:, None] == (step * cap + place)[None, :]).astype(BF)
+    local = slot_row - me * slots
     kinds = jnp.arange(2, dtype=I32)
-    kind_cell = (step * 2 + kinds[:, None]) * cap + place
-    kind_cells = jnp.arange(2 * shards * cap, dtype=I32)
-    place_rows = (kind_cell[:, :, None] == kind_cells).astype(BF).reshape(2 * rows, -1)
-    spots = jnp.arange(cap, dtype=I32)
-    picked = (spots[:, None] == place[None, :]) & (owner[None, :] == me)
-    pick = picked.astype(BF)
-    local = slot_row - me * slots
     in_cols = jnp.arange(slots * 2 * rank, dtype=I32)
     mask_in = (local[:, None] == (in_cols // (2 * rank))[None, :]).astype(F32)
-    spot_slot = jnp.sum(jnp.where(picked, local[None, :] + 1, 0), axis=1) - 1
-    out_cols = jnp.arange(slots * rank, dtype=I32)
-    mask_out = (spot_slot[:, None] == (out_cols // rank)[None, :]).astype(F32)
     rank_at = in_cols % rank
     kind_at = in_cols // rank % 2
     row_at = in_cols // (2 * rank) * (2 * half_rank) + kind_at * half_rank + rank_at % half_rank
@@ -395,20 +420,41 @@
         & ((rank_at // half_rank)[None, :] == side[:, None])[None, :, :, None]
     ).astype(BF)
 
-    x, low_own = low_in_pairs(token_parts, shrink_gu.reshape(slots * 2 * rank, width), mask_in)
-    low_got = swap(low_own)
-    base_got = swap(base_half(there, x, gate_weight, up_weight, half, BF))
-    delta = ways.deliver(expand_rows(at_here, low_own, low_got, pick, cols, near, far, half))
-    base_own = base_half(here, x, gate_weight, up_weight, half, F32)
-    hidden, *sent = hidden_half(base_own, base_got, delta, place_rows, send_rows)
-    hidden_far = swap(hidden)
-    hidden_rows = ways.deliver(sent)
-    base = down_base(here, hidden, hidden_far, down_weight)
-    out_own = low_out_pairs(at_here, hidden_rows, shrink_down.reshape(slots * rank, -1), mask_out)
-    out_got = swap(out_own)
-    expand = expand_down.reshape(slots * rank, width)
-    parts = ways.deliver(add_delta(base, out_own, out_got, pick, expand, shards))
-    return sum(part.astype(F32) for part in parts).astype(BF)
+    def finish(cap):
+        cells = jnp.arange(shards * cap, dtype=I32)
+        send_rows = (cells[:, None] == (step * cap + place)[None, :]).astype(BF)
+        kind_cell = (step * 2 + kinds[:, None]) * cap + place
+        kind_cells = jnp.arange(2 * shards * cap, dtype=I32)
+        place_rows = (kind_cell[:, :, None] == kind_cells).astype(BF).reshape(2 * rows, -1)
+        spots = jnp.arange(cap, dtype=I32)
+        picked = (spots[:, None] == place[None, :]) & (owner[None, :] == me)
+        pick = picked.astype(BF)
+        spot_slot = jnp.sum(jnp.where(picked, local[None, :] + 1, 0), axis=1) - 1
+        out_cols = jnp.arange(slots * rank, dtype=I32)
+        mask_out = (spot_slot[:, None] == (out_cols // rank)[None, :]).astype(F32)
+
+        x, low_own = low_in_pairs(token_parts, shrink_gu.reshape(slots * 2 * rank, width), mask_in)
+        low_got = swap(low_own)
+        made = expand_rows(at_here, low_own, low_got, pick, cols, near, far, half)
+        x, *made = tied(x, *made)
+        base_got = swap(base_half(there, x, gate_weight, up_weight, half, BF))
+        delta = ways.deliver(made)
+        base_own = base_half(here, x, gate_weight, up_weight, half, F32)
+        hidden, *sent = hidden_half(base_own, base_got, delta, place_rows, send_rows)
+        hidden_far = swap(hidden)
+        hidden_rows = ways.deliver(sent)
+        base = down_base(here, hidden, hidden_far, down_weight)
+        base, *hidden_rows = tied(base, *hidden_rows)
+        shrink = shrink_down.reshape(slots * rank, -1)
+        out_own = low_out_pairs(at_here, hidden_rows, shrink, mask_out)
+        out_got = swap(out_own)
+        expand = expand_down.reshape(slots * rank, width)
+        parts = ways.deliver(add_delta(base, out_own, out_got, pick, expand, shards))
+        return sum(part.astype(F32) for part in parts).astype(BF)
+
+    if most <= USUAL:
+        return finish(most)
+    return lax.cond(highest[0] < USUAL, lambda: finish(USUAL), lambda: finish(most))
 
 
 def solution(mesh):

time: 114 us -> 94.7 us (0.83)
  local copies, waits for them, and re-layouts: 7.94 us -> 1.37 us
  Pallas kernels: 38.8 us -> 32.9 us
  starting transfers between devices: 49.5 us -> 44.7 us
  waiting for transfers between devices: 14.4 us -> 10.7 us
  between operations: 0.28 us -> 1.47 us
    pallas_call x2, Pallas kernels: 20.6 us -> 12.5 us  [base_half(): pl.pallas_call(base_kernel, out_shape=jax.ShapeDtypeStruct((2, rows, half...]
    unnamed x22 -> x6, local copies, waits for them, and re-layouts: 7.36 us -> 0.63 us
    ppermute x21, starting transfers between devices: 37.8 us -> 31.7 us  [deliver(): got[back] = lax.ppermute(blocks[b], 'ff', self.back(a, c))]
    ppermute x21, waiting for transfers between devices: 9.63 us -> 5.76 us  [deliver(): got[back] = lax.ppermute(blocks[b], 'ff', self.back(a, c))]
    pallas_call x1, Pallas kernels: 10.2 us -> 6.59 us  [down_base(): pl.pallas_call(down_kernel, out_shape=jax.ShapeDtypeStruct((rows, width),...]
    pallas_call x1, Pallas kernels: 0.96 us -> 4.42 us  [pick_columns(): pl.pallas_call(copy_kernel, out_shape=jax.ShapeDtypeStruct((depth, count...]
    pallas_call x1, Pallas kernels: 1.03 us -> 2.66 us  [low_in_pairs(): pl.pallas_call(lambda *refs: low_in_kernel(count, *refs), out_shape=(jax....]
    ppermute x0 -> x1, starting transfers between devices: none -> 1.49 us  [per_device(): highest = jnp.maximum(highest, lax.ppermute(highest, 'groups', pairs))]
  transfers between devices with their start and end apart: 33 -> 34, of which waited for: 10 -> 11; matrix products, arithmetic and copies ran while one was open for 2% -> 4% of each run, Pallas kernels for 31% -> 18%
where the time goes in v3:
time: 94.7 us; the launch traced here: 94.5 us
  starting transfers between devices  44.7 us (47%)
  Pallas kernels  32.9 us (35%)
  waiting for transfers between devices  10.7 us (11%)
  other arithmetic  2.86 us (3%)
  between operations  1.47 us (2%)
  local copies, waits for them, and re-layouts  1.37 us (1%)
    ppermute x21, starting transfers between devices, deliver(): got[back] = lax.ppermute(blocks[b], 'ff', self.back(a, c))  31.7 us
    pallas_call x2, Pallas kernels, base_half(): pl.pallas_call(base_kernel, out_shape=jax.ShapeDtypeStruct((2, rows, half...  12.5 us
    ppermute x3, starting transfers between devices, gather(): lax.ppermute(block, 'ff', self.back(-a, 0))  6.96 us
    pallas_call x1, Pallas kernels, down_base(): pl.pallas_call(down_kernel, out_shape=jax.ShapeDtypeStruct((rows, width),...  6.59 us
    ppermute x21, waiting for transfers between devices, deliver(): got[back] = lax.ppermute(blocks[b], 'ff', self.back(a, c))  5.76 us
    pallas_call x1, Pallas kernels, pick_columns(): pl.pallas_call(copy_kernel, out_shape=jax.ShapeDtypeStruct((depth, count...  4.42 us
    ppermute x4, starting transfers between devices, gather(): lax.ppermute(got[a * self.fast], 'ff', self.back(0, -c))  4.12 us
    ppermute x4, waiting for transfers between devices, gather(): lax.ppermute(got[a * self.fast], 'ff', self.back(0, -c))  3.45 us
  transfers between devices with their start and end apart: 34, of which 11 were waited for; matrix products, arithmetic and copies ran while one was open for 4% of the time, Pallas kernels for 18%

profile of v3, /device:TPU:0, one launch (start us, length us, event | category | flops | bytes accessed | tf_op | source)
XLA Modules:
  0.0 94.5 jit_solution(7717616365858626437)
XLA Ops:
  0.0 3.0 %collective-permute-start.51 = (bf16[8,4096]{1,0:T(8,128)(2,1)}, bf16[8,4096]{1,0:T(8,128)(2,1)S(1)}, u32[]{:S(2)}, u32[]{:S(2)}) collective-permute-start(bf16[8,4096]{1,0:T(8,128)(2,1)} %param.12), channel_id=1, source_target_pairs={{0,4},{2,6},{4,8},{6,10},{8,12},{10,14},{12,0},{14,2},{1,5},{3,7},... | collective-permute-start | bytes 196616 | tf_op jit(solution)/shard_map/ppermute | solution.py:62
  3.0 2.6 %collective-permute-start.52 = (bf16[8,4096]{1,0:T(8,128)(2,1)}, bf16[8,4096]{1,0:T(8,128)(2,1)S(1)}, u32[]{:S(2)}, u32[]{:S(2)}) collective-permute-start(bf16[8,4096]{1,0:T(8,128)(2,1)} %param.12), channel_id=1, source_target_pairs={{0,8},{2,10},{4,12},{6,14},{8,0},{10,2},{12,4},{14,6},{1,9},{3,11}... | collective-permute-start | bytes 196616 | tf_op jit(solution)/shard_map/ppermute | solution.py:62
  7.0 1.5 %collective-permute-start.54 = (bf16[8,4096]{1,0:T(8,128)(2,1)}, bf16[8,4096]{1,0:T(8,128)(2,1)S(1)}, u32[]{:S(2)}, u32[]{:S(2)}) collective-permute-start(bf16[8,4096]{1,0:T(8,128)(2,1)} %param.12), channel_id=1, source_target_pairs={{0,2},{2,0},{4,6},{6,4},{8,10},{10,8},{12,14},{14,12},{1,3},{3,1},... | collective-permute-start | bytes 196616 | tf_op jit(solution)/shard_map/ppermute | solution.py:65
  10.1 1.5 %collective-permute-start.50 = (s32[1]{0:T(128)}, s32[1]{0:T(128)}, u32[]{:S(2)}, u32[]{:S(2)}) collective-permute-start(s32[1]{0:T(128)} %bitcast.7), channel_id=1, source_target_pairs={{0,16},{16,0},{1,17},{17,1},{2,18},{18,2},{3,19},{19,3},{4,20},{20... | collective-permute-start | bytes 20 | tf_op jit(solution)/shard_map/ppermute | solution.py:396
  12.2 4.4 %shard_map.114 = bf16[64,8192]{1,0:T(8,128)(2,1)S(1)} custom-call(s32[8]{0:T(128)S(1)} %add_subtract_fusion.at_ref, bf16[64,16384]{1,0:T(8,128)(2,1)} %bitcast.20), custom_call_target="tpu_custom_call" | custom-call | bytes 2097152 | tf_op jit(solution)/shard_map/pallas_call | solution.py:88
  17.6 1.5 %collective-permute-start.56 = (bf16[8,4096]{1,0:T(8,128)(2,1)S(1)}, bf16[8,4096]{1,0:T(8,128)(2,1)S(1)}, u32[]{:S(2)}, u32[]{:S(2)}) collective-permute-start(bf16[8,4096]{1,0:T(8,128)(2,1)S(1)} %collective-permute-done.52), channel_id=1, source_target_pairs={{0,2},{2,0},{4,6},{6,4},{8,10},{10,8},{12,14},{14,12},{1,3},{3,1},... | collective-permute-start | bytes 196616 | tf_op jit(solution)/shard_map/ppermute | solution.py:65
  24.6 69.2 %conditional.6 = (bf16[8,4096]{1,0:T(8,128)(2,1)S(1)}) conditional(s32[]{:T(128)} %bitcast.8, (bf16[4,32,4096]{2,1,0:T(8,128)(2,1)}, f32[64,128]{1,0:T(8,128)S(1)}, bf16[8,4096]{1,0:T(8,128)(2,1)}, bf16[8,4096]{1,0:T(8,128)(2,1)S(1)}, bf16[8,4096]{1,0:T(8,128)(2,1)S(1)}, /*index=5*/bf16[8,4096]{1,0:T(8,128)(2,1)S(1)}, bf16[8,4096]{1,0:T(8,128)(2,1)S(1)}, ...), branch_computations={%region_4.8_spmd, %region_8.12_spmd} | conditional | flops 3658144256 | bytes 84051128
  24.8 2.7 %branch_1_fun.8 = (bf16[64,4096]{1,0:T(8,128)(2,1)S(1)}, f32[64,128]{1,0:T(8,128)S(1)}) custom-call(bf16[128,4096]{1,0:T(8,128)(2,1)} %bitcast.40, f32[64,128]{1,0:T(8,128)S(1)} %get-tuple-element.313.refs_1_, bf16[8,4096]{1,0:T(8,128)(2,1)} %get-tuple-element.314.refs_2_, bf16[8,4096]{1,0:T(8,128)(2,1)S(1)} %get-tuple-element.315.refs_3_, ...), custom_call_target="tpu_custom_call" | custom-call | flops 67108864 | bytes 2097152 | tf_op jit(solution)/shard_map/cond/branch_1_fun/pallas_call | solution.py:118
  28.7 2.5 %branch_1_fun.9 = (bf16[32,1024]{1,0:T(8,128)(2,1)S(1)}, bf16[32,1024]{1,0:T(8,128)(2,1)S(1)}, bf16[32,1024]{1,0:T(8,128)(2,1)S(1)}, bf16[32,1024]{1,0:T(8,128)(...) custom-call(s32[8]{0:T(128)S(1)} %add.279.refs_0_, ...), custom_call_target="tpu_custom_call" | custom-call | flops 67108864 | bytes 2621440 | tf_op jit(solution)/shard_map/cond/branch_1_fun/pallas_call | solution.py:153
  31.2 6.2 %branch_1_fun.11 = bf16[2,64,1024]{2,1,0:T(8,128)(2,1)S(1)} custom-call(s32[1]{0:T(128)S(6)} %sub.87.side_ref, bf16[64,4096]{1,0:T(8,128)(2,1)S(1)} %get-tuple-element.349.x_ref, bf16[4096,2048]{1,0:T(8,128)(2,1)} %get-tuple-element.423.gate_ref, bf16[4096,2048]{1,0:T(8,128)(2,1)} %get-tuple-element.425.up_ref), custom_call_target="tpu_custom_call" | custom-call | flops 1073741824 | bytes 17301504 | tf_op jit(solution)/shard_map/cond/branch_1_fun/pallas_call | solution.py:192
  40.2 3.5 %collective-permute-start.30 = (bf16[32,1024]{1,0:T(8,128)(2,1)S(1)}, bf16[32,1024]{1,0:T(8,128)(2,1)S(1)}, u32[]{:S(2)}, u32[]{:S(2)}) collective-permute-start(bf16[32,1024]{1,0:T(8,128)(2,1)S(1)} %get-tuple-element.359), channel_id=1, source_target_pairs={{0,8},{2,10},{4,12},{6,14},{8,0},{10,2},{12,4},{14,6},{1,9},{3,11}... | collective-permute-start | bytes 196616 | tf_op jit(solution)/shard_map/cond/branch_1_fun/ppermute | solution.py:78
  44.8 2.0 %collective-permute-start.32 = (bf16[32,1024]{1,0:T(8,128)(2,1)S(1)}, bf16[32,1024]{1,0:T(8,128)(2,1)S(1)}, u32[]{:S(2)}, u32[]{:S(2)}) collective-permute-start(bf16[32,1024]{1,0:T(8,128)(2,1)S(1)} %get-tuple-element.361), channel_id=1, source_target_pairs={{0,12},{2,14},{4,0},{6,2},{8,4},{10,6},{12,8},{14,10},{1,13},{3,15... | collective-permute-start | bytes 196616 | tf_op jit(solution)/shard_map/cond/branch_1_fun/ppermute | solution.py:78
  47.4 1.6 %collective-permute-start.33 = (bf16[32,1024]{1,0:T(8,128)(2,1)S(1)}, bf16[32,1024]{1,0:T(8,128)(2,1)S(1)}, u32[]{:S(2)}, u32[]{:S(2)}) collective-permute-start(bf16[32,1024]{1,0:T(8,128)(2,1)S(1)} %get-tuple-element.362), channel_id=1, source_target_pairs={{0,14},{2,12},{4,2},{6,0},{8,6},{10,4},{12,10},{14,8},{1,15},{3,13... | collective-permute-start | bytes 196616 | tf_op jit(solution)/shard_map/cond/branch_1_fun/ppermute | solution.py:78
  49.0 6.2 %branch_1_fun.10.refs_0_ = f32[2,64,1024]{2,1,0:T(8,128)S(1)} custom-call(s32[1]{0:T(128)} %get-tuple-element.311.side_ref.core_ref, bf16[64,4096]{1,0:T(8,128)(2,1)S(1)} %get-tuple-element.349.x_ref, bf16[4096,2048]{1,0:T(8,128)(2,1)} %get-tuple-element.423.gate_ref, bf16[4096,2048]{1,0:T(8,128)(2,1)} %get-tuple-element.425.up_ref), custom_call_target="tpu_custom_call" | custom-call | flops 1073741824 | bytes 17301504 | tf_op jit(solution)/shard_map/cond/branch_1_fun/pallas_call | solution.py:192
  55.3 1.8 %branch_1_fun.12 = (bf16[64,1024]{1,0:T(8,128)(2,1)S(1)}, bf16[16,1024]{1,0:T(8,128)(2,1)S(1)}, bf16[16,1024]{1,0:T(8,128)(2,1)S(1)}, bf16[16,1024]{1,0:T(8,128)...) custom-call(f32[2,64,1024]{2,1,0:T(8,128)S(1)} %branch_1_fun.10.refs, ...), custom_call_target="tpu_custom_call" | custom-call | flops 83886080 | bytes 1572864 | tf_op jit(solution)/shard_map/cond/branch_1_fun/pallas_call | solution.py:232
  60.0 3.2 %collective-permute-start.38 = (bf16[16,1024]{1,0:T(8,128)(2,1)S(1)}, bf16[16,1024]{1,0:T(8,128)(2,1)S(1)}, u32[]{:S(2)}, u32[]{:S(2)}) collective-permute-start(bf16[16,1024]{1,0:T(8,128)(2,1)S(1)} %get-tuple-element.369), channel_id=1, source_target_pairs={{0,8},{2,10},{4,12},{6,14},{8,0},{10,2},{12,4},{14,6},{1,9},{3,11}... | collective-permute-start | bytes 98312 | tf_op jit(solution)/shard_map/cond/branch_1_fun/ppermute | solution.py:78
  63.4 3.4 %collective-permute-start.40 = (bf16[16,1024]{1,0:T(8,128)(2,1)S(1)}, bf16[16,1024]{1,0:T(8,128)(2,1)S(1)}, u32[]{:S(2)}, u32[]{:S(2)}) collective-permute-start(bf16[16,1024]{1,0:T(8,128)(2,1)S(1)} %get-tuple-element.371), channel_id=1, source_target_pairs={{0,12},{2,14},{4,0},{6,2},{8,4},{10,6},{12,8},{14,10},{1,13},{3,15... | collective-permute-start | bytes 98312 | tf_op jit(solution)/shard_map/cond/branch_1_fun/ppermute | solution.py:78
  66.8 1.6 %collective-permute-start.41 = (bf16[16,1024]{1,0:T(8,128)(2,1)S(1)}, bf16[16,1024]{1,0:T(8,128)(2,1)S(1)}, u32[]{:S(2)}, u32[]{:S(2)}) collective-permute-start(bf16[16,1024]{1,0:T(8,128)(2,1)S(1)} %get-tuple-element.372), channel_id=1, source_target_pairs={{0,14},{2,12},{4,2},{6,0},{8,6},{10,4},{12,10},{14,8},{1,15},{3,13... | collective-permute-start | bytes 98312 | tf_op jit(solution)/shard_map/cond/branch_1_fun/ppermute | solution.py:78
  68.5 6.6 %branch_1_fun.13.base_ref = f32[64,4096]{1,0:T(8,128)S(1)} custom-call(s32[1]{0:T(128)} %get-tuple-element.311.side_ref.core_ref, bf16[64,1024]{1,0:T(8,128)(2,1)S(1)} %get-tuple-element.363.near_ref, bf16[64,1024]{1,0:T(8,128)(2,1)S(1)} %collective-permute-done.34.far_ref, bf16[2048,4096]{1,0:T(8,128)(2,1)} %get-tuple-element.427.weight_ref), custom_call_target="tpu_custom_call" | custom-call | flops 1073741824 | bytes 17825792 | tf_op jit(solution)/shard_map/cond/branch_1_fun/pallas_call | solution.py:273
  77.3 1.5 %branch_1_fun.15 = (bf16[8,4096]{1,0:T(8,128)(2,1)S(1)}, bf16[8,4096]{1,0:T(8,128)(2,1)S(1)}, bf16[8,4096]{1,0:T(8,128)(2,1)S(1)}, bf16[8,4096]{1,0:T(8,128)(2,1...) custom-call(f32[64,4096]{1,0:T(8,128)S(1)} %branch_1_fun.13.base_ref, ...), custom_call_target="tpu_custom_call" | custom-call | flops 33554432 | bytes 2097152 | tf_op jit(solution)/shard_map/cond/branch_1_fun/pallas_call | solution.py:334
  80.9 3.8 %collective-permute-start.46 = (bf16[8,4096]{1,0:T(8,128)(2,1)S(1)}, bf16[8,4096]{1,0:T(8,128)(2,1)S(1)}, u32[]{:S(2)}, u32[]{:S(2)}) collective-permute-start(bf16[8,4096]{1,0:T(8,128)(2,1)S(1)} %get-tuple-element.389), channel_id=1, source_target_pairs={{0,8},{2,10},{4,12},{6,14},{8,0},{10,2},{12,4},{14,6},{1,9},{3,11}... | collective-permute-start | bytes 196616 | tf_op jit(solution)/shard_map/cond/branch_1_fun/ppermute | solution.py:78
  84.7 3.7 %collective-permute-start.48 = (bf16[8,4096]{1,0:T(8,128)(2,1)S(1)}, bf16[8,4096]{1,0:T(8,128)(2,1)S(1)}, u32[]{:S(2)}, u32[]{:S(2)}) collective-permute-start(bf16[8,4096]{1,0:T(8,128)(2,1)S(1)} %get-tuple-element.391), channel_id=1, source_target_pairs={{0,12},{2,14},{4,0},{6,2},{8,4},{10,6},{12,8},{14,10},{1,13},{3,15... | collective-permute-start | bytes 196616 | tf_op jit(solution)/shard_map/cond/branch_1_fun/ppermute | solution.py:78
  88.3 1.6 %collective-permute-start.49 = (bf16[8,4096]{1,0:T(8,128)(2,1)S(1)}, bf16[8,4096]{1,0:T(8,128)(2,1)S(1)}, u32[]{:S(2)}, u32[]{:S(2)}) collective-permute-start(bf16[8,4096]{1,0:T(8,128)(2,1)S(1)} %get-tuple-element.392), channel_id=1, source_target_pairs={{0,14},{2,12},{4,2},{6,0},{8,6},{10,4},{12,10},{14,8},{1,15},{3,13... | collective-permute-start | bytes 196616 | tf_op jit(solution)/shard_map/cond/branch_1_fun/ppermute | solution.py:78
  90.7 2.6 %collective-permute-done.47 = bf16[8,4096]{1,0:T(8,128)(2,1)S(1)} collective-permute-done((bf16[8,4096]{1,0:T(8,128)(2,1)S(1)}, bf16[8,4096]{1,0:T(8,128)(2,1)S(1)}, u32[]{:S(2)}, u32[]{:S(2)}) %collective-permute-start.47) | collective-permute-done | bytes 65568 | tf_op jit(solution)/shard_map/cond/branch_1_fun/ppermute | solution.py:78
  (116 shorter events, 23.5 us)
Async XLA Ops:
  0.0 12.2 %collective-permute-start.51 = (bf16[8,4096]{1,0:T(8,128)(2,1)}, bf16[8,4096]{1,0:T(8,128)(2,1)S(1)}, u32[]{:S(2)}, u32[]{:S(2)}) collective-permute-start(bf16[8,4096]{1,0:T(8,128)(2,1)} %param.12), channel_id=1, source_target_pairs={{0,4},{2,6},{4,8},{6,10},{8,12},{10,14},{12,0},{14,2},{1,5},{3,7},... | collective-permute-start | bytes 196616 | tf_op jit(solution)/shard_map/ppermute | solution.py:62
  3.0 9.2 %collective-permute-start.52 = (bf16[8,4096]{1,0:T(8,128)(2,1)}, bf16[8,4096]{1,0:T(8,128)(2,1)S(1)}, u32[]{:S(2)}, u32[]{:S(2)}) collective-permute-start(bf16[8,4096]{1,0:T(8,128)(2,1)} %param.12), channel_id=1, source_target_pairs={{0,8},{2,10},{4,12},{6,14},{8,0},{10,2},{12,4},{14,6},{1,9},{3,11}... | collective-permute-start | bytes 196616 | tf_op jit(solution)/shard_map/ppermute | solution.py:62
  5.6 6.6 %collective-permute-start.53 = (bf16[8,4096]{1,0:T(8,128)(2,1)}, bf16[8,4096]{1,0:T(8,128)(2,1)S(1)}, u32[]{:S(2)}, u32[]{:S(2)}) collective-permute-start(bf16[8,4096]{1,0:T(8,128)(2,1)} %param.12), channel_id=1, source_target_pairs={{0,12},{2,14},{4,0},{6,2},{8,4},{10,6},{12,8},{14,10},{1,13},{3,15... | collective-permute-start | bytes 196616 | tf_op jit(solution)/shard_map/ppermute | solution.py:62
  7.0 14.0 %collective-permute-start.54 = (bf16[8,4096]{1,0:T(8,128)(2,1)}, bf16[8,4096]{1,0:T(8,128)(2,1)S(1)}, u32[]{:S(2)}, u32[]{:S(2)}) collective-permute-start(bf16[8,4096]{1,0:T(8,128)(2,1)} %param.12), channel_id=1, source_target_pairs={{0,2},{2,0},{4,6},{6,4},{8,10},{10,8},{12,14},{14,12},{1,3},{3,1},... | collective-permute-start | bytes 196616 | tf_op jit(solution)/shard_map/ppermute | solution.py:65
  10.1 9.1 %collective-permute-start.50 = (s32[1]{0:T(128)}, s32[1]{0:T(128)}, u32[]{:S(2)}, u32[]{:S(2)}) collective-permute-start(s32[1]{0:T(128)} %bitcast.7), channel_id=1, source_target_pairs={{0,16},{16,0},{1,17},{17,1},{2,18},{18,2},{3,19},{19,3},{4,20},{20... | collective-permute-start | bytes 20 | tf_op jit(solution)/shard_map/ppermute | solution.py:396
  16.7 7.8 %collective-permute-start.58 = (bf16[64,8192]{1,0:T(8,128)(2,1)S(1)}, bf16[64,8192]{1,0:T(8,128)(2,1)S(1)}, u32[]{:S(2)}, u32[]{:S(2)}) collective-permute-start(bf16[64,8192]{1,0:T(8,128)(2,1)S(1)} %shard_map.114), channel_id=1, source_target_pairs={{0,1},{1,0},{2,3},{3,2},{4,5},{5,4},{6,7},{7,6},{8,9},{9,8},{10,11... | collective-permute-start | bytes 3145736 | tf_op jit(solution)/shard_map/ppermute | solution.py:378
  37.5 17.8 %collective-permute-start.26 = (bf16[2,64,1024]{2,1,0:T(8,128)(2,1)S(1)}, bf16[2,64,1024]{2,1,0:T(8,128)(2,1)S(1)}, u32[]{:S(2)}, u32[]{:S(2)}) collective-permute-start(bf16[2,64,1024]{2,1,0:T(8,128)(2,1)S(1)} %branch_1_fun.11), channel_id=1, source_target_pairs={{0,1},{1,0},{2,3},{3,2},{4,5},{5,4},{6,7},{7,6},{8,9},{9,8},{10,11... | collective-permute-start | bytes 786440 | tf_op jit(solution)/shard_map/cond/branch_1_fun/ppermute | solution.py:378
  38.3 6.6 %collective-permute-start.28 = (bf16[32,1024]{1,0:T(8,128)(2,1)S(1)}, bf16[32,1024]{1,0:T(8,128)(2,1)S(1)}, u32[]{:S(2)}, u32[]{:S(2)}) collective-permute-start(bf16[32,1024]{1,0:T(8,128)(2,1)S(1)} %get-tuple-element.357), channel_id=1, source_target_pairs={{0,4},{2,6},{4,8},{6,10},{8,12},{10,14},{12,0},{14,2},{1,5},{3,7},... | collective-permute-start | bytes 196616 | tf_op jit(solution)/shard_map/cond/branch_1_fun/ppermute | solution.py:78
  39.2 8.2 %collective-permute-start.29 = (bf16[32,1024]{1,0:T(8,128)(2,1)S(1)}, bf16[32,1024]{1,0:T(8,128)(2,1)S(1)}, u32[]{:S(2)}, u32[]{:S(2)}) collective-permute-start(bf16[32,1024]{1,0:T(8,128)(2,1)S(1)} %get-tuple-element.358), channel_id=1, source_target_pairs={{0,6},{2,4},{4,10},{6,8},{8,14},{10,12},{12,2},{14,0},{1,7},{3,5},... | collective-permute-start | bytes 196616 | tf_op jit(solution)/shard_map/cond/branch_1_fun/ppermute | solution.py:78
  40.2 15.1 %collective-permute-start.30 = (bf16[32,1024]{1,0:T(8,128)(2,1)S(1)}, bf16[32,1024]{1,0:T(8,128)(2,1)S(1)}, u32[]{:S(2)}, u32[]{:S(2)}) collective-permute-start(bf16[32,1024]{1,0:T(8,128)(2,1)S(1)} %get-tuple-element.359), channel_id=1, source_target_pairs={{0,8},{2,10},{4,12},{6,14},{8,0},{10,2},{12,4},{14,6},{1,9},{3,11}... | collective-permute-start | bytes 196616 | tf_op jit(solution)/shard_map/cond/branch_1_fun/ppermute | solution.py:78
  43.6 11.6 %collective-permute-start.31 = (bf16[32,1024]{1,0:T(8,128)(2,1)S(1)}, bf16[32,1024]{1,0:T(8,128)(2,1)S(1)}, u32[]{:S(2)}, u32[]{:S(2)}) collective-permute-start(bf16[32,1024]{1,0:T(8,128)(2,1)S(1)} %get-tuple-element.360), channel_id=1, source_target_pairs={{0,10},{2,8},{4,14},{6,12},{8,2},{10,0},{12,6},{14,4},{1,11},{3,9}... | collective-permute-start | bytes 196616 | tf_op jit(solution)/shard_map/cond/branch_1_fun/ppermute | solution.py:78
  44.8 10.4 %collective-permute-start.32 = (bf16[32,1024]{1,0:T(8,128)(2,1)S(1)}, bf16[32,1024]{1,0:T(8,128)(2,1)S(1)}, u32[]{:S(2)}, u32[]{:S(2)}) collective-permute-start(bf16[32,1024]{1,0:T(8,128)(2,1)S(1)} %get-tuple-element.361), channel_id=1, source_target_pairs={{0,12},{2,14},{4,0},{6,2},{8,4},{10,6},{12,8},{14,10},{1,13},{3,15... | collective-permute-start | bytes 196616 | tf_op jit(solution)/shard_map/cond/branch_1_fun/ppermute | solution.py:78
  47.4 7.9 %collective-permute-start.33 = (bf16[32,1024]{1,0:T(8,128)(2,1)S(1)}, bf16[32,1024]{1,0:T(8,128)(2,1)S(1)}, u32[]{:S(2)}, u32[]{:S(2)}) collective-permute-start(bf16[32,1024]{1,0:T(8,128)(2,1)S(1)} %get-tuple-element.362), channel_id=1, source_target_pairs={{0,14},{2,12},{4,2},{6,0},{8,6},{10,4},{12,10},{14,8},{1,15},{3,13... | collective-permute-start | bytes 196616 | tf_op jit(solution)/shard_map/cond/branch_1_fun/ppermute | solution.py:78
  57.1 9.7 %collective-permute-start.34 = (bf16[64,1024]{1,0:T(8,128)(2,1)S(1)}, bf16[64,1024]{1,0:T(8,128)(2,1)S(1)}, u32[]{:S(2)}, u32[]{:S(2)}) collective-permute-start(bf16[64,1024]{1,0:T(8,128)(2,1)S(1)} %get-tuple-element.363.near_ref), channel_id=1, source_target_pairs={{0,1},{1,0},{2,3},{3,2},{4,5},{5,4},{6,7},{7,6},{8,9},{9,8},{10,11... | collective-permute-start | bytes 393224 | tf_op jit(solution)/shard_map/cond/branch_1_fun/ppermute | solution.py:378
  59.2 15.9 %collective-permute-start.37 = (bf16[16,1024]{1,0:T(8,128)(2,1)S(1)}, bf16[16,1024]{1,0:T(8,128)(2,1)S(1)}, u32[]{:S(2)}, u32[]{:S(2)}) collective-permute-start(bf16[16,1024]{1,0:T(8,128)(2,1)S(1)} %get-tuple-element.368), channel_id=1, source_target_pairs={{0,6},{2,4},{4,10},{6,8},{8,14},{10,12},{12,2},{14,0},{1,7},{3,5},... | collective-permute-start | bytes 98312 | tf_op jit(solution)/shard_map/cond/branch_1_fun/ppermute | solution.py:78
  60.0 15.1 %collective-permute-start.38 = (bf16[16,1024]{1,0:T(8,128)(2,1)S(1)}, bf16[16,1024]{1,0:T(8,128)(2,1)S(1)}, u32[]{:S(2)}, u32[]{:S(2)}) collective-permute-start(bf16[16,1024]{1,0:T(8,128)(2,1)S(1)} %get-tuple-element.369), channel_id=1, source_target_pairs={{0,8},{2,10},{4,12},{6,14},{8,0},{10,2},{12,4},{14,6},{1,9},{3,11}... | collective-permute-start | bytes 98312 | tf_op jit(solution)/shard_map/cond/branch_1_fun/ppermute | solution.py:78
  63.2 11.9 %collective-permute-start.39 = (bf16[16,1024]{1,0:T(8,128)(2,1)S(1)}, bf16[16,1024]{1,0:T(8,128)(2,1)S(1)}, u32[]{:S(2)}, u32[]{:S(2)}) collective-permute-start(bf16[16,1024]{1,0:T(8,128)(2,1)S(1)} %get-tuple-element.370), channel_id=1, source_target_pairs={{0,10},{2,8},{4,14},{6,12},{8,2},{10,0},{12,6},{14,4},{1,11},{3,9}... | collective-permute-start | bytes 98312 | tf_op jit(solution)/shard_map/cond/branch_1_fun/ppermute | solution.py:78
  63.4 11.7 %collective-permute-start.40 = (bf16[16,1024]{1,0:T(8,128)(2,1)S(1)}, bf16[16,1024]{1,0:T(8,128)(2,1)S(1)}, u32[]{:S(2)}, u32[]{:S(2)}) collective-permute-start(bf16[16,1024]{1,0:T(8,128)(2,1)S(1)} %get-tuple-element.371), channel_id=1, source_target_pairs={{0,12},{2,14},{4,0},{6,2},{8,4},{10,6},{12,8},{14,10},{1,13},{3,15... | collective-permute-start | bytes 98312 | tf_op jit(solution)/shard_map/cond/branch_1_fun/ppermute | solution.py:78
  66.8 8.3 %collective-permute-start.41 = (bf16[16,1024]{1,0:T(8,128)(2,1)S(1)}, bf16[16,1024]{1,0:T(8,128)(2,1)S(1)}, u32[]{:S(2)}, u32[]{:S(2)}) collective-permute-start(bf16[16,1024]{1,0:T(8,128)(2,1)S(1)} %get-tuple-element.372), channel_id=1, source_target_pairs={{0,14},{2,12},{4,2},{6,0},{8,6},{10,4},{12,10},{14,8},{1,15},{3,13... | collective-permute-start | bytes 98312 | tf_op jit(solution)/shard_map/cond/branch_1_fun/ppermute | solution.py:78
  79.3 9.1 %collective-permute-start.44 = (bf16[8,4096]{1,0:T(8,128)(2,1)S(1)}, bf16[8,4096]{1,0:T(8,128)(2,1)S(1)}, u32[]{:S(2)}, u32[]{:S(2)}) collective-permute-start(bf16[8,4096]{1,0:T(8,128)(2,1)S(1)} %get-tuple-element.387), channel_id=1, source_target_pairs={{0,4},{2,6},{4,8},{6,10},{8,12},{10,14},{12,0},{14,2},{1,5},{3,7},... | collective-permute-start | bytes 196616 | tf_op jit(solution)/shard_map/cond/branch_1_fun/ppermute | solution.py:78
  80.7 9.3 %collective-permute-start.45 = (bf16[8,4096]{1,0:T(8,128)(2,1)S(1)}, bf16[8,4096]{1,0:T(8,128)(2,1)S(1)}, u32[]{:S(2)}, u32[]{:S(2)}) collective-permute-start(bf16[8,4096]{1,0:T(8,128)(2,1)S(1)} %get-tuple-element.388), channel_id=1, source_target_pairs={{0,6},{2,4},{4,10},{6,8},{8,14},{10,12},{12,2},{14,0},{1,7},{3,5},... | collective-permute-start | bytes 196616 | tf_op jit(solution)/shard_map/cond/branch_1_fun/ppermute | solution.py:78
  80.9 9.8 %collective-permute-start.46 = (bf16[8,4096]{1,0:T(8,128)(2,1)S(1)}, bf16[8,4096]{1,0:T(8,128)(2,1)S(1)}, u32[]{:S(2)}, u32[]{:S(2)}) collective-permute-start(bf16[8,4096]{1,0:T(8,128)(2,1)S(1)} %get-tuple-element.389), channel_id=1, source_target_pairs={{0,8},{2,10},{4,12},{6,14},{8,0},{10,2},{12,4},{14,6},{1,9},{3,11}... | collective-permute-start | bytes 196616 | tf_op jit(solution)/shard_map/cond/branch_1_fun/ppermute | solution.py:78
  84.7 8.6 %collective-permute-start.47 = (bf16[8,4096]{1,0:T(8,128)(2,1)S(1)}, bf16[8,4096]{1,0:T(8,128)(2,1)S(1)}, u32[]{:S(2)}, u32[]{:S(2)}) collective-permute-start(bf16[8,4096]{1,0:T(8,128)(2,1)S(1)} %get-tuple-element.390), channel_id=1, source_target_pairs={{0,10},{2,8},{4,14},{6,12},{8,2},{10,0},{12,6},{14,4},{1,11},{3,9}... | collective-permute-start | bytes 196616 | tf_op jit(solution)/shard_map/cond/branch_1_fun/ppermute | solution.py:78
  84.7 8.6 %collective-permute-start.48 = (bf16[8,4096]{1,0:T(8,128)(2,1)S(1)}, bf16[8,4096]{1,0:T(8,128)(2,1)S(1)}, u32[]{:S(2)}, u32[]{:S(2)}) collective-permute-start(bf16[8,4096]{1,0:T(8,128)(2,1)S(1)} %get-tuple-element.391), channel_id=1, source_target_pairs={{0,12},{2,14},{4,0},{6,2},{8,4},{10,6},{12,8},{14,10},{1,13},{3,15... | collective-permute-start | bytes 196616 | tf_op jit(solution)/shard_map/cond/branch_1_fun/ppermute | solution.py:78
  (13 other events, 76.7 us)

commit v4 on v3

--- a/solution.py
+++ b/solution.py
@@ -1,3 +1,5 @@
+import functools
+
 import jax
 import jax.numpy as jnp
 from jax import lax
@@ -50,6 +52,12 @@
         else:
             self.order = steps
 
+    def sent_at(self):
+        steps = jnp.arange(self.shards, dtype=I32)
+        if not self.direct:
+            return steps
+        return steps % self.fast * self.slow + steps // self.fast
+
     def back(self, a, c):
         S, F = self.slow, self.fast
         return [(s * F + f, (s - a) % S * F + (f - c) % F) for s in range(S) for f in range(F)]
@@ -67,9 +75,12 @@
                 )
         return got
 
+    def spread(self, blocks):
+        return lax.all_to_all(blocks, "ff", 0, 0, tiled=True)
+
     def deliver(self, blocks):
         if not self.direct:
-            return list(lax.all_to_all(jnp.stack(blocks), "ff", 0, 0, tiled=True))
+            return list(self.spread(jnp.stack(blocks)))
         got = [None] * self.shards
         got[0] = blocks[0]
         for b in range(1, self.shards):
@@ -78,25 +89,53 @@
             got[back] = lax.ppermute(blocks[b], "ff", self.back(a, c))
         return got
 
-
-def copy_kernel(at_ref, in_ref, out_ref):
-    out_ref[...] = in_ref[...]
-
-
-def pick_columns(at, factors, half):
-    depth, count = factors.shape[0], at.shape[0]
-    return pl.pallas_call(
-        copy_kernel,
-        out_shape=jax.ShapeDtypeStruct((depth, count * half), factors.dtype),
+    def slow_steps(self, blocks):
+        got = [blocks[0]] + [None] * (self.slow - 1)
+        for a in range(1, self.slow):
+            got[(-a) % self.slow] = lax.ppermute(blocks[a], "ff", self.back(a, 0))
+        return got
+
+
+def stage_kernel(
+    here_ref, there_ref, x_ref, expand_ref, shrink_ref, kept_ref, near_ref, far_ref, held_ref, sems
+):
+    half = near_ref.shape[1] // (sems.shape[0] - 1)
+    copies = []
+    for side, (at_ref, out) in enumerate(((there_ref, far_ref), (here_ref, near_ref))):
+        for b in range(sems.shape[0] - 1):
+            columns = pl.ds(pl.multiple_of(at_ref[b] * half, half), half)
+            put = out.at[:, pl.ds(b * half, half)]
+            copies.append(pltpu.make_async_copy(expand_ref.at[:, columns], put, sems.at[b, side]))
+    copies.append(pltpu.make_async_copy(shrink_ref, held_ref, sems.at[sems.shape[0] - 1, 0]))
+    for copy in copies:
+        copy.start()
+    kept_ref[...] = x_ref[...]
+    for copy in copies:
+        copy.wait()
+
+
+def stage(at_here, at_there, x, expand, shrink):
+    depth, width = expand.shape
+    shards = at_here.shape[0]
+    out = jax.ShapeDtypeStruct((depth, width // 2), BF)
+    return pl.pallas_call(
+        stage_kernel,
+        out_shape=(
+            jax.ShapeDtypeStruct(x.shape, BF),
+            out,
+            out,
+            jax.ShapeDtypeStruct(shrink.shape, BF),
+        ),
         grid_spec=pltpu.PrefetchScalarGridSpec(
-            num_scalar_prefetch=1,
-            grid=(count,),
-            in_specs=[pl.BlockSpec((depth, half), lambda j, at: (0, at[j]))],
-            out_specs=pl.BlockSpec((depth, half), lambda j, at: (0, j)),
-        ),
-        compiler_params=params(8),
-        cost_estimate=cost(0, 4 * depth * count * half),
-    )(at, factors)
+            num_scalar_prefetch=2,
+            grid=(1,),
+            in_specs=[fixed(x)] + [pl.BlockSpec(memory_space=pl.ANY)] * 2,
+            out_specs=(fixed(x), fixed(out), fixed(out), fixed(shrink)),
+            scratch_shapes=[pltpu.SemaphoreType.DMA((shards + 1, 2))],
+        ),
+        compiler_params=params(16),
+        cost_estimate=cost(0, 2 * (2 * expand.size + 2 * shrink.size)),
+    )(at_here, at_there, x, expand, shrink)
 
 
 def low_in_kernel(count, shrink_ref, mask_ref, *refs):
@@ -130,10 +169,7 @@
     )(shrink, mask, *parts)
 
 
-def expand_kernel(count, at_ref, own_ref, got_ref, pick_ref, cols_ref, far_ref, *refs):
-    near_refs, out_refs = refs[:count], refs[count:]
-    cap = pick_ref.shape[0]
-    half = out_refs[0].shape[1]
+def expand_kernel(fast, own_ref, got_ref, pick_ref, cols_ref, near_ref, far_ref, *out_refs):
     low = (own_ref[...] + got_ref[...]).astype(BF)
     picked = dot(pick_ref[...], low).astype(BF)
     lhs = [
@@ -141,28 +177,24 @@
         for side in range(2)
     ]
     lhs = [side.astype(BF) for side in lhs]
-    for b in range(count):
-        far = far_ref[:, b * half : (b + 1) * half]
-        out_refs[b][...] = (dot(lhs[0], near_refs[b][...]) + dot(lhs[1], far)).astype(BF)
-
-
-def expand_rows(at, own, got, pick, cols, near, far, half):
-    cap, count, depth = pick.shape[0], at.shape[0], near.shape[0]
-    column = lambda b: pl.BlockSpec((depth, half), lambda i, at: (0, at[b]))
-    out = jax.ShapeDtypeStruct((2 * cap, half), BF)
-    return pl.pallas_call(
-        lambda *refs: expand_kernel(count, *refs),
-        out_shape=(out,) * count,
-        grid_spec=pltpu.PrefetchScalarGridSpec(
-            num_scalar_prefetch=1,
-            grid=(1,),
-            in_specs=[fixed(own), fixed(got), fixed(pick), fixed(cols), fixed(far)]
-            + [column(b) for b in range(count)],
-            out_specs=(fixed(out),) * count,
-        ),
+    tall = lhs[0].shape[0]
+    half = out_refs[0].shape[1]
+    for b in range(near_ref.shape[1] // half):
+        here = pl.ds(b * half, half)
+        delta = dot(lhs[0], near_ref[:, here]) + dot(lhs[1], far_ref[:, here])
+        out_refs[b % fast][pl.ds(b // fast * tall, tall)] = delta.astype(BF)
+
+
+def expand_rows(own, got, pick, cols, near, far, shards, fast):
+    cap = pick.shape[0]
+    depth, width = near.shape
+    out = jax.ShapeDtypeStruct((2 * cap * shards // fast, width // shards), BF)
+    return pl.pallas_call(
+        functools.partial(expand_kernel, fast),
+        out_shape=(out,) * fast,
         compiler_params=params(16),
-        cost_estimate=cost(8 * cap * depth * count * half, 4 * (depth + cap) * count * half),
-    )(at, own, got, pick, cols, far, *[near] * count)
+        cost_estimate=cost(8 * cap * depth * width, 4 * (depth + cap) * width),
+    )(own, got, pick, cols, near, far)
 
 
 def base_kernel(side_ref, x_ref, gate_ref, up_ref, out_ref, held, sums, sems):
@@ -211,39 +243,57 @@
 def hidden_kernel(count, own_ref, got_ref, place_ref, send_ref, *refs):
     parts, hid_ref, out_refs = refs[:count], refs[count], refs[count + 1 :]
     rows = hid_ref.shape[0]
-    cap = out_refs[0].shape[0]
+    tall = out_refs[0].shape[0]
     delta = dot(place_ref[...], jnp.concatenate([part[...] for part in parts], axis=0))
     gate = own_ref[0] + got_ref[0].astype(F32) + delta[:rows]
     up = own_ref[1] + got_ref[1].astype(F32) + delta[rows:]
     hidden = (gate / (1.0 + jnp.exp(-gate)) * up).astype(BF)
     hid_ref[...] = hidden
     sent = dot(send_ref[...], hidden).astype(BF)
-    for b in range(count):
-        out_refs[b][...] = sent[b * cap : (b + 1) * cap]
-
-
-def hidden_half(own, got, parts, place, send):
-    count = len(parts)
+    for n, out_ref in enumerate(out_refs):
+        out_ref[...] = sent[n * tall : (n + 1) * tall]
+
+
+def hidden_half(own, got, parts, place, send, count):
     rows, half = own.shape[1:]
     block = min(256, half)
-    cap = send.shape[0] // count
+    tall = send.shape[0] // count
     both = pl.BlockSpec((2, rows, block), lambda n: (0, 0, n))
     flat = lambda depth: pl.BlockSpec((depth, block), lambda n: (0, n))
     return pl.pallas_call(
-        lambda *refs: hidden_kernel(count, *refs),
+        functools.partial(hidden_kernel, len(parts)),
         out_shape=(jax.ShapeDtypeStruct((rows, half), BF),)
-        + (jax.ShapeDtypeStruct((cap, half), BF),) * count,
+        + (jax.ShapeDtypeStruct((tall, half), BF),) * count,
         grid=(half // block,),
-        in_specs=[both, both, fixed(place), fixed(send)] + [flat(parts[0].shape[0])] * count,
-        out_specs=(flat(rows),) + (flat(cap),) * count,
+        in_specs=[both, both, fixed(place), fixed(send)] + [flat(part.shape[0]) for part in parts],
+        out_specs=(flat(rows),) + (flat(tall),) * count,
         compiler_params=params(40),
         cost_estimate=cost(
-            2 * half * (place.size + send.size), 2 * half * (6 * rows + 3 * count * cap)
+            2 * half * (place.size + send.size),
+            2 * half * (6 * rows + place.shape[1] + send.shape[0]),
         ),
     )(own, got, place, send, *parts)
 
 
-def down_kernel(core_ref, near_ref, far_ref, weight_ref, out_ref, held, sems):
+def relay_kernel(own_ref, got_ref, *out_refs):
+    cap = out_refs[0].shape[0] // 2
+    for a, out_ref in enumerate(out_refs):
+        here = pl.ds(a * cap, cap)
+        out_ref[:cap] = own_ref[here]
+        out_ref[cap:] = got_ref[here]
+
+
+def relay(own, got, count):
+    tall, half = own.shape
+    return pl.pallas_call(
+        relay_kernel,
+        out_shape=(jax.ShapeDtypeStruct((2 * tall // count, half), BF),) * count,
+        compiler_params=params(16),
+        cost_estimate=cost(0, 8 * tall * half),
+    )(own, got)
+
+
+def down_kernel(first, core_ref, near_ref, far_ref, weight_ref, out_ref, held, sems):
     chunks = sems.shape[1]
     half, width = held.shape[1:]
     block = width // chunks
@@ -253,7 +303,9 @@
         for side, at in enumerate((core_ref[0], 1 - core_ref[0])):
             lines = pl.ds(pl.multiple_of(at * half, half), half)
             copy = pltpu.make_async_copy(
-                weight_ref.at[lines, here], held.at[side, :, here], sems.at[side, c]
+                weight_ref.at[lines, pl.ds(first + c * block, block)],
+                held.at[side, :, here],
+                sems.at[side, c],
             )
             copy.start()
             copies.append(copy)
@@ -266,12 +318,11 @@
         )
 
 
-def down_base(core, near, far, weight):
+def down_base(core, near, far, weight, first, width):
     rows, half = near.shape
-    width = weight.shape[1]
     chunks = max(width // 512, 1)
     return pl.pallas_call(
-        down_kernel,
+        functools.partial(down_kernel, first),
         out_shape=jax.ShapeDtypeStruct((rows, width), F32),
         grid_spec=pltpu.PrefetchScalarGridSpec(
             num_scalar_prefetch=1,
@@ -289,57 +340,63 @@
 
 
 def low_out_kernel(count, at_ref, mask_ref, *refs):
-    parts, shrinks, out_ref = refs[:count], refs[count : 2 * count], refs[2 * count]
-    pairs = sum(dot_last(part[...], shrink[...]) for part, shrink in zip(parts, shrinks))
+    parts, shrinks, out_ref = refs[:count], refs[count:-1], refs[-1]
+    cap = out_ref.shape[0]
+    blocks = [part[r : r + cap] for part in parts for r in range(0, part.shape[0], cap)]
+    pairs = sum(dot_last(block, shrink[...]) for block, shrink in zip(blocks, shrinks))
     out_ref[...] = jnp.where(mask_ref[...] > 0, pairs, 0.0)
 
 
 def low_out_pairs(at, parts, shrink, mask):
     count = len(parts)
-    cap, half = parts[0].shape
-    depth = shrink.shape[0]
+    half = parts[0].shape[1]
+    cap, depth = mask.shape
     column = lambda b: pl.BlockSpec((depth, half), lambda i, at: (0, at[b]))
     return pl.pallas_call(
-        lambda *refs: low_out_kernel(count, *refs),
+        functools.partial(low_out_kernel, count),
         out_shape=jax.ShapeDtypeStruct((cap, depth), F32),
         grid_spec=pltpu.PrefetchScalarGridSpec(
             num_scalar_prefetch=1,
             grid=(1,),
             in_specs=[fixed(mask)]
             + [fixed(part) for part in parts]
-            + [column(b) for b in range(count)],
+            + [column(b) for b in range(at.shape[0])],
             out_specs=fixed(mask),
         ),
         compiler_params=params(16),
-        cost_estimate=cost(2 * cap * depth * count * half, 2 * count * half * (depth + cap)),
-    )(at, mask, *parts, *[shrink] * count)
-
-
-def add_kernel(base_ref, own_ref, got_ref, pick_ref, expand_ref, *out_refs):
+        cost_estimate=cost(
+            2 * cap * depth * at.shape[0] * half, 2 * at.shape[0] * half * (depth + cap)
+        ),
+    )(at, mask, *parts, *[shrink] * at.shape[0])
+
+
+def add_kernel(count, *refs):
+    bases = refs[:count]
+    own_ref, got_ref, pick_ref, expand_ref = refs[count : count + 4]
+    out_refs = refs[count + 4 :]
     low = (own_ref[...] + got_ref[...]).astype(BF)
     spread = lax.dot_general(
         pick_ref[...], low, (((0,), (0,)), ((), ())), preferred_element_type=F32
     ).astype(BF)
-    total = base_ref[...] + dot(spread, expand_ref[...])
     own_rows = out_refs[0].shape[0]
-    for b, out_ref in enumerate(out_refs):
-        out_ref[...] = total[b * own_rows : (b + 1) * own_rows].astype(BF)
-
-
-def add_delta(base, own, got, pick, expand, count):
-    rows, width = base.shape
-    block = min(1024, width)
-    depth = expand.shape[0]
-    flat = lambda tall: pl.BlockSpec((tall, block), lambda n: (0, n))
-    return pl.pallas_call(
-        add_kernel,
+    first = 0
+    for base_ref in bases:
+        here = pl.ds(first, base_ref.shape[1])
+        total = base_ref[...] + dot(spread, expand_ref[:, here])
+        for b, out_ref in enumerate(out_refs):
+            out_ref[:, here] = total[b * own_rows : (b + 1) * own_rows].astype(BF)
+        first += base_ref.shape[1]
+
+
+def add_delta(bases, own, got, pick, expand, count):
+    rows = bases[0].shape[0]
+    depth, width = expand.shape
+    return pl.pallas_call(
+        functools.partial(add_kernel, len(bases)),
         out_shape=(jax.ShapeDtypeStruct((rows // count, width), BF),) * count,
-        grid=(width // block,),
-        in_specs=[flat(rows), fixed(own), fixed(got), fixed(pick), flat(depth)],
-        out_specs=(flat(rows // count),) * count,
-        compiler_params=params(24),
+        compiler_params=params(32),
         cost_estimate=cost(2 * rows * depth * width, width * (6 * rows + 2 * depth)),
-    )(base, own, got, pick, expand)
+    )(*bases, own, got, pick, expand)
 
 
 def tied(first, *others):
@@ -375,13 +432,23 @@
     there = 1 - here
     at_here = 2 * order + core
     at_there = 2 * order + 1 - core
+    split = ways.fast if ways.direct else 1
     swap = lambda a: lax.ppermute(a, "var", [(0, 1), (1, 0)])
 
     token_parts = ways.gather(tokens)
-    at_there, *token_parts[:: ways.fast] = tied(at_there, *token_parts[:: ways.fast])
-
-    near = expand_gu.reshape(slots * 2 * half_rank, -1)
-    far = swap(pick_columns(at_there, near, half))
+    kept, near, far, shrink_in = stage(
+        at_here,
+        at_there,
+        tokens,
+        expand_gu.reshape(slots * 2 * half_rank, -1),
+        shrink_gu.reshape(slots * 2 * rank, width),
+    )
+    if ways.direct:
+        token_parts[0] = kept
+        variant_ids, far, *token_parts[:: ways.fast] = tied(
+            variant_ids, far, *token_parts[:: ways.fast]
+        )
+    far = swap(far)
 
     ids = variant_ids[:, 0]
     matches = ids[:, None] == jnp.arange(variants, dtype=I32)[None, :]
@@ -400,10 +467,9 @@
     ).reshape(rows)
     slot_row, place = turned(slot_row), turned(place)
     owner = slot_row // slots
-    step = jnp.sum(
-        jnp.where(owner[:, None] == order[None, :], jnp.arange(shards, dtype=I32)[None, :], 0),
-        axis=1,
-    )
+    named = owner[:, None] == order[None, :]
+    block = jnp.sum(jnp.where(named, jnp.arange(shards, dtype=I32)[None, :], 0), axis=1)
+    step = jnp.sum(jnp.where(named, ways.sent_at()[None, :], 0), axis=1)
     local = slot_row - me * slots
     kinds = jnp.arange(2, dtype=I32)
     in_cols = jnp.arange(slots * 2 * rank, dtype=I32)
@@ -420,10 +486,14 @@
         & ((rank_at // half_rank)[None, :] == side[:, None])[None, :, :, None]
     ).astype(BF)
 
-    def finish(cap):
+    highest, token_parts[-1] = tied(highest, token_parts[-1])
+    x, low_own = low_in_pairs(token_parts, shrink_in, mask_in)
+    low_got = swap(low_own)
+
+    def partial_sums(cap):
         cells = jnp.arange(shards * cap, dtype=I32)
         send_rows = (cells[:, None] == (step * cap + place)[None, :]).astype(BF)
-        kind_cell = (step * 2 + kinds[:, None]) * cap + place
+        kind_cell = (block * 2 + kinds[:, None]) * cap + place
         kind_cells = jnp.arange(2 * shards * cap, dtype=I32)
         place_rows = (kind_cell[:, :, None] == kind_cells).astype(BF).reshape(2 * rows, -1)
         spots = jnp.arange(cap, dtype=I32)
@@ -433,28 +503,49 @@
         out_cols = jnp.arange(slots * rank, dtype=I32)
         mask_out = (spot_slot[:, None] == (out_cols // rank)[None, :]).astype(F32)
 
-        x, low_own = low_in_pairs(token_parts, shrink_gu.reshape(slots * 2 * rank, width), mask_in)
-        low_got = swap(low_own)
-        made = expand_rows(at_here, low_own, low_got, pick, cols, near, far, half)
-        x, *made = tied(x, *made)
-        base_got = swap(base_half(there, x, gate_weight, up_weight, half, BF))
-        delta = ways.deliver(made)
-        base_own = base_half(here, x, gate_weight, up_weight, half, F32)
-        hidden, *sent = hidden_half(base_own, base_got, delta, place_rows, send_rows)
+        made = expand_rows(low_own, low_got, pick, cols, near, far, shards, split)
+        held, *made = tied(x, *made)
+        if split == 2:
+            beside = lax.ppermute(made[1], "ff", ways.back(0, 1))
+            base_there = base_half(there, held, gate_weight, up_weight, half, BF)
+            base_there, beside = tied(base_there, beside)
+            made = relay(made[0], beside, ways.slow)
+            held, *made = tied(held, *made)
+            delta = ways.slow_steps(made)
+        else:
+            base_there = base_half(there, held, gate_weight, up_weight, half, BF)
+            delta = [ways.spread(made[0].reshape(shards, 2 * cap, half))]
+            delta = [delta[0].reshape(2 * shards * cap, half)]
+        base_got = swap(base_there)
+        base_own = base_half(here, held, gate_weight, up_weight, half, F32)
+        hidden, *sent = hidden_half(base_own, base_got, delta, place_rows, send_rows, split)
         hidden_far = swap(hidden)
-        hidden_rows = ways.deliver(sent)
-        base = down_base(here, hidden, hidden_far, down_weight)
-        base, *hidden_rows = tied(base, *hidden_rows)
+        side = width // 2
+        if split == 2:
+            beside = lax.ppermute(sent[1], "ff", ways.back(0, 1))
+            left = down_base(here, hidden, hidden_far, down_weight, 0, side)
+            left, beside = tied(left, beside)
+            sent = relay(sent[0], beside, ways.slow)
+            hidden, *sent = tied(hidden, *sent)
+            got = ways.slow_steps(sent)
+        else:
+            left = down_base(here, hidden, hidden_far, down_weight, 0, side)
+            got = [ways.spread(sent[0].reshape(shards, cap, half)).reshape(shards * cap, half)]
+        right = down_base(here, hidden, hidden_far, down_weight, side, width - side)
+        right, *got = tied(right, *got)
         shrink = shrink_down.reshape(slots * rank, -1)
-        out_own = low_out_pairs(at_here, hidden_rows, shrink, mask_out)
+        out_own = low_out_pairs(at_here, got, shrink, mask_out)
         out_got = swap(out_own)
         expand = expand_down.reshape(slots * rank, width)
-        parts = ways.deliver(add_delta(base, out_own, out_got, pick, expand, shards))
-        return sum(part.astype(F32) for part in parts).astype(BF)
+        return ways.deliver(add_delta([left, right], out_own, out_got, pick, expand, shards))
 
     if most <= USUAL:
-        return finish(most)
-    return lax.cond(highest[0] < USUAL, lambda: finish(USUAL), lambda: finish(most))
+        parts = partial_sums(most)
+    else:
+        parts = lax.cond(
+            highest[0] < USUAL, lambda: partial_sums(USUAL), lambda: partial_sums(most)
+        )
+    return sum(part.astype(F32) for part in parts).astype(BF)
 
 
 def solution(mesh):

time: 94.7 us -> 88.5 us (0.935)
  starting transfers between devices: 44.7 us -> 34.4 us
  waiting for transfers between devices: 10.7 us -> 14.6 us
  Pallas kernels: 32.9 us -> 29.1 us
  local copies, waits for them, and re-layouts: 1.37 us -> 4.4 us
    ppermute x21 -> x7, starting transfers between devices: 31.7 us -> 11.2 us  [deliver(): got[back] = lax.ppermute(blocks[b], 'ff', self.back(a, c))]
    ppermute x0 -> x8, starting transfers between devices: none -> 10.4 us  [the longest x6 9.19 us: slow_steps(): got[-a % self.slow] = lax.ppermute(blocks[a], 'ff', self.back(a, 0))]
    ppermute x0 -> x8, waiting for transfers between devices: none -> 4.67 us  [the longest x6 3.23 us: slow_steps(): got[-a % self.slow] = lax.ppermute(blocks[a], 'ff', self.back(a, 0))]
    unnamed x6 -> x10, local copies, waits for them, and re-layouts: 0.63 us -> 3.66 us
    pallas_call x6 -> x9, Pallas kernels: 17.7 us -> 15.6 us  [the longest x2 8.23 us: down_base(): pl.pallas_call(functools.partial(down_kernel, first), out_shape=jax.Shape...]
    ppermute x21 -> x7, waiting for transfers between devices: 5.76 us -> 3.78 us  [deliver(): got[back] = lax.ppermute(blocks[b], 'ff', self.back(a, c))]
    pallas_call x1, Pallas kernels: 2.66 us -> 1.03 us  [low_in_pairs(): pl.pallas_call(lambda *refs: low_in_kernel(count, *refs), out_shape=(jax....]
    ppermute x5, waiting for transfers between devices: 1.49 us -> 3.06 us  [per_device(): swap = lambda a: lax.ppermute(a, 'var', [(0, 1), (1, 0)])]
  transfers between devices with their start and end apart: 34 -> 28, of which waited for: 11 -> 12; matrix products, arithmetic and copies ran while one was open for 4% -> 4% of each run, Pallas kernels for 18% -> 27%
where the time goes in v4:
time: 88.5 us; the launch traced here: 88.3 us
  starting transfers between devices  34.4 us (39%)
  Pallas kernels  29.1 us (33%)
  waiting for transfers between devices  14.6 us (16%)
  local copies, waits for them, and re-layouts  4.4 us (5%)
  other arithmetic  3.54 us (4%)
  between operations  1.56 us (2%)
    pallas_call x2, Pallas kernels, base_half(): pl.pallas_call(base_kernel, out_shape=jax.ShapeDtypeStruct((2, rows, half...  12.5 us
    ppermute x7, starting transfers between devices, deliver(): got[back] = lax.ppermute(blocks[b], 'ff', self.back(a, c))  11.2 us
    ppermute x6, starting transfers between devices, slow_steps(): got[-a % self.slow] = lax.ppermute(blocks[a], 'ff', self.back(a, 0))  9.19 us
    pallas_call x2, Pallas kernels, down_base(): pl.pallas_call(functools.partial(down_kernel, first), out_shape=jax.Shape...  8.23 us
    ppermute x3, starting transfers between devices, gather(): lax.ppermute(block, 'ff', self.back(-a, 0))  6.96 us
    ppermute x4, starting transfers between devices, gather(): lax.ppermute(got[a * self.fast], 'ff', self.back(0, -c))  4.06 us
    ppermute x7, waiting for transfers between devices, deliver(): got[back] = lax.ppermute(blocks[b], 'ff', self.back(a, c))  3.78 us
    unnamed x10, local copies, waits for them, and re-layouts  3.66 us
  transfers between devices with their start and end apart: 28, of which 12 were waited for; matrix products, arithmetic and copies ran while one was open for 4% of the time, Pallas kernels for 27%

profile of v4, /device:TPU:0, one launch (start us, length us, event | category | flops | bytes accessed | tf_op | source)
XLA Modules:
  0.0 88.3 jit_solution(5895157034632941995)
XLA Ops:
  0.0 3.0 %collective-permute-start.36 = (bf16[8,4096]{1,0:T(8,128)(2,1)}, bf16[8,4096]{1,0:T(8,128)(2,1)S(1)}, u32[]{:S(2)}, u32[]{:S(2)}) collective-permute-start(bf16[8,4096]{1,0:T(8,128)(2,1)} %x_ref.1), channel_id=1, source_target_pairs={{0,4},{2,6},{4,8},{6,10},{8,12},{10,14},{12,0},{14,2},{1,5},{3,7},... | collective-permute-start | bytes 196616 | tf_op jit(solution)/shard_map/ppermute | solution.py:70
  3.0 2.6 %collective-permute-start.37 = (bf16[8,4096]{1,0:T(8,128)(2,1)}, bf16[8,4096]{1,0:T(8,128)(2,1)S(1)}, u32[]{:S(2)}, u32[]{:S(2)}) collective-permute-start(bf16[8,4096]{1,0:T(8,128)(2,1)} %x_ref.1), channel_id=1, source_target_pairs={{0,8},{2,10},{4,12},{6,14},{8,0},{10,2},{12,4},{14,6},{1,9},{3,11}... | collective-permute-start | bytes 196616 | tf_op jit(solution)/shard_map/ppermute | solution.py:70
  7.0 1.5 %collective-permute-start.41 = (bf16[8,4096]{1,0:T(8,128)(2,1)}, bf16[8,4096]{1,0:T(8,128)(2,1)S(1)}, u32[]{:S(2)}, u32[]{:S(2)}) collective-permute-start(bf16[8,4096]{1,0:T(8,128)(2,1)} %x_ref.1), channel_id=1, source_target_pairs={{0,2},{2,0},{4,6},{6,4},{8,10},{10,8},{12,14},{14,12},{1,3},{3,1},... | collective-permute-start | bytes 196616 | tf_op jit(solution)/shard_map/ppermute | solution.py:73
  9.1 1.6 %copy-done = bf16[4,2,8,16384]{3,2,1,0:T(8,128)(2,1)S(1)} copy-done((bf16[4,2,8,16384]{3,2,1,0:T(8,128)(2,1)S(1)}, bf16[4,2,8,16384]{3,2,1,0:T(8,128)(2,1)}, u32[]{:S(2)}) %copy-start) | copy-done | bytes 2097176
  12.7 2.2 %shard_map.100 = (bf16[8,4096]{1,0:T(8,128)(2,1)S(1)}, bf16[64,8192]{1,0:T(8,128)(2,1)}, bf16[64,8192]{1,0:T(8,128)(2,1)S(1)}, bf16[128,4096]{1,0:T(8,128)(2,1)S(1)}) custom-call(s32[8]{0:T(128)S(1)} %multiply_add_fusion.4.here_ref, s32[8]{0:T(128)S(1)} %get-tuple-element.560.there_ref, bf16[8,4096]{1,0:T(8,128)(2,1)S(1)} %copy-done.2, ...), custom_call_target="tpu_custom_call" | custom-call | bytes 6291456 | tf_op jit(solution)/shard_map/pallas_call | solution.py:121
  16.7 1.5 %collective-permute-start.39 = (s32[1]{0:T(128)}, s32[1]{0:T(128)}, u32[]{:S(2)}, u32[]{:S(2)}) collective-permute-start(s32[1]{0:T(128)} %bitcast.9), channel_id=1, source_target_pairs={{0,16},{16,0},{1,17},{17,1},{2,18},{18,2},{3,19},{19,3},{4,20},{20... | collective-permute-start | bytes 20 | tf_op jit(solution)/shard_map/ppermute | solution.py:463
  18.9 1.5 %collective-permute-start.42 = (bf16[8,4096]{1,0:T(8,128)(2,1)S(1)}, bf16[8,4096]{1,0:T(8,128)(2,1)S(1)}, u32[]{:S(2)}, u32[]{:S(2)}) collective-permute-start(bf16[8,4096]{1,0:T(8,128)(2,1)S(1)} %collective-permute-done.36.refs_4_), channel_id=1, source_target_pairs={{0,2},{2,0},{4,6},{6,4},{8,10},{10,8},{12,14},{14,12},{1,3},{3,1},... | collective-permute-start | bytes 196616 | tf_op jit(solution)/shard_map/ppermute | solution.py:73
  23.3 1.4 %collective-permute-done.42.refs_5_ = bf16[8,4096]{1,0:T(8,128)(2,1)S(1)} collective-permute-done((bf16[8,4096]{1,0:T(8,128)(2,1)S(1)}, bf16[8,4096]{1,0:T(8,128)(2,1)S(1)}, u32[]{:S(2)}, u32[]{:S(2)}) %collective-permute-start.42) | collective-permute-done | bytes 65568 | tf_op jit(solution)/shard_map/ppermute | solution.py:73
  27.9 59.7 %conditional.2 = (bf16[8,4096]{1,0:T(8,128)(2,1)S(1)}, f32[8,4096]{1,0:T(8,128)S(1)}, f32[8,4096]{1,0:T(8,128)S(1)}, f32[8,4096]{1,0:T(8,128)S(1)}, f32[8,4096]{...) conditional(s32[]{:T(128)} %bitcast.10, (s32[64]{0:T(128)S(1)}, ...), branch_computations={%region_4.9_spmd, %region_9.14_spmd} | conditional | flops 3590742272 | bytes 88115232
  28.3 2.2 %branch_1_fun.10 = (bf16[128,1024]{1,0:T(8,128)(2,1)S(1)}, bf16[128,1024]{1,0:T(8,128)(2,1)S(1)}) custom-call(f32[64,128]{1,0:T(8,128)S(1)} %get-tuple-element.404.own_ref, f32[64,128]{1,0:T(8,128)S(1)} %get-tuple-element.405.got_ref, bf16[16,64]{1,0:T(8,128)(2,1)S(1)} %fusion.14.pick_ref.refs_4_, bf16[2,2,128,64]{3,2,1,0:T(8,128)(2,1)S(1)} %get-tuple-element.416.cols_ref, ...), custom_call_target="tpu_custom_call" | custom-call | flops 67108864 | bytes 2621440 | tf_op jit(solution)/shard_map/cond/branch_1_fun/pallas_call | solution.py:192
  31.6 6.2 %branch_1_fun.11 = bf16[2,64,1024]{2,1,0:T(8,128)(2,1)S(1)} custom-call(s32[1]{0:T(128)S(6)} %sub.103.side_ref, bf16[64,4096]{1,0:T(8,128)(2,1)S(1)} %get-tuple-element.431.x_ref, bf16[4096,2048]{1,0:T(8,128)(2,1)} %get-tuple-element.423.gate_ref, bf16[4096,2048]{1,0:T(8,128)(2,1)} %get-tuple-element.424.up_ref), custom_call_target="tpu_custom_call" | custom-call | flops 1073741824 | bytes 17301504 | tf_op jit(solution)/shard_map/cond/branch_1_fun/pallas_call | solution.py:224
  40.1 2.8 %collective-permute-start.22 = (bf16[64,1024]{1,0:T(8,128)(2,1)S(1)}, bf16[64,1024]{1,0:T(8,128)(2,1)S(1)}, u32[]{:S(2)}, u32[]{:S(2)}) collective-permute-start(bf16[64,1024]{1,0:T(8,128)(2,1)S(1)} %get-tuple-element.443), channel_id=1, source_target_pairs={{0,12},{2,14},{4,0},{6,2},{8,4},{10,6},{12,8},{14,10},{1,13},{3,15... | collective-permute-start | bytes 393224 | tf_op jit(solution)/shard_map/cond/branch_1_fun/ppermute | solution.py:95
  43.0 6.2 %branch_1_fun.13.own_ref = f32[2,64,1024]{2,1,0:T(8,128)S(1)} custom-call(s32[1]{0:T(128)} %get-tuple-element.402.side_ref.core_ref, bf16[64,4096]{1,0:T(8,128)(2,1)S(1)} %get-tuple-element.431.x_ref, bf16[4096,2048]{1,0:T(8,128)(2,1)} %get-tuple-element.423.gate_ref, bf16[4096,2048]{1,0:T(8,128)(2,1)} %get-tuple-element.424.up_ref), custom_call_target="tpu_custom_call" | custom-call | flops 1073741824 | bytes 17301504 | tf_op jit(solution)/shard_map/cond/branch_1_fun/pallas_call | solution.py:224
  49.3 3.2 %collective-permute-done.21.refs_2_ = bf16[64,1024]{1,0:T(8,128)(2,1)S(1)} collective-permute-done((bf16[64,1024]{1,0:T(8,128)(2,1)S(1)}, bf16[64,1024]{1,0:T(8,128)(2,1)S(1)}, u32[]{:S(2)}, u32[]{:S(2)}) %collective-permute-start.21) | collective-permute-done | bytes 131104 | tf_op jit(solution)/shard_map/cond/branch_1_fun/ppermute | solution.py:95
  52.5 1.6 %branch_1_fun.14 = (bf16[64,1024]{1,0:T(8,128)(2,1)S(1)}, bf16[64,1024]{1,0:T(8,128)(2,1)S(1)}, bf16[64,1024]{1,0:T(8,128)(2,1)S(1)}) custom-call(f32[2,64,1024]{2,1,0:T(8,128)S(1)} %branch_1_fun.13.own_ref, bf16[2,64,1024]{2,1,0:T(8,128)(2,1)S(1)} %collective-permute-done.19.got_ref, bf16[128,256]{1,0:T(8,128)(2,1)S(1)} %fusion.11.place_ref, ...), custom_call_target="tpu_custom_call" | custom-call | flops 83886080 | bytes 1572864 | tf_op jit(solution)/shard_map/cond/branch_1_fun/pallas_call | solution.py:263
  55.6 4.2 %branch_1_fun.15.refs_0_ = f32[64,2048]{1,0:T(8,128)S(1)} custom-call(s32[1]{0:T(128)} %get-tuple-element.402.side_ref.core_ref, bf16[64,1024]{1,0:T(8,128)(2,1)S(1)} %get-tuple-element.454.near_ref, bf16[64,1024]{1,0:T(8,128)(2,1)S(1)} %collective-permute-done.23.far_ref, bf16[2048,4096]{1,0:T(8,128)(2,1)} %get-tuple-element.445.weight_ref), custom_call_target="tpu_custom_call" | custom-call | flops 536870912 | bytes 8912896 | tf_op jit(solution)/shard_map/cond/branch_1_fun/pallas_call | solution.py:324
  60.2 2.9 %collective-permute-start.25 = (bf16[32,1024]{1,0:T(8,128)(2,1)S(1)}, bf16[32,1024]{1,0:T(8,128)(2,1)S(1)}, u32[]{:S(2)}, u32[]{:S(2)}) collective-permute-start(bf16[32,1024]{1,0:T(8,128)(2,1)S(1)} %get-tuple-element.456), channel_id=1, source_target_pairs={{0,4},{2,6},{4,8},{6,10},{8,12},{10,14},{12,0},{14,2},{1,5},{3,7},... | collective-permute-start | bytes 196616 | tf_op jit(solution)/shard_map/cond/branch_1_fun/ppermute | solution.py:95
  63.3 2.1 %collective-permute-start.27 = (bf16[32,1024]{1,0:T(8,128)(2,1)S(1)}, bf16[32,1024]{1,0:T(8,128)(2,1)S(1)}, u32[]{:S(2)}, u32[]{:S(2)}) collective-permute-start(bf16[32,1024]{1,0:T(8,128)(2,1)S(1)} %get-tuple-element.458), channel_id=1, source_target_pairs={{0,12},{2,14},{4,0},{6,2},{8,4},{10,6},{12,8},{14,10},{1,13},{3,15... | collective-permute-start | bytes 196616 | tf_op jit(solution)/shard_map/cond/branch_1_fun/ppermute | solution.py:95
  65.6 4.1 %branch_1_fun.17.refs_1_ = f32[64,2048]{1,0:T(8,128)S(1)} custom-call(s32[1]{0:T(128)} %get-tuple-element.402.side_ref.core_ref, bf16[64,1024]{1,0:T(8,128)(2,1)S(1)} %get-tuple-element.454.near_ref, bf16[64,1024]{1,0:T(8,128)(2,1)S(1)} %collective-permute-done.23.far_ref, bf16[2048,4096]{1,0:T(8,128)(2,1)} %get-tuple-element.445.weight_ref), custom_call_target="tpu_custom_call" | custom-call | flops 536870912 | bytes 8912896 | tf_op jit(solution)/shard_map/cond/branch_1_fun/pallas_call | solution.py:324
  72.9 1.4 %collective-permute-start.30 = (bf16[8,4096]{1,0:T(8,128)(2,1)S(1)}, bf16[8,4096]{1,0:T(8,128)(2,1)S(1)}, u32[]{:S(2)}, u32[]{:S(2)}) collective-permute-start(bf16[8,4096]{1,0:T(8,128)(2,1)S(1)} %get-tuple-element.470), channel_id=1, source_target_pairs={{0,4},{2,6},{4,8},{6,10},{8,12},{10,14},{12,0},{14,2},{1,5},{3,7},... | collective-permute-start | bytes 196616 | tf_op jit(solution)/shard_map/cond/branch_1_fun/ppermute | solution.py:89
  75.2 3.0 %collective-permute-start.32 = (bf16[8,4096]{1,0:T(8,128)(2,1)S(1)}, bf16[8,4096]{1,0:T(8,128)(2,1)S(1)}, u32[]{:S(2)}, u32[]{:S(2)}) collective-permute-start(bf16[8,4096]{1,0:T(8,128)(2,1)S(1)} %get-tuple-element.472), channel_id=1, source_target_pairs={{0,8},{2,10},{4,12},{6,14},{8,0},{10,2},{12,4},{14,6},{1,9},{3,11}... | collective-permute-start | bytes 196616 | tf_op jit(solution)/shard_map/cond/branch_1_fun/ppermute | solution.py:89
  78.2 3.7 %collective-permute-start.34 = (bf16[8,4096]{1,0:T(8,128)(2,1)S(1)}, bf16[8,4096]{1,0:T(8,128)(2,1)S(1)}, u32[]{:S(2)}, u32[]{:S(2)}) collective-permute-start(bf16[8,4096]{1,0:T(8,128)(2,1)S(1)} %get-tuple-element.474), channel_id=1, source_target_pairs={{0,12},{2,14},{4,0},{6,2},{8,4},{10,6},{12,8},{14,10},{1,13},{3,15... | collective-permute-start | bytes 196616 | tf_op jit(solution)/shard_map/cond/branch_1_fun/ppermute | solution.py:89
  81.9 1.5 %collective-permute-start.35 = (bf16[8,4096]{1,0:T(8,128)(2,1)S(1)}, bf16[8,4096]{1,0:T(8,128)(2,1)S(1)}, u32[]{:S(2)}, u32[]{:S(2)}) collective-permute-start(bf16[8,4096]{1,0:T(8,128)(2,1)S(1)} %get-tuple-element.475), channel_id=1, source_target_pairs={{0,14},{2,12},{4,2},{6,0},{8,6},{10,4},{12,10},{14,8},{1,15},{3,13... | collective-permute-start | bytes 196616 | tf_op jit(solution)/shard_map/cond/branch_1_fun/ppermute | solution.py:89
  84.6 2.3 %collective-permute-done.33 = bf16[8,4096]{1,0:T(8,128)(2,1)S(1)} collective-permute-done((bf16[8,4096]{1,0:T(8,128)(2,1)S(1)}, bf16[8,4096]{1,0:T(8,128)(2,1)S(1)}, u32[]{:S(2)}, u32[]{:S(2)}) %collective-permute-start.33) | collective-permute-done | bytes 65568 | tf_op jit(solution)/shard_map/cond/branch_1_fun/ppermute | solution.py:89
  (119 shorter events, 23.3 us)
Async XLA Ops:
  0.0 14.9 %collective-permute-start.36 = (bf16[8,4096]{1,0:T(8,128)(2,1)}, bf16[8,4096]{1,0:T(8,128)(2,1)S(1)}, u32[]{:S(2)}, u32[]{:S(2)}) collective-permute-start(bf16[8,4096]{1,0:T(8,128)(2,1)} %x_ref.1), channel_id=1, source_target_pairs={{0,4},{2,6},{4,8},{6,10},{8,12},{10,14},{12,0},{14,2},{1,5},{3,7},... | collective-permute-start | bytes 196616 | tf_op jit(solution)/shard_map/ppermute | solution.py:70
  3.0 11.9 %collective-permute-start.37 = (bf16[8,4096]{1,0:T(8,128)(2,1)}, bf16[8,4096]{1,0:T(8,128)(2,1)S(1)}, u32[]{:S(2)}, u32[]{:S(2)}) collective-permute-start(bf16[8,4096]{1,0:T(8,128)(2,1)} %x_ref.1), channel_id=1, source_target_pairs={{0,8},{2,10},{4,12},{6,14},{8,0},{10,2},{12,4},{14,6},{1,9},{3,11}... | collective-permute-start | bytes 196616 | tf_op jit(solution)/shard_map/ppermute | solution.py:70
  5.6 9.3 %collective-permute-start.38 = (bf16[8,4096]{1,0:T(8,128)(2,1)}, bf16[8,4096]{1,0:T(8,128)(2,1)S(1)}, u32[]{:S(2)}, u32[]{:S(2)}) collective-permute-start(bf16[8,4096]{1,0:T(8,128)(2,1)} %x_ref.1), channel_id=1, source_target_pairs={{0,12},{2,14},{4,0},{6,2},{8,4},{10,6},{12,8},{14,10},{1,13},{3,15... | collective-permute-start | bytes 196616 | tf_op jit(solution)/shard_map/ppermute | solution.py:70
  7.0 16.3 %collective-permute-start.41 = (bf16[8,4096]{1,0:T(8,128)(2,1)}, bf16[8,4096]{1,0:T(8,128)(2,1)S(1)}, u32[]{:S(2)}, u32[]{:S(2)}) collective-permute-start(bf16[8,4096]{1,0:T(8,128)(2,1)} %x_ref.1), channel_id=1, source_target_pairs={{0,2},{2,0},{4,6},{6,4},{8,10},{10,8},{12,14},{14,12},{1,3},{3,1},... | collective-permute-start | bytes 196616 | tf_op jit(solution)/shard_map/ppermute | solution.py:73
  15.0 12.8 %collective-permute-start.45 = (bf16[64,8192]{1,0:T(8,128)(2,1)S(1)}, bf16[64,8192]{1,0:T(8,128)(2,1)}, u32[]{:S(2)}, u32[]{:S(2)}) collective-permute-start(bf16[64,8192]{1,0:T(8,128)(2,1)S(1)} %get-tuple-element.510), channel_id=1, source_target_pairs={{0,1},{1,0},{2,3},{3,2},{4,5},{5,4},{6,7},{7,6},{8,9},{9,8},{10,11... | collective-permute-start | bytes 3145736 | tf_op jit(solution)/shard_map/ppermute | solution.py:436
  18.4 4.9 %collective-permute-start.40 = (bf16[8,4096]{1,0:T(8,128)(2,1)S(1)}, bf16[8,4096]{1,0:T(8,128)(2,1)S(1)}, u32[]{:S(2)}, u32[]{:S(2)}) collective-permute-start(bf16[8,4096]{1,0:T(8,128)(2,1)S(1)} %collective-permute-done.38.refs_8_), channel_id=1, source_target_pairs={{0,2},{2,0},{4,6},{6,4},{8,10},{10,8},{12,14},{14,12},{1,3},{3,1},... | collective-permute-start | bytes 196616 | tf_op jit(solution)/shard_map/ppermute | solution.py:73
  18.9 5.8 %collective-permute-start.42 = (bf16[8,4096]{1,0:T(8,128)(2,1)S(1)}, bf16[8,4096]{1,0:T(8,128)(2,1)S(1)}, u32[]{:S(2)}, u32[]{:S(2)}) collective-permute-start(bf16[8,4096]{1,0:T(8,128)(2,1)S(1)} %collective-permute-done.36.refs_4_), channel_id=1, source_target_pairs={{0,2},{2,0},{4,6},{6,4},{8,10},{10,8},{12,14},{14,12},{1,3},{3,1},... | collective-permute-start | bytes 196616 | tf_op jit(solution)/shard_map/ppermute | solution.py:73
  20.4 5.0 %collective-permute-start.43 = (bf16[8,4096]{1,0:T(8,128)(2,1)S(1)}, bf16[8,4096]{1,0:T(8,128)(2,1)S(1)}, u32[]{:S(2)}, u32[]{:S(2)}) collective-permute-start(bf16[8,4096]{1,0:T(8,128)(2,1)S(1)} %collective-permute-done.37.refs_6_), channel_id=1, source_target_pairs={{0,2},{2,0},{4,6},{6,4},{8,10},{10,8},{12,14},{14,12},{1,3},{3,1},... | collective-permute-start | bytes 196616 | tf_op jit(solution)/shard_map/ppermute | solution.py:73
  30.5 8.4 %collective-permute-start.18 = (bf16[128,1024]{1,0:T(8,128)(2,1)S(1)}, bf16[128,1024]{1,0:T(8,128)(2,1)S(1)}, u32[]{:S(2)}, u32[]{:S(2)}) collective-permute-start(bf16[128,1024]{1,0:T(8,128)(2,1)S(1)} %get-tuple-element.425), channel_id=1, source_target_pairs={{0,2},{2,0},{4,6},{6,4},{8,10},{10,8},{12,14},{14,12},{1,3},{3,1},... | collective-permute-start | bytes 786440 | tf_op jit(solution)/shard_map/cond/branch_1_fun/ppermute | solution.py:509
  39.0 13.5 %collective-permute-start.19 = (bf16[2,64,1024]{2,1,0:T(8,128)(2,1)S(1)}, bf16[2,64,1024]{2,1,0:T(8,128)(2,1)S(1)}, u32[]{:S(2)}, u32[]{:S(2)}) collective-permute-start(bf16[2,64,1024]{2,1,0:T(8,128)(2,1)S(1)} %branch_1_fun.11), channel_id=1, source_target_pairs={{0,1},{1,0},{2,3},{3,2},{4,5},{5,4},{6,7},{7,6},{8,9},{9,8},{10,11... | collective-permute-start | bytes 786440 | tf_op jit(solution)/shard_map/cond/branch_1_fun/ppermute | solution.py:436
  39.0 10.2 %collective-permute-start.20 = (bf16[64,1024]{1,0:T(8,128)(2,1)S(1)}, bf16[64,1024]{1,0:T(8,128)(2,1)S(1)}, u32[]{:S(2)}, u32[]{:S(2)}) collective-permute-start(bf16[64,1024]{1,0:T(8,128)(2,1)S(1)} %get-tuple-element.441), channel_id=1, source_target_pairs={{0,4},{2,6},{4,8},{6,10},{8,12},{10,14},{12,0},{14,2},{1,5},{3,7},... | collective-permute-start | bytes 393224 | tf_op jit(solution)/shard_map/cond/branch_1_fun/ppermute | solution.py:95
  39.8 12.7 %collective-permute-start.21 = (bf16[64,1024]{1,0:T(8,128)(2,1)S(1)}, bf16[64,1024]{1,0:T(8,128)(2,1)S(1)}, u32[]{:S(2)}, u32[]{:S(2)}) collective-permute-start(bf16[64,1024]{1,0:T(8,128)(2,1)S(1)} %get-tuple-element.442), channel_id=1, source_target_pairs={{0,8},{2,10},{4,12},{6,14},{8,0},{10,2},{12,4},{14,6},{1,9},{3,11}... | collective-permute-start | bytes 393224 | tf_op jit(solution)/shard_map/cond/branch_1_fun/ppermute | solution.py:95
  40.1 12.4 %collective-permute-start.22 = (bf16[64,1024]{1,0:T(8,128)(2,1)S(1)}, bf16[64,1024]{1,0:T(8,128)(2,1)S(1)}, u32[]{:S(2)}, u32[]{:S(2)}) collective-permute-start(bf16[64,1024]{1,0:T(8,128)(2,1)S(1)} %get-tuple-element.443), channel_id=1, source_target_pairs={{0,12},{2,14},{4,0},{6,2},{8,4},{10,6},{12,8},{14,10},{1,13},{3,15... | collective-permute-start | bytes 393224 | tf_op jit(solution)/shard_map/cond/branch_1_fun/ppermute | solution.py:95
  54.2 5.9 %collective-permute-start.24 = (bf16[64,1024]{1,0:T(8,128)(2,1)S(1)}, bf16[64,1024]{1,0:T(8,128)(2,1)S(1)}, u32[]{:S(2)}, u32[]{:S(2)}) collective-permute-start(bf16[64,1024]{1,0:T(8,128)(2,1)S(1)} %get-tuple-element.446), channel_id=1, source_target_pairs={{0,2},{2,0},{4,6},{6,4},{8,10},{10,8},{12,14},{14,12},{1,3},{3,1},... | collective-permute-start | bytes 393224 | tf_op jit(solution)/shard_map/cond/branch_1_fun/ppermute | solution.py:525
  60.2 9.5 %collective-permute-start.25 = (bf16[32,1024]{1,0:T(8,128)(2,1)S(1)}, bf16[32,1024]{1,0:T(8,128)(2,1)S(1)}, u32[]{:S(2)}, u32[]{:S(2)}) collective-permute-start(bf16[32,1024]{1,0:T(8,128)(2,1)S(1)} %get-tuple-element.456), channel_id=1, source_target_pairs={{0,4},{2,6},{4,8},{6,10},{8,12},{10,14},{12,0},{14,2},{1,5},{3,7},... | collective-permute-start | bytes 196616 | tf_op jit(solution)/shard_map/cond/branch_1_fun/ppermute | solution.py:95
  63.0 6.6 %collective-permute-start.26 = (bf16[32,1024]{1,0:T(8,128)(2,1)S(1)}, bf16[32,1024]{1,0:T(8,128)(2,1)S(1)}, u32[]{:S(2)}, u32[]{:S(2)}) collective-permute-start(bf16[32,1024]{1,0:T(8,128)(2,1)S(1)} %get-tuple-element.457), channel_id=1, source_target_pairs={{0,8},{2,10},{4,12},{6,14},{8,0},{10,2},{12,4},{14,6},{1,9},{3,11}... | collective-permute-start | bytes 196616 | tf_op jit(solution)/shard_map/cond/branch_1_fun/ppermute | solution.py:95
  63.3 6.3 %collective-permute-start.27 = (bf16[32,1024]{1,0:T(8,128)(2,1)S(1)}, bf16[32,1024]{1,0:T(8,128)(2,1)S(1)}, u32[]{:S(2)}, u32[]{:S(2)}) collective-permute-start(bf16[32,1024]{1,0:T(8,128)(2,1)S(1)} %get-tuple-element.458), channel_id=1, source_target_pairs={{0,12},{2,14},{4,0},{6,2},{8,4},{10,6},{12,8},{14,10},{1,13},{3,15... | collective-permute-start | bytes 196616 | tf_op jit(solution)/shard_map/cond/branch_1_fun/ppermute | solution.py:95
  72.2 5.9 %collective-permute-start.29 = (bf16[8,4096]{1,0:T(8,128)(2,1)S(1)}, bf16[8,4096]{1,0:T(8,128)(2,1)S(1)}, u32[]{:S(2)}, u32[]{:S(2)}) collective-permute-start(bf16[8,4096]{1,0:T(8,128)(2,1)S(1)} %get-tuple-element.469), channel_id=1, source_target_pairs={{0,2},{2,0},{4,6},{6,4},{8,10},{10,8},{12,14},{14,12},{1,3},{3,1},... | collective-permute-start | bytes 196616 | tf_op jit(solution)/shard_map/cond/branch_1_fun/ppermute | solution.py:89
  72.9 9.0 %collective-permute-start.30 = (bf16[8,4096]{1,0:T(8,128)(2,1)S(1)}, bf16[8,4096]{1,0:T(8,128)(2,1)S(1)}, u32[]{:S(2)}, u32[]{:S(2)}) collective-permute-start(bf16[8,4096]{1,0:T(8,128)(2,1)S(1)} %get-tuple-element.470), channel_id=1, source_target_pairs={{0,4},{2,6},{4,8},{6,10},{8,12},{10,14},{12,0},{14,2},{1,5},{3,7},... | collective-permute-start | bytes 196616 | tf_op jit(solution)/shard_map/cond/branch_1_fun/ppermute | solution.py:89
  74.2 9.2 %collective-permute-start.31 = (bf16[8,4096]{1,0:T(8,128)(2,1)S(1)}, bf16[8,4096]{1,0:T(8,128)(2,1)S(1)}, u32[]{:S(2)}, u32[]{:S(2)}) collective-permute-start(bf16[8,4096]{1,0:T(8,128)(2,1)S(1)} %get-tuple-element.471), channel_id=1, source_target_pairs={{0,6},{2,4},{4,10},{6,8},{8,14},{10,12},{12,2},{14,0},{1,7},{3,5},... | collective-permute-start | bytes 196616 | tf_op jit(solution)/shard_map/cond/branch_1_fun/ppermute | solution.py:89
  75.2 9.5 %collective-permute-start.32 = (bf16[8,4096]{1,0:T(8,128)(2,1)S(1)}, bf16[8,4096]{1,0:T(8,128)(2,1)S(1)}, u32[]{:S(2)}, u32[]{:S(2)}) collective-permute-start(bf16[8,4096]{1,0:T(8,128)(2,1)S(1)} %get-tuple-element.472), channel_id=1, source_target_pairs={{0,8},{2,10},{4,12},{6,14},{8,0},{10,2},{12,4},{14,6},{1,9},{3,11}... | collective-permute-start | bytes 196616 | tf_op jit(solution)/shard_map/cond/branch_1_fun/ppermute | solution.py:89
  78.2 8.7 %collective-permute-start.33 = (bf16[8,4096]{1,0:T(8,128)(2,1)S(1)}, bf16[8,4096]{1,0:T(8,128)(2,1)S(1)}, u32[]{:S(2)}, u32[]{:S(2)}) collective-permute-start(bf16[8,4096]{1,0:T(8,128)(2,1)S(1)} %get-tuple-element.473), channel_id=1, source_target_pairs={{0,10},{2,8},{4,14},{6,12},{8,2},{10,0},{12,6},{14,4},{1,11},{3,9}... | collective-permute-start | bytes 196616 | tf_op jit(solution)/shard_map/cond/branch_1_fun/ppermute | solution.py:89
  78.2 8.8 %collective-permute-start.34 = (bf16[8,4096]{1,0:T(8,128)(2,1)S(1)}, bf16[8,4096]{1,0:T(8,128)(2,1)S(1)}, u32[]{:S(2)}, u32[]{:S(2)}) collective-permute-start(bf16[8,4096]{1,0:T(8,128)(2,1)S(1)} %get-tuple-element.474), channel_id=1, source_target_pairs={{0,12},{2,14},{4,0},{6,2},{8,4},{10,6},{12,8},{14,10},{1,13},{3,15... | collective-permute-start | bytes 196616 | tf_op jit(solution)/shard_map/cond/branch_1_fun/ppermute | solution.py:89
  81.9 5.4 %collective-permute-start.35 = (bf16[8,4096]{1,0:T(8,128)(2,1)S(1)}, bf16[8,4096]{1,0:T(8,128)(2,1)S(1)}, u32[]{:S(2)}, u32[]{:S(2)}) collective-permute-start(bf16[8,4096]{1,0:T(8,128)(2,1)S(1)} %get-tuple-element.475), channel_id=1, source_target_pairs={{0,14},{2,12},{4,2},{6,0},{8,6},{10,4},{12,10},{14,8},{1,15},{3,13... | collective-permute-start | bytes 196616 | tf_op jit(solution)/shard_map/cond/branch_1_fun/ppermute | solution.py:89
  (9 other events, 31.6 us)

commit v5 on v4

--- a/solution.py
+++ b/solution.py
@@ -25,7 +25,7 @@
 
 
 def params(mib):
-    return pltpu.CompilerParams(vmem_limit_bytes=mib * MIB)
+    return pltpu.CompilerParams(vmem_limit_bytes=int(mib * MIB))
 
 
 def cost(flops, moved):
@@ -46,17 +46,17 @@
         me = lax.axis_index("ff").astype(I32)
         steps = jnp.arange(self.shards, dtype=I32)
         if self.direct:
-            slow = (me // self.fast - steps // self.fast) % self.slow
-            fast = (me % self.fast - steps % self.fast) % self.fast
+            slow = (me // self.fast - steps % self.slow) % self.slow
+            fast = (me % self.fast - steps // self.slow) % self.fast
             self.order = slow * self.fast + fast
         else:
             self.order = steps
 
-    def sent_at(self):
+    def arrival(self):
         steps = jnp.arange(self.shards, dtype=I32)
         if not self.direct:
             return steps
-        return steps % self.fast * self.slow + steps // self.fast
+        return steps % self.slow * self.fast + steps // self.slow
 
     def back(self, a, c):
         S, F = self.slow, self.fast
@@ -65,29 +65,15 @@
     def gather(self, block):
         if not self.direct:
             return list(lax.all_gather(block, "ff"))
-        got = [None] * self.shards
-        for a in range(self.slow):
-            got[a * self.fast] = lax.ppermute(block, "ff", self.back(-a, 0)) if a else block
-        for a in range(self.slow):
-            for c in range(1, self.fast):
-                got[a * self.fast + c] = lax.ppermute(
-                    got[a * self.fast], "ff", self.back(0, -c)
-                )
+        got = [block] + [
+            lax.ppermute(block, "ff", self.back(-a, 0)) for a in range(1, self.slow)
+        ]
+        for c in range(1, self.fast):
+            got += [lax.ppermute(part, "ff", self.back(0, -c)) for part in got[: self.slow]]
         return got
 
     def spread(self, blocks):
         return lax.all_to_all(blocks, "ff", 0, 0, tiled=True)
-
-    def deliver(self, blocks):
-        if not self.direct:
-            return list(self.spread(jnp.stack(blocks)))
-        got = [None] * self.shards
-        got[0] = blocks[0]
-        for b in range(1, self.shards):
-            a, c = b // self.fast, b % self.fast
-            back = (-a) % self.slow * self.fast + (-c) % self.fast
-            got[back] = lax.ppermute(blocks[b], "ff", self.back(a, c))
-        return got
 
     def slow_steps(self, blocks):
         got = [blocks[0]] + [None] * (self.slow - 1)
@@ -107,9 +93,9 @@
             put = out.at[:, pl.ds(b * half, half)]
             copies.append(pltpu.make_async_copy(expand_ref.at[:, columns], put, sems.at[b, side]))
     copies.append(pltpu.make_async_copy(shrink_ref, held_ref, sems.at[sems.shape[0] - 1, 0]))
+    copies.append(pltpu.make_async_copy(x_ref, kept_ref, sems.at[sems.shape[0] - 1, 1]))
     for copy in copies:
         copy.start()
-    kept_ref[...] = x_ref[...]
     for copy in copies:
         copy.wait()
 
@@ -129,11 +115,11 @@
         grid_spec=pltpu.PrefetchScalarGridSpec(
             num_scalar_prefetch=2,
             grid=(1,),
-            in_specs=[fixed(x)] + [pl.BlockSpec(memory_space=pl.ANY)] * 2,
-            out_specs=(fixed(x), fixed(out), fixed(out), fixed(shrink)),
+            in_specs=[pl.BlockSpec(memory_space=pltpu.HBM)] * 3,
+            out_specs=(pl.BlockSpec(memory_space=pl.ANY),) * 4,
             scratch_shapes=[pltpu.SemaphoreType.DMA((shards + 1, 2))],
         ),
-        compiler_params=params(16),
+        compiler_params=params(51.25),
         cost_estimate=cost(0, 2 * (2 * expand.size + 2 * shrink.size)),
     )(at_here, at_there, x, expand, shrink)
 
@@ -172,17 +158,15 @@
 def expand_kernel(fast, own_ref, got_ref, pick_ref, cols_ref, near_ref, far_ref, *out_refs):
     low = (own_ref[...] + got_ref[...]).astype(BF)
     picked = dot(pick_ref[...], low).astype(BF)
-    lhs = [
-        jnp.concatenate([dot(picked, cols_ref[kind, side]) for kind in range(2)], axis=0)
-        for side in range(2)
-    ]
-    lhs = [side.astype(BF) for side in lhs]
-    tall = lhs[0].shape[0]
+    lhs = jnp.concatenate([dot(picked, cols_ref[kind]) for kind in range(2)], axis=0).astype(BF)
+    tall = lhs.shape[0]
     half = out_refs[0].shape[1]
-    for b in range(near_ref.shape[1] // half):
+    count = near_ref.shape[1] // half
+    for b in range(count):
         here = pl.ds(b * half, half)
-        delta = dot(lhs[0], near_ref[:, here]) + dot(lhs[1], far_ref[:, here])
-        out_refs[b % fast][pl.ds(b // fast * tall, tall)] = delta.astype(BF)
+        both = jnp.concatenate([near_ref[:, here], far_ref[:, here]], axis=0)
+        at = b % (count // fast)
+        out_refs[b * fast // count][pl.ds(at * tall, tall)] = dot(lhs, both).astype(BF)
 
 
 def expand_rows(own, got, pick, cols, near, far, shards, fast):
@@ -227,7 +211,7 @@
         grid_spec=pltpu.PrefetchScalarGridSpec(
             num_scalar_prefetch=1,
             grid=(1,),
-            in_specs=[fixed(x), pl.BlockSpec(memory_space=pl.ANY), pl.BlockSpec(memory_space=pl.ANY)],
+            in_specs=[fixed(x)] + [pl.BlockSpec(memory_space=pltpu.HBM)] * 2,
             out_specs=pl.BlockSpec((2, rows, half), lambda n, side: (0, 0, 0)),
             scratch_shapes=[
                 pltpu.VMEM((2, width, half), BF),
@@ -293,19 +277,19 @@
     )(own, got)
 
 
-def down_kernel(first, core_ref, near_ref, far_ref, weight_ref, out_ref, held, sems):
+def down_kernel(core_ref, near_ref, far_ref, weight_ref, *refs):
+    out_refs, held, sems = refs[:-2], refs[-2], refs[-1]
     chunks = sems.shape[1]
     half, width = held.shape[1:]
     block = width // chunks
+    tall = out_refs[0].shape[0]
     copies = []
     for c in range(chunks):
         here = pl.ds(c * block, block)
         for side, at in enumerate((core_ref[0], 1 - core_ref[0])):
             lines = pl.ds(pl.multiple_of(at * half, half), half)
             copy = pltpu.make_async_copy(
-                weight_ref.at[lines, pl.ds(first + c * block, block)],
-                held.at[side, :, here],
-                sems.at[side, c],
+                weight_ref.at[lines, here], held.at[side, :, here], sems.at[side, c]
             )
             copy.start()
             copies.append(copy)
@@ -313,22 +297,24 @@
         here = pl.ds(c * block, block)
         copies[2 * c].wait()
         copies[2 * c + 1].wait()
-        out_ref[:, here] = dot(near_ref[...], held[0, :, here]) + dot(
-            far_ref[...], held[1, :, here]
-        )
-
-
-def down_base(core, near, far, weight, first, width):
+        total = dot(near_ref[...], held[0, :, here]) + dot(far_ref[...], held[1, :, here])
+        for n, out_ref in enumerate(out_refs):
+            out_ref[:, here] = total[n * tall : (n + 1) * tall].astype(out_ref.dtype)
+
+
+def down_base(core, near, far, weight, kinds):
     rows, half = near.shape
+    width = weight.shape[1]
     chunks = max(width // 512, 1)
-    return pl.pallas_call(
-        functools.partial(down_kernel, first),
-        out_shape=jax.ShapeDtypeStruct((rows, width), F32),
+    outs = tuple(jax.ShapeDtypeStruct((rows // len(kinds), width), kind) for kind in kinds)
+    return pl.pallas_call(
+        down_kernel,
+        out_shape=outs,
         grid_spec=pltpu.PrefetchScalarGridSpec(
             num_scalar_prefetch=1,
             grid=(1,),
-            in_specs=[fixed(near), fixed(far), pl.BlockSpec(memory_space=pl.ANY)],
-            out_specs=pl.BlockSpec((rows, width), lambda n, core: (0, 0)),
+            in_specs=[fixed(near), fixed(far), pl.BlockSpec(memory_space=pltpu.HBM)],
+            out_specs=tuple(fixed(out) for out in outs),
             scratch_shapes=[
                 pltpu.VMEM((2, half, width), BF),
                 pltpu.SemaphoreType.DMA((2, chunks)),
@@ -342,7 +328,7 @@
 def low_out_kernel(count, at_ref, mask_ref, *refs):
     parts, shrinks, out_ref = refs[:count], refs[count:-1], refs[-1]
     cap = out_ref.shape[0]
-    blocks = [part[r : r + cap] for part in parts for r in range(0, part.shape[0], cap)]
+    blocks = [part[r : r + cap] for r in range(0, parts[0].shape[0], cap) for part in parts]
     pairs = sum(dot_last(block, shrink[...]) for block, shrink in zip(blocks, shrinks))
     out_ref[...] = jnp.where(mask_ref[...] > 0, pairs, 0.0)
 
@@ -370,33 +356,41 @@
     )(at, mask, *parts, *[shrink] * at.shape[0])
 
 
-def add_kernel(count, *refs):
-    bases = refs[:count]
-    own_ref, got_ref, pick_ref, expand_ref = refs[count : count + 4]
-    out_refs = refs[count + 4 :]
-    low = (own_ref[...] + got_ref[...]).astype(BF)
-    spread = lax.dot_general(
-        pick_ref[...], low, (((0,), (0,)), ((), ())), preferred_element_type=F32
-    ).astype(BF)
-    own_rows = out_refs[0].shape[0]
-    first = 0
-    for base_ref in bases:
-        here = pl.ds(first, base_ref.shape[1])
-        total = base_ref[...] + dot(spread, expand_ref[:, here])
+def add_kernel(owners, *refs):
+    base_refs, refs = refs[:owners], refs[owners:]
+    low_refs, refs = refs[: 2 * owners], refs[2 * owners :]
+    pick_refs, expand_refs, out_refs = refs[:owners], refs[owners : 2 * owners], refs[2 * owners :]
+    spreads = []
+    for n in range(owners):
+        low = (low_refs[2 * n][...] + low_refs[2 * n + 1][...]).astype(BF)
+        spread = lax.dot_general(
+            pick_refs[n][...], low, (((0,), (0,)), ((), ())), preferred_element_type=F32
+        )
+        spreads.append(spread.astype(BF))
+    spread = jnp.concatenate(spreads, axis=1)
+    own_rows, width = out_refs[0].shape
+    block = min(1024, width)
+    for first in range(0, width, block):
+        here = pl.ds(first, block)
+        expand = jnp.concatenate([ref[:, here] for ref in expand_refs], axis=0)
+        total = dot(spread, expand)
+        for base_ref in base_refs:
+            total += base_ref[:, here].astype(F32)
         for b, out_ref in enumerate(out_refs):
             out_ref[:, here] = total[b * own_rows : (b + 1) * own_rows].astype(BF)
-        first += base_ref.shape[1]
-
-
-def add_delta(bases, own, got, pick, expand, count):
-    rows = bases[0].shape[0]
-    depth, width = expand.shape
+
+
+def add_delta(bases, lows, picks, expands, count):
+    rows, width = bases[0].shape
+    depth = expands[0].shape[0]
     return pl.pallas_call(
         functools.partial(add_kernel, len(bases)),
         out_shape=(jax.ShapeDtypeStruct((rows // count, width), BF),) * count,
         compiler_params=params(32),
-        cost_estimate=cost(2 * rows * depth * width, width * (6 * rows + 2 * depth)),
-    )(*bases, own, got, pick, expand)
+        cost_estimate=cost(
+            2 * rows * depth * len(bases) * width, width * (6 * rows + 2 * depth) * len(bases)
+        ),
+    )(*bases, *lows, *picks, *expands)
 
 
 def tied(first, *others):
@@ -443,12 +437,10 @@
         expand_gu.reshape(slots * 2 * half_rank, -1),
         shrink_gu.reshape(slots * 2 * rank, width),
     )
+    far = swap(far)
     if ways.direct:
         token_parts[0] = kept
-        variant_ids, far, *token_parts[:: ways.fast] = tied(
-            variant_ids, far, *token_parts[:: ways.fast]
-        )
-    far = swap(far)
+        variant_ids, token_parts[ways.slow + 1] = tied(variant_ids, token_parts[ways.slow + 1])
 
     ids = variant_ids[:, 0]
     matches = ids[:, None] == jnp.arange(variants, dtype=I32)[None, :]
@@ -468,8 +460,8 @@
     slot_row, place = turned(slot_row), turned(place)
     owner = slot_row // slots
     named = owner[:, None] == order[None, :]
-    block = jnp.sum(jnp.where(named, jnp.arange(shards, dtype=I32)[None, :], 0), axis=1)
-    step = jnp.sum(jnp.where(named, ways.sent_at()[None, :], 0), axis=1)
+    step = jnp.sum(jnp.where(named, jnp.arange(shards, dtype=I32)[None, :], 0), axis=1)
+    arrival = jnp.sum(jnp.where(named, ways.arrival()[None, :], 0), axis=1)
     local = slot_row - me * slots
     kinds = jnp.arange(2, dtype=I32)
     in_cols = jnp.arange(slots * 2 * rank, dtype=I32)
@@ -477,14 +469,11 @@
     rank_at = in_cols % rank
     kind_at = in_cols // rank % 2
     row_at = in_cols // (2 * rank) * (2 * half_rank) + kind_at * half_rank + rank_at % half_rank
-    near_cols = jnp.arange(slots * 2 * half_rank, dtype=I32)
-    hit = row_at[:, None] == near_cols[None, :]
-    side = jnp.stack([core, 1 - core])
-    cols = (
-        hit[None, None]
-        & (kind_at[None, :] == kinds[:, None])[:, None, :, None]
-        & ((rank_at // half_rank)[None, :] == side[:, None])[None, :, :, None]
-    ).astype(BF)
+    depth = slots * 2 * half_rank
+    both_cols = jnp.arange(2 * depth, dtype=I32)
+    wanted = row_at + jnp.where(rank_at // half_rank == core, 0, depth)
+    hit = wanted[:, None] == both_cols[None, :]
+    cols = (hit[None] & (kind_at[None, :] == kinds[:, None])[:, :, None]).astype(BF)
 
     highest, token_parts[-1] = tied(highest, token_parts[-1])
     x, low_own = low_in_pairs(token_parts, shrink_in, mask_in)
@@ -493,7 +482,7 @@
     def partial_sums(cap):
         cells = jnp.arange(shards * cap, dtype=I32)
         send_rows = (cells[:, None] == (step * cap + place)[None, :]).astype(BF)
-        kind_cell = (block * 2 + kinds[:, None]) * cap + place
+        kind_cell = (arrival * 2 + kinds[:, None]) * cap + place
         kind_cells = jnp.arange(2 * shards * cap, dtype=I32)
         place_rows = (kind_cell[:, :, None] == kind_cells).astype(BF).reshape(2 * rows, -1)
         spots = jnp.arange(cap, dtype=I32)
@@ -505,39 +494,57 @@
 
         made = expand_rows(low_own, low_got, pick, cols, near, far, shards, split)
         held, *made = tied(x, *made)
+        expand = expand_down.reshape(slots * rank, width)
         if split == 2:
             beside = lax.ppermute(made[1], "ff", ways.back(0, 1))
             base_there = base_half(there, held, gate_weight, up_weight, half, BF)
-            base_there, beside = tied(base_there, beside)
+            base_there, beside, expand = tied(base_there, beside, expand)
             made = relay(made[0], beside, ways.slow)
             held, *made = tied(held, *made)
             delta = ways.slow_steps(made)
+            expand_beside = lax.ppermute(expand, "ff", ways.back(0, 1))
         else:
             base_there = base_half(there, held, gate_weight, up_weight, half, BF)
-            delta = [ways.spread(made[0].reshape(shards, 2 * cap, half))]
-            delta = [delta[0].reshape(2 * shards * cap, half)]
+            delta = ways.spread(made[0].reshape(shards, 2 * cap, half))
+            delta = [delta.reshape(2 * shards * cap, half)]
         base_got = swap(base_there)
         base_own = base_half(here, held, gate_weight, up_weight, half, F32)
+        if split == 2:
+            base_own, expand_beside = tied(base_own, expand_beside)
         hidden, *sent = hidden_half(base_own, base_got, delta, place_rows, send_rows, split)
         hidden_far = swap(hidden)
-        side = width // 2
+        shrink = shrink_down.reshape(slots * rank, -1)
         if split == 2:
             beside = lax.ppermute(sent[1], "ff", ways.back(0, 1))
-            left = down_base(here, hidden, hidden_far, down_weight, 0, side)
-            left, beside = tied(left, beside)
-            sent = relay(sent[0], beside, ways.slow)
-            hidden, *sent = tied(hidden, *sent)
-            got = ways.slow_steps(sent)
+            base, base_sent = down_base(here, hidden, hidden_far, down_weight, (F32, BF))
+            base_sent, beside = tied(base_sent, beside)
+            base_beside = lax.ppermute(base_sent, "ff", ways.back(0, 1))
+            got = ways.slow_steps(relay(sent[0], beside, ways.slow))
         else:
-            left = down_base(here, hidden, hidden_far, down_weight, 0, side)
+            (base,) = down_base(here, hidden, hidden_far, down_weight, (F32,))
             got = [ways.spread(sent[0].reshape(shards, cap, half)).reshape(shards * cap, half)]
-        right = down_base(here, hidden, hidden_far, down_weight, side, width - side)
-        right, *got = tied(right, *got)
-        shrink = shrink_down.reshape(slots * rank, -1)
+        base, *got = tied(base, *got)
         out_own = low_out_pairs(at_here, got, shrink, mask_out)
         out_got = swap(out_own)
-        expand = expand_down.reshape(slots * rank, width)
-        return ways.deliver(add_delta([left, right], out_own, out_got, pick, expand, shards))
+        if split == 1:
+            parts = add_delta([base], [out_own, out_got], [pick], [expand], shards)
+            return list(ways.spread(jnp.stack(parts)))
+        out_beside = lax.ppermute(out_own, "ff", ways.back(0, 1))
+        across = [
+            (2 * f + v, 2 * g + 1 - v) for f, g in ways.back(0, 1) for v in range(2)
+        ]
+        out_across = lax.ppermute(out_own, ("ff", "var"), across)
+        near_rows = rows // 2
+        next_owner = order[ways.slow]
+        next_pick = (spots[:, None] == place[None, :]) & (owner[None, :] == next_owner)
+        parts = add_delta(
+            [base, base_beside],
+            [out_own, out_got, out_beside, out_across],
+            [pick[:, :near_rows], next_pick.astype(BF)[:, :near_rows]],
+            [expand, expand_beside],
+            ways.slow,
+        )
+        return ways.slow_steps(parts)
 
     if most <= USUAL:
         parts = partial_sums(most)

time: 88.5 us -> 119 us (1.34)
  Pallas kernels: 29.1 us -> 59 us
  waiting for transfers between devices: 14.6 us -> 19.2 us
  local copies, waits for them, and re-layouts: 4.4 us -> 2.2 us
  starting transfers between devices: 34.4 us -> 32.2 us
    pallas_call x1, Pallas kernels: 2.16 us -> 33.6 us  [stage(): pl.pallas_call(stage_kernel, out_shape=(jax.ShapeDtypeStruct(x.shape, BF)...]
    ppermute x11 -> x8, starting transfers between devices: 15.3 us -> 7.79 us  [the longest x4 4.07 us: gather(): lax.ppermute(part, 'ff', self.back(0, -c))]
    ppermute x6 -> x9, waiting for transfers between devices: 3.23 us -> 8.9 us  [slow_steps(): got[-a % self.slow] = lax.ppermute(blocks[a], 'ff', self.back(a, 0))]
    ppermute x6 -> x9, starting transfers between devices: 9.19 us -> 14.8 us  [slow_steps(): got[-a % self.slow] = lax.ppermute(blocks[a], 'ff', self.back(a, 0))]
    unnamed x10 -> x6, local copies, waits for them, and re-layouts: 3.66 us -> 0.85 us
    ppermute x1, waiting for transfers between devices: 0.01 us -> 2.06 us  [per_device(): highest = jnp.maximum(highest, lax.ppermute(highest, 'groups', pairs))]
    ppermute x5, waiting for transfers between devices: 3.06 us -> 1.19 us  [per_device(): swap = lambda a: lax.ppermute(a, 'var', [(0, 1), (1, 0)])]
    pallas_call x2 -> x1, Pallas kernels: 8.23 us -> 6.54 us  [down_base(): pl.pallas_call(down_kernel, out_shape=outs, grid_spec=pltpu.PrefetchScala...]
  transfers between devices with their start and end apart: 28 -> 28, of which waited for: 12 -> 12; matrix products, arithmetic and copies ran while one was open for 4% -> 3% of each run, Pallas kernels for 27% -> 46%
where the time goes in v5:
time: 119 us
  Pallas kernels  59 us (50%)
  starting transfers between devices  32.2 us (27%)
  waiting for transfers between devices  19.2 us (16%)
  other arithmetic  3.86 us (3%)
  local copies, waits for them, and re-layouts  2.2 us (2%)
  between operations  1.49 us (1%)
    pallas_call x1, Pallas kernels, stage(): pl.pallas_call(stage_kernel, out_shape=(jax.ShapeDtypeStruct(x.shape, BF)...  33.6 us
    ppermute x9, starting transfers between devices, slow_steps(): got[-a % self.slow] = lax.ppermute(blocks[a], 'ff', self.back(a, 0))  14.8 us
    pallas_call x2, Pallas kernels, base_half(): pl.pallas_call(base_kernel, out_shape=jax.ShapeDtypeStruct((2, rows, half...  12.5 us
    ppermute x9, waiting for transfers between devices, slow_steps(): got[-a % self.slow] = lax.ppermute(blocks[a], 'ff', self.back(a, 0))  8.9 us
    pallas_call x1, Pallas kernels, down_base(): pl.pallas_call(down_kernel, out_shape=outs, grid_spec=pltpu.PrefetchScala...  6.54 us
    ppermute x3, starting transfers between devices, gather(): lax.ppermute(block, 'ff', self.back(-a, 0))  6.06 us
    ppermute x4, starting transfers between devices, gather(): lax.ppermute(part, 'ff', self.back(0, -c))  4.07 us
  transfers between devices with their start and end apart: 28, of which 12 were waited for; matrix products, arithmetic and copies ran while one was open for 3% of the time, Pallas kernels for 46%

profile of v5, /device:TPU:0, one launch (start us, length us, event | category | flops | bytes accessed | tf_op | source)
XLA Modules:
  0.0 118.5 jit_solution(887025632893317661)
XLA Ops:
  0.0 3.0 %collective-permute-start.36 = (bf16[8,4096]{1,0:T(8,128)(2,1)}, bf16[8,4096]{1,0:T(8,128)(2,1)S(1)}, u32[]{:S(2)}, u32[]{:S(2)}) collective-permute-start(bf16[8,4096]{1,0:T(8,128)(2,1)} %x_ref.1), channel_id=1, source_target_pairs={{0,4},{2,6},{4,8},{6,10},{8,12},{10,14},{12,0},{14,2},{1,5},{3,7},... | collective-permute-start | bytes 196616 | tf_op jit(solution)/shard_map/ppermute | solution.py:69
  3.0 2.0 %collective-permute-start.39 = (bf16[8,4096]{1,0:T(8,128)(2,1)}, bf16[8,4096]{1,0:T(8,128)(2,1)S(1)}, u32[]{:S(2)}, u32[]{:S(2)}) collective-permute-start(bf16[8,4096]{1,0:T(8,128)(2,1)} %x_ref.1), channel_id=1, source_target_pairs={{0,12},{2,14},{4,0},{6,2},{8,4},{10,6},{12,8},{14,10},{1,13},{3,15... | collective-permute-start | bytes 196616 | tf_op jit(solution)/shard_map/ppermute | solution.py:69
  6.1 1.5 %collective-permute-start.42 = (bf16[8,4096]{1,0:T(8,128)(2,1)}, bf16[8,4096]{1,0:T(8,128)(2,1)S(1)}, u32[]{:S(2)}, u32[]{:S(2)}) collective-permute-start(bf16[8,4096]{1,0:T(8,128)(2,1)} %x_ref.1), channel_id=1, source_target_pairs={{0,2},{2,0},{4,6},{6,4},{8,10},{10,8},{12,14},{14,12},{1,3},{3,1},... | collective-permute-start | bytes 196616 | tf_op jit(solution)/shard_map/ppermute | solution.py:72
  8.5 33.6 %shard_map.100 = (bf16[8,4096]{1,0:T(8,128)(2,1)S(1)}, bf16[64,8192]{1,0:T(8,128)(2,1)}, bf16[64,8192]{1,0:T(8,128)(2,1)S(1)}, bf16[128,4096]{1,0:T(8,128)(2,1)S(1)}) custom-call(s32[8]{0:T(128)S(1)} %multiply_add_fusion.4.here_ref, s32[8]{0:T(128)S(1)} %get-tuple-element.526.there_ref, bf16[8,4096]{1,0:T(8,128)(2,1)S(1)} %copy-done, ...), custom_call_target="tpu_custom_call" | custom-call | bytes 6291456 | tf_op jit(solution)/shard_map/pallas_call | solution.py:107
  43.0 1.5 %collective-permute-start.40 = (bf16[8,4096]{1,0:T(8,128)(2,1)S(1)}, bf16[8,4096]{1,0:T(8,128)(2,1)S(1)}, u32[]{:S(2)}, u32[]{:S(2)}) collective-permute-start(bf16[8,4096]{1,0:T(8,128)(2,1)S(1)} %collective-permute-done.39.refs_5_), channel_id=1, source_target_pairs={{0,2},{2,0},{4,6},{6,4},{8,10},{10,8},{12,14},{14,12},{1,3},{3,1},... | collective-permute-start | bytes 196616 | tf_op jit(solution)/shard_map/ppermute | solution.py:72
  45.0 2.3 %collective-permute-done.37.refs_7_ = bf16[8,4096]{1,0:T(8,128)(2,1)S(1)} collective-permute-done((bf16[8,4096]{1,0:T(8,128)(2,1)S(1)}, bf16[8,4096]{1,0:T(8,128)(2,1)S(1)}, u32[]{:S(2)}, u32[]{:S(2)}) %collective-permute-start.37) | collective-permute-done | bytes 65568 | tf_op jit(solution)/shard_map/ppermute | solution.py:72
  49.2 1.5 %collective-permute-start.38 = (s32[1]{0:T(128)}, s32[1]{0:T(128)}, u32[]{:S(2)}, u32[]{:S(2)}) collective-permute-start(s32[1]{0:T(128)} %bitcast.11), channel_id=1, source_target_pairs={{0,16},{16,0},{1,17},{17,1},{2,18},{18,2},{3,19},{19,3},{4,20},{20... | collective-permute-start | bytes 20 | tf_op jit(solution)/shard_map/ppermute | solution.py:455
  50.8 2.1 %collective-permute-done.38 = s32[1]{0:T(128)} collective-permute-done((s32[1]{0:T(128)}, s32[1]{0:T(128)}, u32[]{:S(2)}, u32[]{:S(2)}) %collective-permute-start.38) | collective-permute-done | bytes 36 | tf_op jit(solution)/shard_map/ppermute | solution.py:455
  56.6 61.2 %conditional.2 = (bf16[8,4096]{1,0:T(8,128)(2,1)S(1)}, f32[8,4096]{1,0:T(8,128)S(1)}, f32[8,4096]{1,0:T(8,128)S(1)}, f32[8,4096]{1,0:T(8,128)S(1)}) conditional(s32[]{:T(128)} %bitcast.12, (s32[]{:T(128)}, s32[64]{0:T(128)S(1)}, pred[8,8,8]{2,1,0:T(8,128)(4,1)S(1)}, s32[8,8,8]{2,1,0:T(8,128)S(1)}, s32[64]{0:T(128)S(1)}, ...), branch_computations={%region_4.9_spmd, %region_9.14_spmd} | conditional | flops 3590612992 | bytes 90021480
  58.3 2.2 %branch_1_fun.9 = (bf16[128,1024]{1,0:T(8,128)(2,1)S(1)}, bf16[128,1024]{1,0:T(8,128)(2,1)S(1)}) custom-call(f32[64,128]{1,0:T(8,128)S(1)} %get-tuple-element.403.own_ref, f32[64,128]{1,0:T(8,128)S(1)} %get-tuple-element.404.got_ref, bf16[16,64]{1,0:T(8,128)(2,1)S(1)} %get-tuple-element.533.pick_ref, bf16[2,128,128]{2,1,0:T(8,128)(2,1)S(1)} %get-tuple-element.415.cols_ref, ...), custom_call_target="tpu_custom_call" | custom-call | flops 67108864 | bytes 2621440 | tf_op jit(solution)/shard_map/cond/branch_1_fun/pallas_call | solution.py:176
  61.3 6.3 %branch_1_fun.10 = bf16[2,64,1024]{2,1,0:T(8,128)(2,1)S(1)} custom-call(s32[1]{0:T(128)S(6)} %sub.102.side_ref, bf16[64,4096]{1,0:T(8,128)(2,1)S(1)} %get-tuple-element.431.x_ref, bf16[4096,2048]{1,0:T(8,128)(2,1)} %get-tuple-element.422.gate_ref, bf16[4096,2048]{1,0:T(8,128)(2,1)} %get-tuple-element.423.up_ref), custom_call_target="tpu_custom_call" | custom-call | flops 1073741824 | bytes 17301504 | tf_op jit(solution)/shard_map/cond/branch_1_fun/pallas_call | solution.py:208
  69.6 1.6 %collective-permute-start.21 = (bf16[64,1024]{1,0:T(8,128)(2,1)S(1)}, bf16[64,1024]{1,0:T(8,128)(2,1)S(1)}, u32[]{:S(2)}, u32[]{:S(2)}) collective-permute-start(bf16[64,1024]{1,0:T(8,128)(2,1)S(1)} %get-tuple-element.442), channel_id=1, source_target_pairs={{0,4},{2,6},{4,8},{6,10},{8,12},{10,14},{12,0},{14,2},{1,5},{3,7},... | collective-permute-start | bytes 393224 | tf_op jit(solution)/shard_map/cond/branch_1_fun/ppermute | solution.py:81
  71.9 2.8 %collective-permute-start.23 = (bf16[64,1024]{1,0:T(8,128)(2,1)S(1)}, bf16[64,1024]{1,0:T(8,128)(2,1)S(1)}, u32[]{:S(2)}, u32[]{:S(2)}) collective-permute-start(bf16[64,1024]{1,0:T(8,128)(2,1)S(1)} %get-tuple-element.444), channel_id=1, source_target_pairs={{0,12},{2,14},{4,0},{6,2},{8,4},{10,6},{12,8},{14,10},{1,13},{3,15... | collective-permute-start | bytes 393224 | tf_op jit(solution)/shard_map/cond/branch_1_fun/ppermute | solution.py:81
  74.8 6.2 %branch_1_fun.12.own_ref = f32[2,64,1024]{2,1,0:T(8,128)S(1)} custom-call(s32[1]{0:T(128)} %bitcast.5.side_ref.core_ref, bf16[64,4096]{1,0:T(8,128)(2,1)S(1)} %get-tuple-element.431.x_ref, bf16[4096,2048]{1,0:T(8,128)(2,1)} %get-tuple-element.422.gate_ref, bf16[4096,2048]{1,0:T(8,128)(2,1)} %get-tuple-element.423.up_ref), custom_call_target="tpu_custom_call" | custom-call | flops 1073741824 | bytes 17301504 | tf_op jit(solution)/shard_map/cond/branch_1_fun/pallas_call | solution.py:208
  83.1 1.6 %branch_1_fun.13 = (bf16[64,1024]{1,0:T(8,128)(2,1)S(1)}, bf16[64,1024]{1,0:T(8,128)(2,1)S(1)}, bf16[64,1024]{1,0:T(8,128)(2,1)S(1)}) custom-call(f32[2,64,1024]{2,1,0:T(8,128)S(1)} %branch_1_fun.12.own_ref, bf16[2,64,1024]{2,1,0:T(8,128)(2,1)S(1)} %collective-permute-done.20.got_ref, bf16[128,256]{1,0:T(8,128)(2,1)S(1)} %fusion.9.place_ref, ...), custom_call_target="tpu_custom_call" | custom-call | flops 83886080 | bytes 1572864 | tf_op jit(solution)/shard_map/cond/branch_1_fun/pallas_call | solution.py:247
  84.8 1.5 %collective-permute-start.25 = (bf16[64,1024]{1,0:T(8,128)(2,1)S(1)}, bf16[64,1024]{1,0:T(8,128)(2,1)S(1)}, u32[]{:S(2)}, u32[]{:S(2)}) collective-permute-start(bf16[64,1024]{1,0:T(8,128)(2,1)S(1)} %get-tuple-element.450), channel_id=1, source_target_pairs={{0,2},{2,0},{4,6},{6,4},{8,10},{10,8},{12,14},{14,12},{1,3},{3,1},... | collective-permute-start | bytes 393224 | tf_op jit(solution)/shard_map/cond/branch_1_fun/ppermute | solution.py:518
  86.3 6.5 %branch_1_fun.14 = (f32[32,4096]{1,0:T(8,128)S(1)}, bf16[32,4096]{1,0:T(8,128)(2,1)S(1)}) custom-call(s32[1]{0:T(128)} %bitcast.5.side_ref.core_ref, bf16[64,1024]{1,0:T(8,128)(2,1)S(1)} %get-tuple-element.445.near_ref, bf16[64,1024]{1,0:T(8,128)(2,1)S(1)} %collective-permute-done.24.far_ref, bf16[2048,4096]{1,0:T(8,128)(2,1)} %get-tuple-element.446.weight_ref), custom_call_target="tpu_custom_call" | custom-call | flops 1073741824 | bytes 17825792 | tf_op jit(solution)/shard_map/cond/branch_1_fun/pallas_call | solution.py:310
  92.9 3.4 %collective-permute-start.26 = (bf16[32,1024]{1,0:T(8,128)(2,1)S(1)}, bf16[32,1024]{1,0:T(8,128)(2,1)S(1)}, u32[]{:S(2)}, u32[]{:S(2)}) collective-permute-start(bf16[32,1024]{1,0:T(8,128)(2,1)S(1)} %get-tuple-element.453), channel_id=1, source_target_pairs={{0,4},{2,6},{4,8},{6,10},{8,12},{10,14},{12,0},{14,2},{1,5},{3,7},... | collective-permute-start | bytes 196616 | tf_op jit(solution)/shard_map/cond/branch_1_fun/ppermute | solution.py:81
  100.0 2.4 %collective-permute-done.27.refs_2_ = bf16[32,1024]{1,0:T(8,128)(2,1)S(1)} collective-permute-done((bf16[32,1024]{1,0:T(8,128)(2,1)S(1)}, bf16[32,1024]{1,0:T(8,128)(2,1)S(1)}, u32[]{:S(2)}, u32[]{:S(2)}) %collective-permute-start.27) | collective-permute-done | bytes 65568 | tf_op jit(solution)/shard_map/cond/branch_1_fun/ppermute | solution.py:81
  105.7 1.8 %collective-permute-done.31.refs_4_ = f32[16,64]{1,0:T(8,128)S(1)} collective-permute-done((f32[16,64]{1,0:T(8,128)S(1)}, f32[16,64]{1,0:T(8,128)S(1)}, u32[]{:S(2)}, u32[]{:S(2)}) %collective-permute-start.31) | collective-permute-done | bytes 4128 | tf_op jit(solution)/shard_map/cond/branch_1_fun/ppermute | solution.py:532
  108.7 1.4 %collective-permute-start.33 = (bf16[8,4096]{1,0:T(8,128)(2,1)S(1)}, bf16[8,4096]{1,0:T(8,128)(2,1)S(1)}, u32[]{:S(2)}, u32[]{:S(2)}) collective-permute-start(bf16[8,4096]{1,0:T(8,128)(2,1)S(1)} %get-tuple-element.467), channel_id=1, source_target_pairs={{0,4},{2,6},{4,8},{6,10},{8,12},{10,14},{12,0},{14,2},{1,5},{3,7},... | collective-permute-start | bytes 196616 | tf_op jit(solution)/shard_map/cond/branch_1_fun/ppermute | solution.py:81
  110.1 1.6 %collective-permute-start.34 = (bf16[8,4096]{1,0:T(8,128)(2,1)S(1)}, bf16[8,4096]{1,0:T(8,128)(2,1)S(1)}, u32[]{:S(2)}, u32[]{:S(2)}) collective-permute-start(bf16[8,4096]{1,0:T(8,128)(2,1)S(1)} %get-tuple-element.468), channel_id=1, source_target_pairs={{0,8},{2,10},{4,12},{6,14},{8,0},{10,2},{12,4},{14,6},{1,9},{3,11}... | collective-permute-start | bytes 196616 | tf_op jit(solution)/shard_map/cond/branch_1_fun/ppermute | solution.py:81
  112.5 3.0 %collective-permute-done.33 = bf16[8,4096]{1,0:T(8,128)(2,1)S(1)} collective-permute-done((bf16[8,4096]{1,0:T(8,128)(2,1)S(1)}, bf16[8,4096]{1,0:T(8,128)(2,1)S(1)}, u32[]{:S(2)}, u32[]{:S(2)}) %collective-permute-start.33) | collective-permute-done | bytes 65568 | tf_op jit(solution)/shard_map/cond/branch_1_fun/ppermute | solution.py:81
  115.5 2.1 %collective-permute-done.34 = bf16[8,4096]{1,0:T(8,128)(2,1)S(1)} collective-permute-done((bf16[8,4096]{1,0:T(8,128)(2,1)S(1)}, bf16[8,4096]{1,0:T(8,128)(2,1)S(1)}, u32[]{:S(2)}, u32[]{:S(2)}) %collective-permute-start.34) | collective-permute-done | bytes 65568 | tf_op jit(solution)/shard_map/cond/branch_1_fun/ppermute | solution.py:81
  (109 shorter events, 24.5 us)
Async XLA Ops:
  0.0 42.4 %collective-permute-start.36 = (bf16[8,4096]{1,0:T(8,128)(2,1)}, bf16[8,4096]{1,0:T(8,128)(2,1)S(1)}, u32[]{:S(2)}, u32[]{:S(2)}) collective-permute-start(bf16[8,4096]{1,0:T(8,128)(2,1)} %x_ref.1), channel_id=1, source_target_pairs={{0,4},{2,6},{4,8},{6,10},{8,12},{10,14},{12,0},{14,2},{1,5},{3,7},... | collective-permute-start | bytes 196616 | tf_op jit(solution)/shard_map/ppermute | solution.py:69
  3.0 40.0 %collective-permute-start.39 = (bf16[8,4096]{1,0:T(8,128)(2,1)}, bf16[8,4096]{1,0:T(8,128)(2,1)S(1)}, u32[]{:S(2)}, u32[]{:S(2)}) collective-permute-start(bf16[8,4096]{1,0:T(8,128)(2,1)} %x_ref.1), channel_id=1, source_target_pairs={{0,12},{2,14},{4,0},{6,2},{8,4},{10,6},{12,8},{14,10},{1,13},{3,15... | collective-permute-start | bytes 196616 | tf_op jit(solution)/shard_map/ppermute | solution.py:69
  5.1 39.5 %collective-permute-start.41 = (bf16[8,4096]{1,0:T(8,128)(2,1)}, bf16[8,4096]{1,0:T(8,128)(2,1)S(1)}, u32[]{:S(2)}, u32[]{:S(2)}) collective-permute-start(bf16[8,4096]{1,0:T(8,128)(2,1)} %x_ref.1), channel_id=1, source_target_pairs={{0,8},{2,10},{4,12},{6,14},{8,0},{10,2},{12,4},{14,6},{1,9},{3,11}... | collective-permute-start | bytes 196616 | tf_op jit(solution)/shard_map/ppermute | solution.py:69
  6.1 48.1 %collective-permute-start.42 = (bf16[8,4096]{1,0:T(8,128)(2,1)}, bf16[8,4096]{1,0:T(8,128)(2,1)S(1)}, u32[]{:S(2)}, u32[]{:S(2)}) collective-permute-start(bf16[8,4096]{1,0:T(8,128)(2,1)} %x_ref.1), channel_id=1, source_target_pairs={{0,2},{2,0},{4,6},{6,4},{8,10},{10,8},{12,14},{14,12},{1,3},{3,1},... | collective-permute-start | bytes 196616 | tf_op jit(solution)/shard_map/ppermute | solution.py:72
  42.1 14.4 %collective-permute-start.45 = (bf16[64,8192]{1,0:T(8,128)(2,1)S(1)}, bf16[64,8192]{1,0:T(8,128)(2,1)}, u32[]{:S(2)}, u32[]{:S(2)}) collective-permute-start(bf16[64,8192]{1,0:T(8,128)(2,1)S(1)} %get-tuple-element.492), channel_id=1, source_target_pairs={{0,1},{1,0},{2,3},{3,2},{4,5},{5,4},{6,7},{7,6},{8,9},{9,8},{10,11... | collective-permute-start | bytes 3145736 | tf_op jit(solution)/shard_map/ppermute | solution.py:430
  42.5 4.9 %collective-permute-start.37 = (bf16[8,4096]{1,0:T(8,128)(2,1)S(1)}, bf16[8,4096]{1,0:T(8,128)(2,1)S(1)}, u32[]{:S(2)}, u32[]{:S(2)}) collective-permute-start(bf16[8,4096]{1,0:T(8,128)(2,1)S(1)} %collective-permute-done.36.refs_3_), channel_id=1, source_target_pairs={{0,2},{2,0},{4,6},{6,4},{8,10},{10,8},{12,14},{14,12},{1,3},{3,1},... | collective-permute-start | bytes 196616 | tf_op jit(solution)/shard_map/ppermute | solution.py:72
  43.0 11.1 %collective-permute-start.40 = (bf16[8,4096]{1,0:T(8,128)(2,1)S(1)}, bf16[8,4096]{1,0:T(8,128)(2,1)S(1)}, u32[]{:S(2)}, u32[]{:S(2)}) collective-permute-start(bf16[8,4096]{1,0:T(8,128)(2,1)S(1)} %collective-permute-done.39.refs_5_), channel_id=1, source_target_pairs={{0,2},{2,0},{4,6},{6,4},{8,10},{10,8},{12,14},{14,12},{1,3},{3,1},... | collective-permute-start | bytes 196616 | tf_op jit(solution)/shard_map/ppermute | solution.py:72
  44.5 9.6 %collective-permute-start.43 = (bf16[8,4096]{1,0:T(8,128)(2,1)S(1)}, bf16[8,4096]{1,0:T(8,128)(2,1)S(1)}, u32[]{:S(2)}, u32[]{:S(2)}) collective-permute-start(bf16[8,4096]{1,0:T(8,128)(2,1)S(1)} %collective-permute-done.41.refs_4_), channel_id=1, source_target_pairs={{0,2},{2,0},{4,6},{6,4},{8,10},{10,8},{12,14},{14,12},{1,3},{3,1},... | collective-permute-start | bytes 196616 | tf_op jit(solution)/shard_map/ppermute | solution.py:72
  49.2 3.6 %collective-permute-start.38 = (s32[1]{0:T(128)}, s32[1]{0:T(128)}, u32[]{:S(2)}, u32[]{:S(2)}) collective-permute-start(s32[1]{0:T(128)} %bitcast.11), channel_id=1, source_target_pairs={{0,16},{16,0},{1,17},{17,1},{2,18},{18,2},{3,19},{19,3},{4,20},{20... | collective-permute-start | bytes 20 | tf_op jit(solution)/shard_map/ppermute | solution.py:455
  60.5 8.4 %collective-permute-start.18 = (bf16[128,1024]{1,0:T(8,128)(2,1)S(1)}, bf16[128,1024]{1,0:T(8,128)(2,1)S(1)}, u32[]{:S(2)}, u32[]{:S(2)}) collective-permute-start(bf16[128,1024]{1,0:T(8,128)(2,1)S(1)} %get-tuple-element.424), channel_id=1, source_target_pairs={{0,2},{2,0},{4,6},{6,4},{8,10},{10,8},{12,14},{14,12},{1,3},{3,1},... | collective-permute-start | bytes 786440 | tf_op jit(solution)/shard_map/cond/branch_1_fun/ppermute | solution.py:499
  68.9 13.2 %collective-permute-start.19 = (bf16[64,4096]{1,0:T(8,128)(2,1)S(1)}, bf16[64,4096]{1,0:T(8,128)(2,1)S(1)}, u32[]{:S(2)}, u32[]{:S(2)}) collective-permute-start(bf16[64,4096]{1,0:T(8,128)(2,1)S(1)} %bitcast.50), channel_id=1, source_target_pairs={{0,2},{2,0},{4,6},{6,4},{8,10},{10,8},{12,14},{14,12},{1,3},{3,1},... | collective-permute-start | bytes 1572872 | tf_op jit(solution)/shard_map/cond/branch_1_fun/ppermute | solution.py:505
  69.5 13.6 %collective-permute-start.20 = (bf16[2,64,1024]{2,1,0:T(8,128)(2,1)S(1)}, bf16[2,64,1024]{2,1,0:T(8,128)(2,1)S(1)}, u32[]{:S(2)}, u32[]{:S(2)}) collective-permute-start(bf16[2,64,1024]{2,1,0:T(8,128)(2,1)S(1)} %branch_1_fun.10), channel_id=1, source_target_pairs={{0,1},{1,0},{2,3},{3,2},{4,5},{5,4},{6,7},{7,6},{8,9},{9,8},{10,11... | collective-permute-start | bytes 786440 | tf_op jit(solution)/shard_map/cond/branch_1_fun/ppermute | solution.py:430
  69.6 12.5 %collective-permute-start.21 = (bf16[64,1024]{1,0:T(8,128)(2,1)S(1)}, bf16[64,1024]{1,0:T(8,128)(2,1)S(1)}, u32[]{:S(2)}, u32[]{:S(2)}) collective-permute-start(bf16[64,1024]{1,0:T(8,128)(2,1)S(1)} %get-tuple-element.442), channel_id=1, source_target_pairs={{0,4},{2,6},{4,8},{6,10},{8,12},{10,14},{12,0},{14,2},{1,5},{3,7},... | collective-permute-start | bytes 393224 | tf_op jit(solution)/shard_map/cond/branch_1_fun/ppermute | solution.py:81
  71.2 11.9 %collective-permute-start.22 = (bf16[64,1024]{1,0:T(8,128)(2,1)S(1)}, bf16[64,1024]{1,0:T(8,128)(2,1)S(1)}, u32[]{:S(2)}, u32[]{:S(2)}) collective-permute-start(bf16[64,1024]{1,0:T(8,128)(2,1)S(1)} %get-tuple-element.443), channel_id=1, source_target_pairs={{0,8},{2,10},{4,12},{6,14},{8,0},{10,2},{12,4},{14,6},{1,9},{3,11}... | collective-permute-start | bytes 393224 | tf_op jit(solution)/shard_map/cond/branch_1_fun/ppermute | solution.py:81
  71.9 11.2 %collective-permute-start.23 = (bf16[64,1024]{1,0:T(8,128)(2,1)S(1)}, bf16[64,1024]{1,0:T(8,128)(2,1)S(1)}, u32[]{:S(2)}, u32[]{:S(2)}) collective-permute-start(bf16[64,1024]{1,0:T(8,128)(2,1)S(1)} %get-tuple-element.444), channel_id=1, source_target_pairs={{0,12},{2,14},{4,0},{6,2},{8,4},{10,6},{12,8},{14,10},{1,13},{3,15... | collective-permute-start | bytes 393224 | tf_op jit(solution)/shard_map/cond/branch_1_fun/ppermute | solution.py:81
  84.8 8.1 %collective-permute-start.25 = (bf16[64,1024]{1,0:T(8,128)(2,1)S(1)}, bf16[64,1024]{1,0:T(8,128)(2,1)S(1)}, u32[]{:S(2)}, u32[]{:S(2)}) collective-permute-start(bf16[64,1024]{1,0:T(8,128)(2,1)S(1)} %get-tuple-element.450), channel_id=1, source_target_pairs={{0,2},{2,0},{4,6},{6,4},{8,10},{10,8},{12,14},{14,12},{1,3},{3,1},... | collective-permute-start | bytes 393224 | tf_op jit(solution)/shard_map/cond/branch_1_fun/ppermute | solution.py:518
  92.9 7.1 %collective-permute-start.26 = (bf16[32,1024]{1,0:T(8,128)(2,1)S(1)}, bf16[32,1024]{1,0:T(8,128)(2,1)S(1)}, u32[]{:S(2)}, u32[]{:S(2)}) collective-permute-start(bf16[32,1024]{1,0:T(8,128)(2,1)S(1)} %get-tuple-element.453), channel_id=1, source_target_pairs={{0,4},{2,6},{4,8},{6,10},{8,12},{10,14},{12,0},{14,2},{1,5},{3,7},... | collective-permute-start | bytes 196616 | tf_op jit(solution)/shard_map/cond/branch_1_fun/ppermute | solution.py:81
  96.2 6.1 %collective-permute-start.27 = (bf16[32,1024]{1,0:T(8,128)(2,1)S(1)}, bf16[32,1024]{1,0:T(8,128)(2,1)S(1)}, u32[]{:S(2)}, u32[]{:S(2)}) collective-permute-start(bf16[32,1024]{1,0:T(8,128)(2,1)S(1)} %get-tuple-element.454), channel_id=1, source_target_pairs={{0,8},{2,10},{4,12},{6,14},{8,0},{10,2},{12,4},{14,6},{1,9},{3,11}... | collective-permute-start | bytes 196616 | tf_op jit(solution)/shard_map/cond/branch_1_fun/ppermute | solution.py:81
  97.4 5.4 %collective-permute-start.28 = (bf16[32,1024]{1,0:T(8,128)(2,1)S(1)}, bf16[32,1024]{1,0:T(8,128)(2,1)S(1)}, u32[]{:S(2)}, u32[]{:S(2)}) collective-permute-start(bf16[32,1024]{1,0:T(8,128)(2,1)S(1)} %get-tuple-element.455), channel_id=1, source_target_pairs={{0,12},{2,14},{4,0},{6,2},{8,4},{10,6},{12,8},{14,10},{1,13},{3,15... | collective-permute-start | bytes 196616 | tf_op jit(solution)/shard_map/cond/branch_1_fun/ppermute | solution.py:81
  98.7 9.5 %collective-permute-start.29 = (bf16[32,4096]{1,0:T(8,128)(2,1)S(1)}, bf16[32,4096]{1,0:T(8,128)(2,1)S(1)}, u32[]{:S(2)}, u32[]{:S(2)}) collective-permute-start(bf16[32,4096]{1,0:T(8,128)(2,1)S(1)} %get-tuple-element.457), channel_id=1, source_target_pairs={{0,2},{2,0},{4,6},{6,4},{8,10},{10,8},{12,14},{14,12},{1,3},{3,1},... | collective-permute-start | bytes 786440 | tf_op jit(solution)/shard_map/cond/branch_1_fun/ppermute | solution.py:521
  103.8 3.7 %collective-permute-start.31 = (f32[16,64]{1,0:T(8,128)S(1)}, f32[16,64]{1,0:T(8,128)S(1)}, u32[]{:S(2)}, u32[]{:S(2)}) collective-permute-start(f32[16,64]{1,0:T(8,128)S(1)} %branch_1_fun.16.refs_2_), channel_id=1, source_target_pairs={{0,2},{2,0},{4,6},{6,4},{8,10},{10,8},{12,14},{14,12},{1,3},{3,1},... | collective-permute-start | bytes 12296 | tf_op jit(solution)/shard_map/cond/branch_1_fun/ppermute | solution.py:532
  108.7 6.8 %collective-permute-start.33 = (bf16[8,4096]{1,0:T(8,128)(2,1)S(1)}, bf16[8,4096]{1,0:T(8,128)(2,1)S(1)}, u32[]{:S(2)}, u32[]{:S(2)}) collective-permute-start(bf16[8,4096]{1,0:T(8,128)(2,1)S(1)} %get-tuple-element.467), channel_id=1, source_target_pairs={{0,4},{2,6},{4,8},{6,10},{8,12},{10,14},{12,0},{14,2},{1,5},{3,7},... | collective-permute-start | bytes 196616 | tf_op jit(solution)/shard_map/cond/branch_1_fun/ppermute | solution.py:81
  110.1 7.5 %collective-permute-start.34 = (bf16[8,4096]{1,0:T(8,128)(2,1)S(1)}, bf16[8,4096]{1,0:T(8,128)(2,1)S(1)}, u32[]{:S(2)}, u32[]{:S(2)}) collective-permute-start(bf16[8,4096]{1,0:T(8,128)(2,1)S(1)} %get-tuple-element.468), channel_id=1, source_target_pairs={{0,8},{2,10},{4,12},{6,14},{8,0},{10,2},{12,4},{14,6},{1,9},{3,11}... | collective-permute-start | bytes 196616 | tf_op jit(solution)/shard_map/cond/branch_1_fun/ppermute | solution.py:81
  111.7 6.0 %collective-permute-start.35 = (bf16[8,4096]{1,0:T(8,128)(2,1)S(1)}, bf16[8,4096]{1,0:T(8,128)(2,1)S(1)}, u32[]{:S(2)}, u32[]{:S(2)}) collective-permute-start(bf16[8,4096]{1,0:T(8,128)(2,1)S(1)} %get-tuple-element.469), channel_id=1, source_target_pairs={{0,12},{2,14},{4,0},{6,2},{8,4},{10,6},{12,8},{14,10},{1,13},{3,15... | collective-permute-start | bytes 196616 | tf_op jit(solution)/shard_map/cond/branch_1_fun/ppermute | solution.py:81
  (7 other events, 38.1 us)
